TPU v7x, 256 devices: a whole 4x4x8 slice. The times are simulated.
256 devices in a mesh: task: 4 (over x_lo, core), row: 8 (over y, x_hi), col: 8 (over z).
Axes of the slice: x: 4 (x_hi: 2, x_lo: 2; x = x_hi * 2 + x_lo), y: 4, z: 8, core: 2. Of those that a mesh axis runs over, the one named last changes fastest.
Arguments:
- acts: bfloat16 [4, 6, 512, 14336], P('task', None, 'col', 'row'), may hold values from -6 to 6
- grads: bfloat16 [4, 6, 512, 8192], P('task', None, 'row', 'col'), may hold values from -0.29882812 to 0.29882812
- weights: bfloat16 [4, 14336, 8192], P('task', 'row', 'col'), may hold values from -6 to 6
Outputs:
- merged: bfloat16 [14336, 8192], P('row', 'col')
All inputs are finite; a program needn't handle non-finite values.
Results may differ from a plain program's by a relative error of at most 0.001.
Values may be sent and summed in bfloat16 or wider, within the bound.
No kernel may reach another device: no remote copies, remote signals or barrier semaphores. Data moves between devices by JAX's collectives and lax.ppermute only.
A program may use at most 128 MiB of HBM per device.

v0:
```python
import jax
import jax.numpy as jnp
from jax import lax
from jax.sharding import PartitionSpec as P

EPS = 1e-06


def outer_square(fisher, left, right):
    sample_grad = lax.dot_general(
        left, right, (((0,), (0,)), ((), ())), preferred_element_type=jnp.float32
    )
    return fisher + sample_grad * sample_grad


def body(acts, grads, weights):
    count = acts.shape[1]
    fisher = jnp.zeros((acts.shape[3], grads.shape[3]), jnp.float32)
    all_acts = lax.all_gather(acts, "col", axis=2, tiled=True)
    all_grads = lax.all_gather(grads, "row", axis=2, tiled=True)

    def add_whole(sample_id, total):
        left = lax.dynamic_index_in_dim(all_acts[0], sample_id, 0, keepdims=False)
        right = lax.dynamic_index_in_dim(all_grads[0], sample_id, 0, keepdims=False)
        return outer_square(total, left, right)

    fisher = lax.fori_loop(0, count, add_whole, fisher)
    numerator, denominator = (
        lax.psum_scatter(
            fisher * weights[0].astype(jnp.float32), "task", scatter_dimension=0, tiled=True
        ),
        lax.psum_scatter(fisher, "task", scatter_dimension=0, tiled=True),
    )
    share = (numerator / (denominator + EPS)).astype(jnp.bfloat16)
    return lax.all_gather(share, "task", axis=0, tiled=True)


def solution(mesh):
    placed = (P("task", None, "col", "row"), P("task", None, "row", "col"), P("task", "row", "col"))
    return jax.shard_map(
        body, mesh=mesh, in_specs=placed, out_specs=P("row", "col"), check_vma=False
    )
```

profile of v0, /device:TPU:1, one launch (start us, length us, event | category | flops | bytes accessed | tf_op | source)
XLA Modules:
  0.0 488.2 jit_solution(9583102421559123416)
XLA Ops:
  6.5 0.0 all-gather.6.cloned.1.call-start
  6.5 0.7 all-gather.6.cloned.1.call-update
  7.3 0.0 all-gather.4.cloned.1.call-start
  7.3 0.7 all-gather.4.cloned.1.call-update
  8.0 0.0 reduce-scatter.5.cloned.1.call-start
  8.1 99.3 %all-gather.6.cloned.1.call-done = bf16[1,6,512,1024]{3,2,1,0:T(8,128)(2,1)} async-done(((bf16[1,6,64,1024]{3,2,1,0:T(8,128)(2,1)}), bf16[1,6,512,1024]{3,2,1,0:T(8,128)(2,1)}) %all-gather.6.cloned.1.call-update) | async-done | bytes 6291472 | tf_op jit(solution)/shard_map/all_gather | solution.py:20
  107.3 118.8 %all-gather.4.cloned.1.call-done = bf16[1,6,512,1792]{3,2,1,0:T(8,128)(2,1)} async-done(((bf16[1,6,64,1792]{3,2,1,0:T(8,128)(2,1)}), bf16[1,6,512,1792]{3,2,1,0:T(8,128)(2,1)}) %all-gather.4.cloned.1.call-update) | async-done | bytes 11010064 | tf_op jit(solution)/shard_map/all_gather | solution.py:19
  226.2 52.2 %while.14 = (s32[]{:T(128)}, f32[1792,1024]{1,0:T(8,128)}, bf16[1,6,512,1792]{3,2,1,0:T(8,128)(2,1)}, bf16[1,6,512,1024]{3,2,1,0:T(8,128)(2,1)}, s32[]{:T(128)}, /*index=5*/s32[]{:T(128)}) while((s32[]{:T(128)}, f32[1792,1024]{1,0:T(8,128)}, bf16[1,6,512,1792]{3,2,1,0:T(8,128)(2,1)}, bf16[1,6,512,1024]{3,2,1,0:T(8,128)(2,1)}, ...), condition=%wide.region_1.2_spmd.clone, body=%wide.region_0.1_spmd.clone.sunk | while | flops 1884553216 | bytes 17565268 | solution.py:27
  226.2 6.9 %select_add_fusion.2 = f32[1792,1024]{1,0:T(8,128)} fusion(f32[1792,1024]{1,0:T(8,128)} %get-tuple-element.140, pred[]{:T(512)S(6)} %compare.3, bf16[1,6,512,1792]{3,2,1,0:T(8,128)(2,1)} %get-tuple-element.147, s32[]{:T(128)S(6)} %copy.6, bf16[1,6,512,1024]{3,2,1,0:T(8,128)(2,1)} %get-tuple-element.148), kind=kOutput, calls=%fused_computation.clone.1 | convolution fusion | flops 1884553216 | bytes 17565184 | tf_op jit(solution)/shard_map/while/body/eval_jaxpr/dot_general | solution.py:10
  233.0 9.1 %select_add_fusion.2 = f32[1792,1024]{1,0:T(8,128)} fusion(f32[1792,1024]{1,0:T(8,128)} %get-tuple-element.140, pred[]{:T(512)S(6)} %compare.3, bf16[1,6,512,1792]{3,2,1,0:T(8,128)(2,1)} %get-tuple-element.147, s32[]{:T(128)S(6)} %copy.6, bf16[1,6,512,1024]{3,2,1,0:T(8,128)(2,1)} %get-tuple-element.148), kind=kOutput, calls=%fused_computation.clone.1 | convolution fusion | flops 1884553216 | bytes 17565184 | tf_op jit(solution)/shard_map/while/body/eval_jaxpr/dot_general | solution.py:10
  242.1 9.1 %select_add_fusion.2 = f32[1792,1024]{1,0:T(8,128)} fusion(f32[1792,1024]{1,0:T(8,128)} %get-tuple-element.140, pred[]{:T(512)S(6)} %compare.3, bf16[1,6,512,1792]{3,2,1,0:T(8,128)(2,1)} %get-tuple-element.147, s32[]{:T(128)S(6)} %copy.6, bf16[1,6,512,1024]{3,2,1,0:T(8,128)(2,1)} %get-tuple-element.148), kind=kOutput, calls=%fused_computation.clone.1 | convolution fusion | flops 1884553216 | bytes 17565184 | tf_op jit(solution)/shard_map/while/body/eval_jaxpr/dot_general | solution.py:10
  251.2 9.1 %select_add_fusion.2 = f32[1792,1024]{1,0:T(8,128)} fusion(f32[1792,1024]{1,0:T(8,128)} %get-tuple-element.140, pred[]{:T(512)S(6)} %compare.3, bf16[1,6,512,1792]{3,2,1,0:T(8,128)(2,1)} %get-tuple-element.147, s32[]{:T(128)S(6)} %copy.6, bf16[1,6,512,1024]{3,2,1,0:T(8,128)(2,1)} %get-tuple-element.148), kind=kOutput, calls=%fused_computation.clone.1 | convolution fusion | flops 1884553216 | bytes 17565184 | tf_op jit(solution)/shard_map/while/body/eval_jaxpr/dot_general | solution.py:10
  260.2 9.1 %select_add_fusion.2 = f32[1792,1024]{1,0:T(8,128)} fusion(f32[1792,1024]{1,0:T(8,128)} %get-tuple-element.140, pred[]{:T(512)S(6)} %compare.3, bf16[1,6,512,1792]{3,2,1,0:T(8,128)(2,1)} %get-tuple-element.147, s32[]{:T(128)S(6)} %copy.6, bf16[1,6,512,1024]{3,2,1,0:T(8,128)(2,1)} %get-tuple-element.148), kind=kOutput, calls=%fused_computation.clone.1 | convolution fusion | flops 1884553216 | bytes 17565184 | tf_op jit(solution)/shard_map/while/body/eval_jaxpr/dot_general | solution.py:10
  269.3 9.1 %select_add_fusion.2 = f32[1792,1024]{1,0:T(8,128)} fusion(f32[1792,1024]{1,0:T(8,128)} %get-tuple-element.140, pred[]{:T(512)S(6)} %compare.3, bf16[1,6,512,1792]{3,2,1,0:T(8,128)(2,1)} %get-tuple-element.147, s32[]{:T(128)S(6)} %copy.6, bf16[1,6,512,1024]{3,2,1,0:T(8,128)(2,1)} %get-tuple-element.148), kind=kOutput, calls=%fused_computation.clone.1 | convolution fusion | flops 1884553216 | bytes 17565184 | tf_op jit(solution)/shard_map/while/body/eval_jaxpr/dot_general | solution.py:10
  278.4 0.0 reduce-scatter.5.cloned.1.call-update
  278.4 0.0 reduce-scatter.3.cloned.1.call-start
  278.4 9.0 %convert_multiply_fusion = f32[1792,1024]{1,0:T(8,128)} fusion(f32[1792,1024]{1,0:T(8,128)} %get-tuple-element.84, bf16[1,1792,1024]{2,1,0:T(8,128)(2,1)} %param.7), kind=kLoop, calls=%fused_computation.6 | loop fusion | flops 3670016 | bytes 18350080 | tf_op jit(solution)/shard_map/mul | solution.py:30
  287.4 0.0 reduce-scatter.3.cloned.1.call-update
  287.4 0.0 all-gather.8.cloned.1.call-start
  287.5 63.5 %reduce-scatter.5.cloned.1.call-done = f32[448,1024]{1,0:T(8,128)} async-done(((f32[1792,1024]{1,0:T(8,128)}), f32[448,1024]{1,0:T(8,128)}) %reduce-scatter.5.cloned.1.call-update) | async-done | bytes 1835024 | tf_op jit(solution)/shard_map/reduce_scatter | solution.py:32
  351.0 77.0 %reduce-scatter.3.cloned.1.call-done = f32[448,1024]{1,0:T(8,128)} async-done(((f32[1792,1024]{1,0:T(8,128)}), f32[448,1024]{1,0:T(8,128)}) %reduce-scatter.3.cloned.1.call-update) | async-done | bytes 1835024 | tf_op jit(solution)/shard_map/reduce_scatter | solution.py:29
  428.1 3.3 divide_convert_fusion
  431.4 0.0 all-gather.8.cloned.1.call-update
  431.4 46.0 %all-gather.8.cloned.1.call-done = bf16[1792,1024]{1,0:T(8,128)(2,1)} async-done(((bf16[448,1024]{1,0:T(8,128)(2,1)}), bf16[1792,1024]{1,0:T(8,128)(2,1)}) %all-gather.8.cloned.1.call-update) | async-done | bytes 3670032 | tf_op jit(solution)/shard_map/all_gather | solution.py:35
  477.5 4.2 copy.11
  (1 shorter events, 0.0 us)
Async XLA Ops:
  6.5 100.8 %all-gather.6.cloned.1.call-start = ((), (), s32[]{:S(2)}) async-start(), calls=%async_computation.3 | async-start | bytes 7077888 | tf_op jit(solution)/shard_map/all_gather | solution.py:20
  7.3 218.9 %all-gather.4.cloned.1.call-start = ((), (), s32[]{:S(2)}) async-start(), calls=%async_computation.2 | async-start | bytes 12386304 | tf_op jit(solution)/shard_map/all_gather | solution.py:19
  8.0 343.0 %reduce-scatter.5.cloned.1.call-start = ((), (), s32[]{:S(2)}) async-start(), calls=%async_computation.5 | async-start | bytes 9175040 | tf_op jit(solution)/shard_map/reduce_scatter | solution.py:32
  278.4 149.7 %reduce-scatter.3.cloned.1.call-start = ((), (), s32[]{:S(2)}) async-start(), calls=%async_computation.4 | async-start | bytes 9175040 | tf_op jit(solution)/shard_map/reduce_scatter | solution.py:29
  287.4 190.0 %all-gather.8.cloned.1.call-start = ((), (), s32[]{:S(2)}) async-start(), calls=%async_computation.6 | async-start | bytes 4587520 | tf_op jit(solution)/shard_map/all_gather | solution.py:35
Sparse Core Ops, SparseCore 0:
  10.0 97.3 all-gather.5
  109.1 117.0 all-gather.3
  278.5 72.4 reduce-scatter.4
  353.4 74.5 reduce-scatter.2
  431.5 45.8 all-gather.7
where the time goes:
time: 488 us
  waiting for transfers between devices  406 us (83%)
  matrix products  52.2 us (11%)
  between operations  13.1 us (3%)
  other arithmetic  12.3 us (3%)
    all_gather x1, waiting for transfers between devices, body(): all_acts = lax.all_gather(acts, 'col', axis=2, tiled=True)  119 us
    all_gather x1, waiting for transfers between devices, body(): all_grads = lax.all_gather(grads, 'row', axis=2, tiled=True)  99.3 us
    reduce_scatter x1, waiting for transfers between devices, body(): lax.psum_scatter(fisher * weights[0].astype(jnp.float32), 'task', scatter...  77 us
    reduce_scatter x1, waiting for transfers between devices, body(): lax.psum_scatter(fisher, 'task', scatter_dimension=0, tiled=True)  63.5 us
    dot_general x6, matrix products, outer_square(): lax.dot_general(left, right, (((0,), (0,)), ((), ())), preferred_element_...  52.2 us
    all_gather x1, waiting for transfers between devices, body(): return lax.all_gather(share, 'task', axis=0, tiled=True)  46 us
  transfers between devices with their start and end apart: 5, of which 5 were waited for; matrix products, arithmetic and copies ran while one was open for 2% of the time, Pallas kernels for 0%

commit v1 on v0

v1 whole, which is shorter than its diff:
```python
import functools

import jax
import jax.numpy as jnp
from jax import lax
from jax.experimental import pallas as pl
from jax.experimental.pallas import tpu as pltpu
from jax.sharding import PartitionSpec as P

EPS = 1e-06
F32, BF16 = jnp.float32, jnp.bfloat16
ANY = pl.BlockSpec(memory_space=pl.ANY)
LIMIT = pltpu.CompilerParams(vmem_limit_bytes=56 * 2**20)


def place():
    task, row = lax.axis_index("task"), lax.axis_index("row")
    return task // 2, task % 2, row // 2, row % 2


def plane(x, dy, hi, lo):
    perm = [
        (t * 8 + 2 * y + h, (t ^ (2 * lo)) * 8 + 2 * ((y + dy) % 4) + (h ^ hi))
        for t in range(4)
        for y in range(4)
        for h in range(2)
    ]
    return lax.ppermute(x, ("task", "row"), perm)


def pair(x):
    return lax.ppermute(x, "task", [(t, t ^ 2) for t in range(4)])


def core(x):
    return lax.ppermute(x, "task", [(t, t ^ 1) for t in range(4)])


def block_of(meta):
    back, flip = meta
    _, _, y, hi = place()
    return 2 * ((y + 4 - back) % 4) + (hi ^ flip if flip else hi)


def fetch(metas, acts, pieces, a, g, sems):
    tok = pieces[0].shape[1]

    def copies(s):
        out = [pltpu.make_async_copy(acts.at[s], a.at[s], sems.at[s])]
        for meta, piece in zip(metas, pieces):
            rows = pl.ds(pl.multiple_of(tok * block_of(meta), tok), tok)
            out.append(pltpu.make_async_copy(piece.at[s], g.at[s, rows], sems.at[s]))
        return out

    return copies


def square_sum(copies, count, a, g, f):
    def step(s, _):
        for c in copies(s):
            c.wait()
        d = lax.dot_general(
            a[s], g[s], (((0,), (0,)), ((), ())), preferred_element_type=F32
        )
        f[...] = jnp.where(s == 0, 0.0, f[...]) + d * d
        return 0

    lax.fori_loop(0, count, step, 0)


def first_kernel(metas, acts, *refs):
    n = len(metas)
    pieces, (out, a, g, f, sems, osem) = refs[:n], refs[n:]
    copies = fetch(metas, acts, pieces, a, g, sems)
    count = a.shape[0]
    for s in range(count):
        for c in copies(s):
            c.start()
    square_sum(copies, count, a, g, f)
    cp = pltpu.make_async_copy(f, out, osem)
    cp.start()
    cp.wait()


def second_kernel(metas, acts, *refs):
    n = len(metas)
    pieces = refs[:n]
    f1_hbm, w1_hbm, w2_hbm, keep, send, a, g, f, f1, w1, w2, sems, xsem, osem = refs[n:]
    copies = fetch(metas, acts, pieces, a, g, sems)
    count = a.shape[0]
    lo, me, _, _ = place()
    rows = f.shape[0]
    half = rows // 2
    own = pl.ds(pl.multiple_of(lo * rows, 16), rows)
    extra = [
        pltpu.make_async_copy(f1_hbm, f1, xsem.at[0]),
        pltpu.make_async_copy(w1_hbm.at[0, own], w1, xsem.at[1]),
        pltpu.make_async_copy(w2_hbm, w2, xsem.at[2]),
    ]
    for s in range(count):
        for c in copies(s):
            c.start()
        if s == 0:
            for c in extra:
                c.start()
    square_sum(copies, count, a, g, f)
    for c in extra:
        c.wait()
    one, two = f1[...], f[...]
    f1[...] = one * w1[...].astype(F32) + two * w2[...].astype(F32)
    f[...] = one + two
    outs = []
    for i, src in enumerate((f1, f)):
        for j, (dst, which) in enumerate(((send, 1 - me), (keep, me))):
            at = pl.ds(pl.multiple_of(which * half, 16), half)
            outs.append(pltpu.make_async_copy(src.at[at], dst.at[i], osem.at[2 * i + j]))
    for c in outs:
        c.start()
    for c in outs:
        c.wait()


def share_kernel(keep, got, out):
    den = keep[1] + got[1]
    out[...] = ((keep[0] + got[0]) / (den + EPS)).astype(BF16)


def gather_kernel(own, by_core, by_pair, by_both, out, held, sems, osems):
    lo, me, _, _ = place()
    n = own.shape[0]
    ins, outs = [], []
    for i, (src, l, c) in enumerate(
        ((own, lo, me), (by_core, lo, 1 - me), (by_pair, 1 - lo, me), (by_both, 1 - lo, 1 - me))
    ):
        at = pl.ds(pl.multiple_of((2 * l + c) * n, 16), n)
        ins.append(pltpu.make_async_copy(src, held.at[i], sems.at[i]))
        outs.append(pltpu.make_async_copy(held.at[i], out.at[at], osems.at[i]))
    for c in ins:
        c.start()
    for i, o in zip(ins, outs):
        i.wait()
        o.start()
    for c in outs:
        c.wait()


def body(acts, grads, weights):
    _, count, tok, rows = acts.shape
    cols = grads.shape[3]
    half = rows // 2
    lo = lax.axis_index("task") // 2
    g0 = grads[0]

    def part(x, which, axis):
        return lax.dynamic_slice_in_dim(x, which * half, half, axis)

    own_acts = part(acts[0], lo, 2)
    a1 = lax.all_gather(own_acts, "col", axis=1, tiled=True)
    gd = plane(g0, 0, 0, 1)
    g0n, g0p = plane(g0, 1, 0, 0), plane(g0, -1, 0, 0)
    gx = plane(g0, 0, 1, 1)
    other_acts = pair(part(acts[0], 1 - lo, 2))
    a2 = lax.all_gather(other_acts, "col", axis=1, tiled=True)
    go = plane(gd, 0, 1, 1)
    g02 = plane(g0n, 1, 0, 0)
    gon, gop = plane(go, 1, 0, 0), plane(go, -1, 0, 0)
    go2 = plane(gop, -1, 0, 0)
    gxn, gxp, gx2 = plane(g0n, 0, 1, 1), plane(g0p, 0, 1, 1), plane(g02, 0, 1, 1)
    gdn, gdp = plane(gd, 1, 0, 0), plane(gd, -1, 0, 0)
    gd2 = plane(gdn, 1, 0, 0)
    w2 = pair(part(weights[0], 1 - lo, 0))

    metas1 = [(0, 0), (1, 0), (3, 0), (2, 0), (0, 1), (1, 1), (3, 1), (2, 1)]
    pieces1 = (g0, g0n, g0p, g02, go, gon, gop, go2)
    pieces2 = (gd, gdn, gdp, gd2, gx, gxn, gxp, gx2)
    total = tok * 8
    common = [
        pltpu.VMEM((count, total, half), BF16),
        pltpu.VMEM((count, total, cols), BF16),
        pltpu.VMEM((half, cols), F32),
    ]
    flops = 2 * count * total * half * cols
    cost = pl.CostEstimate(flops=flops, bytes_accessed=16 * 2**20, transcendentals=0)
    f1 = pl.pallas_call(
        functools.partial(first_kernel, metas1),
        out_shape=jax.ShapeDtypeStruct((half, cols), F32),
        in_specs=[ANY] * 9,
        out_specs=ANY,
        scratch_shapes=common
        + [pltpu.SemaphoreType.DMA((count,)), pltpu.SemaphoreType.DMA],
        compiler_params=LIMIT,
        cost_estimate=cost,
        name="own_task",
    )(a1, *pieces1)
    quarter = half // 2
    two = jax.ShapeDtypeStruct((2, quarter, cols), F32)
    keep, send = pl.pallas_call(
        functools.partial(second_kernel, metas1),
        out_shape=(two, two),
        in_specs=[ANY] * 12,
        out_specs=(ANY, ANY),
        scratch_shapes=common
        + [
            pltpu.VMEM((half, cols), F32),
            pltpu.VMEM((half, cols), BF16),
            pltpu.VMEM((half, cols), BF16),
            pltpu.SemaphoreType.DMA((count,)),
            pltpu.SemaphoreType.DMA((3,)),
            pltpu.SemaphoreType.DMA((4,)),
        ],
        compiler_params=LIMIT,
        cost_estimate=cost,
        name="other_task",
    )(a2, *pieces2, f1, weights, w2)
    got = core(send)
    steps = 4
    q = pl.pallas_call(
        share_kernel,
        grid=(steps,),
        out_shape=jax.ShapeDtypeStruct((quarter, cols), BF16),
        in_specs=[pl.BlockSpec((2, quarter // steps, cols), lambda i: (0, i, 0))] * 2,
        out_specs=pl.BlockSpec((quarter // steps, cols), lambda i: (i, 0)),
        compiler_params=LIMIT,
        name="share",
    )(keep, got)
    by_pair = pair(q)
    by_core = core(q)
    by_both = core(by_pair)
    return pl.pallas_call(
        gather_kernel,
        out_shape=jax.ShapeDtypeStruct((rows, cols), BF16),
        in_specs=[ANY] * 4,
        out_specs=ANY,
        scratch_shapes=[
            pltpu.VMEM((4, quarter, cols), BF16),
            pltpu.SemaphoreType.DMA((4,)),
            pltpu.SemaphoreType.DMA((4,)),
        ],
        compiler_params=LIMIT,
        name="whole",
    )(q, by_core, by_pair, by_both)


def solution(mesh):
    placed = (P("task", None, "col", "row"), P("task", None, "row", "col"), P("task", "row", "col"))
    return jax.shard_map(
        body, mesh=mesh, in_specs=placed, out_specs=P("row", "col"), check_vma=False
    )
```

time: 488 us -> 209 us (0.43)
  waiting for transfers between devices: 406 us -> 124 us
  matrix products: 52.2 us -> 0 us
  starting transfers between devices: 0.16 us -> 31.5 us
  Pallas kernels: 0 us -> 30.1 us
  other arithmetic: 12.3 us -> 0 us
  local copies, waits for them, and re-layouts: 4.25 us -> 9.83 us
    all_gather x3 -> x2, waiting for transfers between devices: 264 us -> 12.5 us  [the longest x1 12.5 us: body(): a2 = lax.all_gather(other_acts, 'col', axis=1, tiled=True)]
    reduce_scatter x2 -> x0, waiting for transfers between devices: 141 us -> none  [the longest x1 77 us: body(): lax.psum_scatter(fisher * weights[0].astype(jnp.float32), 'task', scatter...]
    ppermute x0 -> x21, waiting for transfers between devices: none -> 112 us  [the longest x15 69.5 us: plane(): return lax.ppermute(x, ('task', 'row'), perm)]
    dot_general x6 -> x0, matrix products: 52.2 us -> none  [outer_square(): lax.dot_general(left, right, (((0,), (0,)), ((), ())), preferred_element_...]
    ppermute x0 -> x21, starting transfers between devices: none -> 31.5 us  [the longest x15 25.5 us: plane(): return lax.ppermute(x, ('task', 'row'), perm)]
    pallas_call x0 -> x4, Pallas kernels: none -> 30.1 us  [the longest x1 12 us: body(): pl.pallas_call(functools.partial(second_kernel, metas1), out_shape=(two,...]
    mul x1 -> x0, other arithmetic: 8.98 us -> none  [body(): fisher * weights[0].astype(jnp.float32)]
    dynamic_slice x0 -> x2, local copies, waits for them, and re-layouts: none -> 5.23 us  [part(): return lax.dynamic_slice_in_dim(x, which * half, half, axis)]
  transfers between devices with their start and end apart: 5 -> 23, of which waited for: 5 -> 12; matrix products, arithmetic and copies ran while one was open for 2% -> 1% of each run, Pallas kernels for 0% -> 5%
where the time goes in v1:
time: 209 us
  waiting for transfers between devices  124 us (59%)
  starting transfers between devices  31.5 us (15%)
  Pallas kernels  30.1 us (14%)
  between operations  13.5 us (6%)
  local copies, waits for them, and re-layouts  9.83 us (5%)
    ppermute x15, waiting for transfers between devices, plane(): return lax.ppermute(x, ('task', 'row'), perm)  69.5 us
    ppermute x3, waiting for transfers between devices, pair(): return lax.ppermute(x, 'task', [(t, t ^ 2) for t in range(4)])  33.7 us
    ppermute x15, starting transfers between devices, plane(): return lax.ppermute(x, ('task', 'row'), perm)  25.5 us
    all_gather x1, waiting for transfers between devices, body(): a2 = lax.all_gather(other_acts, 'col', axis=1, tiled=True)  12.5 us
    pallas_call x1, Pallas kernels, body(): pl.pallas_call(functools.partial(second_kernel, metas1), out_shape=(two,...  12 us
    pallas_call x1, Pallas kernels, body(): pl.pallas_call(functools.partial(first_kernel, metas1), out_shape=jax.Sha...  10.3 us
    ppermute x3, waiting for transfers between devices, core(): return lax.ppermute(x, 'task', [(t, t ^ 1) for t in range(4)])  8.34 us
    dynamic_slice x2, local copies, waits for them, and re-layouts, part(): return lax.dynamic_slice_in_dim(x, which * half, half, axis)  5.23 us
  transfers between devices with their start and end apart: 23, of which 12 were waited for; matrix products, arithmetic and copies ran while one was open for 1% of the time, Pallas kernels for 5%

profile of v1, /device:TPU:1, one launch (start us, length us, event | category | flops | bytes accessed | tf_op | source)
XLA Modules:
  0.0 209.1 jit_solution(11029784764463545006)
XLA Ops:
  6.5 2.3 %constant_dynamic-slice_fusion = (bf16[1,6,64,896]{3,2,1,0:T(8,128)(2,1)}, bf16[6,64,896]{2,1,0:T(8,128)(2,1)S(1)}) fusion(bf16[1,6,64,1792]{3,2,1,0:T(8,128)(2,1)} %param.3, s32[]{:T(128)S(6)} %select_n.14, s32[]{:T(128)S(6)} %select_n.13), kind=kLoop, calls=%fused_computation.2 | loop fusion | bytes 2752520 | tf_op jit(solution)/shard_map/dynamic_slice | solution.py:155
  8.9 2.1 %collective-permute-start = (bf16[6,64,896]{2,1,0:T(8,128)(2,1)S(1)}, bf16[6,64,896]{2,1,0:T(8,128)(2,1)S(1)}, u32[]{:S(2)}, u32[]{:S(2)}) collective-permute-start(bf16[6,64,896]{2,1,0:T(8,128)(2,1)S(1)} %get-tuple-element.10), channel_id=1, source_target_pairs={{0,128},{64,192},{128,0},{192,64},{1,129},{65,193},{129,1},{193,65... | collective-permute-start | bytes 2064392 | tf_op jit(solution)/shard_map/ppermute | solution.py:32
  11.0 13.8 %collective-permute-done = bf16[6,64,896]{2,1,0:T(8,128)(2,1)S(1)} collective-permute-done((bf16[6,64,896]{2,1,0:T(8,128)(2,1)S(1)}, bf16[6,64,896]{2,1,0:T(8,128)(2,1)S(1)}, u32[]{:S(2)}, u32[]{:S(2)}) %collective-permute-start) | collective-permute-done | bytes 688160 | tf_op jit(solution)/shard_map/ppermute | solution.py:32
  25.7 2.3 %collective-permute-start.1 = (bf16[6,64,1024]{2,1,0:T(8,128)(2,1)}, bf16[6,64,1024]{2,1,0:T(8,128)(2,1)S(1)}, u32[]{:S(2)}, u32[]{:S(2)}) collective-permute-start(bf16[6,64,1024]{2,1,0:T(8,128)(2,1)} %bitcast.1.refs_0_), channel_id=1, source_target_pairs={{0,128},{8,136},{16,144},{24,152},{32,160},{40,168},{48,176},{56,1... | collective-permute-start | bytes 2359304 | tf_op jit(solution)/shard_map/ppermute | solution.py:28
  28.0 3.0 %collective-permute-start.8 = (bf16[6,64,1024]{2,1,0:T(8,128)(2,1)}, bf16[6,64,1024]{2,1,0:T(8,128)(2,1)S(1)}, u32[]{:S(2)}, u32[]{:S(2)}) collective-permute-start(bf16[6,64,1024]{2,1,0:T(8,128)(2,1)} %bitcast.1.refs_0_), channel_id=1, source_target_pairs={{0,48},{8,56},{16,0},{24,8},{32,16},{40,24},{48,32},{56,40},{64,11... | collective-permute-start | bytes 2359304 | tf_op jit(solution)/shard_map/ppermute | solution.py:28
  31.0 13.0 %collective-permute-done.1.refs_0_ = bf16[6,64,1024]{2,1,0:T(8,128)(2,1)S(1)} collective-permute-done((bf16[6,64,1024]{2,1,0:T(8,128)(2,1)}, bf16[6,64,1024]{2,1,0:T(8,128)(2,1)S(1)}, u32[]{:S(2)}, u32[]{:S(2)}) %collective-permute-start.1) | collective-permute-done | bytes 786464 | tf_op jit(solution)/shard_map/ppermute | solution.py:28
  44.1 3.3 %collective-permute-start.12 = (bf16[6,64,1024]{2,1,0:T(8,128)(2,1)S(1)}, bf16[6,64,1024]{2,1,0:T(8,128)(2,1)S(1)}, u32[]{:S(2)}, u32[]{:S(2)}) collective-permute-start(bf16[6,64,1024]{2,1,0:T(8,128)(2,1)S(1)} %collective-permute-done.1.refs_0_), channel_id=1, source_target_pairs={{0,136},{8,128},{16,152},{24,144},{32,168},{40,160},{48,184},{56,1... | collective-permute-start | bytes 2359304 | tf_op jit(solution)/shard_map/ppermute | solution.py:28
  47.4 1.3 collective-permute-start.6
  48.9 2.5 %collective-permute-start.9 = (bf16[6,64,1024]{2,1,0:T(8,128)(2,1)S(1)}, bf16[6,64,1024]{2,1,0:T(8,128)(2,1)S(1)}, u32[]{:S(2)}, u32[]{:S(2)}) collective-permute-start(bf16[6,64,1024]{2,1,0:T(8,128)(2,1)S(1)} %collective-permute-done.8.refs_2_), channel_id=1, source_target_pairs={{0,136},{8,128},{16,152},{24,144},{32,168},{40,160},{48,184},{56,1... | collective-permute-start | bytes 2359304 | tf_op jit(solution)/shard_map/ppermute | solution.py:28
  51.3 11.6 %collective-permute-done.12.refs_4_ = bf16[6,64,1024]{2,1,0:T(8,128)(2,1)S(1)} collective-permute-done((bf16[6,64,1024]{2,1,0:T(8,128)(2,1)S(1)}, bf16[6,64,1024]{2,1,0:T(8,128)(2,1)S(1)}, u32[]{:S(2)}, u32[]{:S(2)}) %collective-permute-start.12) | collective-permute-done | bytes 786464 | tf_op jit(solution)/shard_map/ppermute | solution.py:28
  63.0 2.6 %collective-permute-start.14 = (bf16[6,64,1024]{2,1,0:T(8,128)(2,1)S(1)}, bf16[6,64,1024]{2,1,0:T(8,128)(2,1)S(1)}, u32[]{:S(2)}, u32[]{:S(2)}) collective-permute-start(bf16[6,64,1024]{2,1,0:T(8,128)(2,1)S(1)} %collective-permute-done.12.refs_4_), channel_id=1, source_target_pairs={{0,48},{8,56},{16,0},{24,8},{32,16},{40,24},{48,32},{56,40},{64,11... | collective-permute-start | bytes 2359304 | tf_op jit(solution)/shard_map/ppermute | solution.py:28
  65.6 2.9 %dynamic-slice_bitcast_fusion = bf16[896,1024]{1,0:T(8,128)(2,1)} fusion(bf16[1,1792,1024]{2,1,0:T(8,128)(2,1)} %refs_9_.1, s32[]{:T(128)S(6)} %select_n.13), kind=kLoop, calls=%fused_computation | loop fusion | bytes 3670020 | tf_op jit(solution)/shard_map/dynamic_slice | solution.py:155
  68.6 11.2 %collective-permute-done.5.refs_4_ = bf16[6,64,1024]{2,1,0:T(8,128)(2,1)S(1)} collective-permute-done((bf16[6,64,1024]{2,1,0:T(8,128)(2,1)}, bf16[6,64,1024]{2,1,0:T(8,128)(2,1)S(1)}, u32[]{:S(2)}, u32[]{:S(2)}) %collective-permute-start.5) | collective-permute-done | bytes 786464 | tf_op jit(solution)/shard_map/ppermute | solution.py:28
  79.8 1.2 collective-permute-start.2
  81.0 15.6 %collective-permute-done.9.refs_6_ = bf16[6,64,1024]{2,1,0:T(8,128)(2,1)S(1)} collective-permute-done((bf16[6,64,1024]{2,1,0:T(8,128)(2,1)S(1)}, bf16[6,64,1024]{2,1,0:T(8,128)(2,1)S(1)}, u32[]{:S(2)}, u32[]{:S(2)}) %collective-permute-start.9) | collective-permute-done | bytes 786464 | tf_op jit(solution)/shard_map/ppermute | solution.py:28
  96.7 1.2 collective-permute-start.13
  97.9 1.5 collective-permute-start.15
  99.4 2.5 %collective-permute-start.7 = (bf16[6,64,1024]{2,1,0:T(8,128)(2,1)}, bf16[6,64,1024]{2,1,0:T(8,128)(2,1)}, u32[]{:S(2)}, u32[]{:S(2)}) collective-permute-start(bf16[6,64,1024]{2,1,0:T(8,128)(2,1)} %collective-permute-done.6.refs_1_), channel_id=1, source_target_pairs={{0,136},{8,128},{16,152},{24,144},{32,168},{40,160},{48,184},{56,1... | collective-permute-start | bytes 2359304 | tf_op jit(solution)/shard_map/ppermute | solution.py:28
  101.9 1.4 collective-permute-start.3
  103.3 14.3 %collective-permute-done.13.refs_5_ = bf16[6,64,1024]{2,1,0:T(8,128)(2,1)S(1)} collective-permute-done((bf16[6,64,1024]{2,1,0:T(8,128)(2,1)S(1)}, bf16[6,64,1024]{2,1,0:T(8,128)(2,1)S(1)}, u32[]{:S(2)}, u32[]{:S(2)}) %collective-permute-start.13) | collective-permute-done | bytes 786464 | tf_op jit(solution)/shard_map/ppermute | solution.py:28
  117.6 2.4 %collective-permute-start.11 = (bf16[6,64,1024]{2,1,0:T(8,128)(2,1)}, bf16[6,64,1024]{2,1,0:T(8,128)(2,1)}, u32[]{:S(2)}, u32[]{:S(2)}) collective-permute-start(bf16[6,64,1024]{2,1,0:T(8,128)(2,1)} %collective-permute-done.10.refs_3_), channel_id=1, source_target_pairs={{0,136},{8,128},{16,152},{24,144},{32,168},{40,160},{48,184},{56,1... | collective-permute-start | bytes 2359304 | tf_op jit(solution)/shard_map/ppermute | solution.py:28
  121.0 10.3 %own_task.1.refs_8_ = f32[896,1024]{1,0:T(8,128)} custom-call(bf16[6,512,896]{2,1,0:T(8,128)(2,1)} %bitcast.6, bf16[6,64,1024]{2,1,0:T(8,128)(2,1)} %bitcast.1.refs_0_, bf16[6,64,1024]{2,1,0:T(8,128)(2,1)} %collective-permute-done.6.refs_1_, bf16[6,64,1024]{2,1,0:T(8,128)(2,1)} %copy-done.9, bf16[6,64,1024]{2,1,0:T(8,128)(2,1)} %collective-permute-done.10.refs_3_, ...), custom_call_target="tpu_custom_call" | custom-call | flops 5637144576 | bytes 16777216 | tf_op jit(solution)/shard_map/own_task/pallas_call | solution.py:184
  132.1 3.0 %collective-permute-done.4.refs_3_ = bf16[6,64,1024]{2,1,0:T(8,128)(2,1)} collective-permute-done((bf16[6,64,1024]{2,1,0:T(8,128)(2,1)}, bf16[6,64,1024]{2,1,0:T(8,128)(2,1)}, u32[]{:S(2)}, u32[]{:S(2)}) %collective-permute-start.4) | collective-permute-done | bytes 786464 | tf_op jit(solution)/shard_map/ppermute | solution.py:28
  135.1 12.5 %all-gather.4.cloned.1.call-done.acts = bf16[6,512,896]{2,1,0:T(8,128)(2,1)} async-done(((bf16[6,64,896]{2,1,0:T(8,128)(2,1)}), bf16[6,512,896]{2,1,0:T(8,128)(2,1)}) %all-gather.4.cloned.1.call-update) | async-done | bytes 5505040 | tf_op jit(solution)/shard_map/all_gather | solution.py:163
  147.6 12.0 %other_task.1 = (f32[2,448,1024]{2,1,0:T(8,128)}, f32[2,448,1024]{2,1,0:T(8,128)}) custom-call(bf16[6,512,896]{2,1,0:T(8,128)(2,1)} %all-gather.4.cloned.1.call-done.acts, bf16[6,64,1024]{2,1,0:T(8,128)(2,1)} %copy-done.5, bf16[6,64,1024]{2,1,0:T(8,128)(2,1)} %collective-permute-done.2.refs_1_, bf16[6,64,1024]{2,1,0:T(8,128)(2,1)} %collective-permute-done.3.refs_2_, ...), custom_call_target="tpu_custom_call" | custom-call | flops 5637144576 | bytes 16777216 | tf_op jit(solution)/shard_map/other_task/pallas_call | solution.py:197
  160.5 6.2 %collective-permute-done.17.got = f32[2,448,1024]{2,1,0:T(8,128)S(1)} collective-permute-done((f32[2,448,1024]{2,1,0:T(8,128)}, f32[2,448,1024]{2,1,0:T(8,128)S(1)}, u32[]{:S(2)}, u32[]{:S(2)}) %collective-permute-start.17) | collective-permute-done | bytes 3670048 | tf_op jit(solution)/shard_map/ppermute | solution.py:36
  166.7 1.8 copy-done
  168.5 4.6 %share.1.own = bf16[448,1024]{1,0:T(8,128)(2,1)} custom-call(f32[2,448,1024]{2,1,0:T(8,128)} %get-tuple-element.7.keep, f32[2,448,1024]{2,1,0:T(8,128)} %copy-done), custom_call_target="tpu_custom_call" | custom-call | tf_op jit(solution)/shard_map/share/pallas_call | solution.py:217
  175.0 19.9 %collective-permute-done.19.by_pair = bf16[448,1024]{1,0:T(8,128)(2,1)S(1)} collective-permute-done((bf16[448,1024]{1,0:T(8,128)(2,1)}, bf16[448,1024]{1,0:T(8,128)(2,1)S(1)}, u32[]{:S(2)}, u32[]{:S(2)}) %collective-permute-start.19) | collective-permute-done | bytes 917536 | tf_op jit(solution)/shard_map/ppermute | solution.py:32
  195.0 1.2 collective-permute-start.20
  196.2 2.1 %collective-permute-done.20.by_both = bf16[448,1024]{1,0:T(8,128)(2,1)S(1)} collective-permute-done((bf16[448,1024]{1,0:T(8,128)(2,1)S(1)}, bf16[448,1024]{1,0:T(8,128)(2,1)S(1)}, u32[]{:S(2)}, u32[]{:S(2)}) %collective-permute-start.20) | collective-permute-done | bytes 917536 | tf_op jit(solution)/shard_map/ppermute | solution.py:36
  199.2 3.1 %whole.1 = bf16[1792,1024]{1,0:T(8,128)(2,1)} custom-call(bf16[448,1024]{1,0:T(8,128)(2,1)} %share.1.own, bf16[448,1024]{1,0:T(8,128)(2,1)} %copy-done.3, bf16[448,1024]{1,0:T(8,128)(2,1)} %copy-done.2, bf16[448,1024]{1,0:T(8,128)(2,1)} %copy-done.4), custom_call_target="tpu_custom_call" | custom-call | tf_op jit(solution)/shard_map/whole/pallas_call | solution.py:229
  (50 shorter events, 6.4 us)
Async XLA Ops:
  6.5 114.5 %all-gather.6.cloned.1.call-start = ((), (), s32[]{:S(2)}) async-start(), calls=%async_computation.1 | async-start | bytes 6193152 | tf_op jit(solution)/shard_map/all_gather | solution.py:158
  8.8 138.8 %all-gather.4.cloned.1.call-start = ((), (), s32[]{:S(2)}) async-start(), calls=%async_computation | async-start | bytes 6193152 | tf_op jit(solution)/shard_map/all_gather | solution.py:163
  8.9 15.9 %collective-permute-start = (bf16[6,64,896]{2,1,0:T(8,128)(2,1)S(1)}, bf16[6,64,896]{2,1,0:T(8,128)(2,1)S(1)}, u32[]{:S(2)}, u32[]{:S(2)}) collective-permute-start(bf16[6,64,896]{2,1,0:T(8,128)(2,1)S(1)} %get-tuple-element.10), channel_id=1, source_target_pairs={{0,128},{64,192},{128,0},{192,64},{1,129},{65,193},{129,1},{193,65... | collective-permute-start | bytes 2064392 | tf_op jit(solution)/shard_map/ppermute | solution.py:32
  25.7 18.3 %collective-permute-start.1 = (bf16[6,64,1024]{2,1,0:T(8,128)(2,1)}, bf16[6,64,1024]{2,1,0:T(8,128)(2,1)S(1)}, u32[]{:S(2)}, u32[]{:S(2)}) collective-permute-start(bf16[6,64,1024]{2,1,0:T(8,128)(2,1)} %bitcast.1.refs_0_), channel_id=1, source_target_pairs={{0,128},{8,136},{16,144},{24,152},{32,160},{40,168},{48,176},{56,1... | collective-permute-start | bytes 2359304 | tf_op jit(solution)/shard_map/ppermute | solution.py:28
  28.0 20.9 %collective-permute-start.8 = (bf16[6,64,1024]{2,1,0:T(8,128)(2,1)}, bf16[6,64,1024]{2,1,0:T(8,128)(2,1)S(1)}, u32[]{:S(2)}, u32[]{:S(2)}) collective-permute-start(bf16[6,64,1024]{2,1,0:T(8,128)(2,1)} %bitcast.1.refs_0_), channel_id=1, source_target_pairs={{0,48},{8,56},{16,0},{24,8},{32,16},{40,24},{48,32},{56,40},{64,11... | collective-permute-start | bytes 2359304 | tf_op jit(solution)/shard_map/ppermute | solution.py:28
  44.1 87.3 %copy-start.5 = (bf16[6,64,1024]{2,1,0:T(8,128)(2,1)}, bf16[6,64,1024]{2,1,0:T(8,128)(2,1)S(1)}, u32[]{:S(2)}) copy-start(bf16[6,64,1024]{2,1,0:T(8,128)(2,1)S(1)} %collective-permute-done.1.refs_0_) | copy-start | bytes 2359300
  44.1 18.9 %collective-permute-start.12 = (bf16[6,64,1024]{2,1,0:T(8,128)(2,1)S(1)}, bf16[6,64,1024]{2,1,0:T(8,128)(2,1)S(1)}, u32[]{:S(2)}, u32[]{:S(2)}) collective-permute-start(bf16[6,64,1024]{2,1,0:T(8,128)(2,1)S(1)} %collective-permute-done.1.refs_0_), channel_id=1, source_target_pairs={{0,136},{8,128},{16,152},{24,144},{32,168},{40,160},{48,184},{56,1... | collective-permute-start | bytes 2359304 | tf_op jit(solution)/shard_map/ppermute | solution.py:28
  47.4 21.2 %collective-permute-start.6 = (bf16[6,64,1024]{2,1,0:T(8,128)(2,1)}, bf16[6,64,1024]{2,1,0:T(8,128)(2,1)}, u32[]{:S(2)}, u32[]{:S(2)}) collective-permute-start(bf16[6,64,1024]{2,1,0:T(8,128)(2,1)} %bitcast.1.refs_0_), channel_id=1, source_target_pairs={{0,16},{8,24},{16,32},{24,40},{32,48},{40,56},{48,0},{56,8},{64,80... | collective-permute-start | bytes 2359304 | tf_op jit(solution)/shard_map/ppermute | solution.py:28
  48.7 31.1 %collective-permute-start.5 = (bf16[6,64,1024]{2,1,0:T(8,128)(2,1)}, bf16[6,64,1024]{2,1,0:T(8,128)(2,1)S(1)}, u32[]{:S(2)}, u32[]{:S(2)}) collective-permute-start(bf16[6,64,1024]{2,1,0:T(8,128)(2,1)} %bitcast.1.refs_0_), channel_id=1, source_target_pairs={{0,136},{8,128},{16,152},{24,144},{32,168},{40,160},{48,184},{56,1... | collective-permute-start | bytes 2359304 | tf_op jit(solution)/shard_map/ppermute | solution.py:28
  48.9 54.4 %copy-start.9 = (bf16[6,64,1024]{2,1,0:T(8,128)(2,1)}, bf16[6,64,1024]{2,1,0:T(8,128)(2,1)S(1)}, u32[]{:S(2)}) copy-start(bf16[6,64,1024]{2,1,0:T(8,128)(2,1)S(1)} %collective-permute-done.8.refs_2_) | copy-start | bytes 2359300
  48.9 47.8 %collective-permute-start.9 = (bf16[6,64,1024]{2,1,0:T(8,128)(2,1)S(1)}, bf16[6,64,1024]{2,1,0:T(8,128)(2,1)S(1)}, u32[]{:S(2)}, u32[]{:S(2)}) collective-permute-start(bf16[6,64,1024]{2,1,0:T(8,128)(2,1)S(1)} %collective-permute-done.8.refs_2_), channel_id=1, source_target_pairs={{0,136},{8,128},{16,152},{24,144},{32,168},{40,160},{48,184},{56,1... | collective-permute-start | bytes 2359304 | tf_op jit(solution)/shard_map/ppermute | solution.py:28
  63.0 54.7 %copy-start.10 = (bf16[6,64,1024]{2,1,0:T(8,128)(2,1)}, bf16[6,64,1024]{2,1,0:T(8,128)(2,1)S(1)}, u32[]{:S(2)}) copy-start(bf16[6,64,1024]{2,1,0:T(8,128)(2,1)S(1)} %collective-permute-done.12.refs_4_) | copy-start | bytes 2359300
  63.0 34.9 %collective-permute-start.14 = (bf16[6,64,1024]{2,1,0:T(8,128)(2,1)S(1)}, bf16[6,64,1024]{2,1,0:T(8,128)(2,1)S(1)}, u32[]{:S(2)}, u32[]{:S(2)}) collective-permute-start(bf16[6,64,1024]{2,1,0:T(8,128)(2,1)S(1)} %collective-permute-done.12.refs_4_), channel_id=1, source_target_pairs={{0,48},{8,56},{16,0},{24,8},{32,16},{40,24},{48,32},{56,40},{64,11... | collective-permute-start | bytes 2359304 | tf_op jit(solution)/shard_map/ppermute | solution.py:28
  68.6 62.9 %collective-permute-start.16 = (bf16[896,1024]{1,0:T(8,128)(2,1)}, bf16[896,1024]{1,0:T(8,128)(2,1)S(1)}, u32[]{:S(2)}, u32[]{:S(2)}) collective-permute-start(bf16[896,1024]{1,0:T(8,128)(2,1)} %dynamic-slice_bitcast_fusion), channel_id=1, source_target_pairs={{0,128},{64,192},{128,0},{192,64},{1,129},{65,193},{129,1},{193,65... | collective-permute-start | bytes 5505032 | tf_op jit(solution)/shard_map/ppermute | solution.py:32
  68.6 30.9 %collective-permute-start.10 = (bf16[6,64,1024]{2,1,0:T(8,128)(2,1)}, bf16[6,64,1024]{2,1,0:T(8,128)(2,1)}, u32[]{:S(2)}, u32[]{:S(2)}) collective-permute-start(bf16[6,64,1024]{2,1,0:T(8,128)(2,1)} %collective-permute-done.6.refs_1_), channel_id=1, source_target_pairs={{0,16},{8,24},{16,32},{24,40},{32,48},{40,56},{48,0},{56,8},{64,80... | collective-permute-start | bytes 2359304 | tf_op jit(solution)/shard_map/ppermute | solution.py:28
  79.8 51.6 %copy-start.6 = (bf16[6,64,1024]{2,1,0:T(8,128)(2,1)}, bf16[6,64,1024]{2,1,0:T(8,128)(2,1)S(1)}, u32[]{:S(2)}) copy-start(bf16[6,64,1024]{2,1,0:T(8,128)(2,1)S(1)} %collective-permute-done.5.refs_4_) | copy-start | bytes 2359300
  79.8 22.1 %collective-permute-start.2 = (bf16[6,64,1024]{2,1,0:T(8,128)(2,1)S(1)}, bf16[6,64,1024]{2,1,0:T(8,128)(2,1)}, u32[]{:S(2)}, u32[]{:S(2)}) collective-permute-start(bf16[6,64,1024]{2,1,0:T(8,128)(2,1)S(1)} %collective-permute-done.1.refs_0_), channel_id=1, source_target_pairs={{0,16},{8,24},{16,32},{24,40},{32,48},{40,56},{48,0},{56,8},{64,80... | collective-permute-start | bytes 2359304 | tf_op jit(solution)/shard_map/ppermute | solution.py:28
  96.7 5.2 %copy-start.7 = (bf16[6,64,1024]{2,1,0:T(8,128)(2,1)}, bf16[6,64,1024]{2,1,0:T(8,128)(2,1)S(1)}, u32[]{:S(2)}) copy-start(bf16[6,64,1024]{2,1,0:T(8,128)(2,1)S(1)} %collective-permute-done.9.refs_6_) | copy-start | bytes 2359300
  96.7 20.9 %collective-permute-start.13 = (bf16[6,64,1024]{2,1,0:T(8,128)(2,1)S(1)}, bf16[6,64,1024]{2,1,0:T(8,128)(2,1)S(1)}, u32[]{:S(2)}, u32[]{:S(2)}) collective-permute-start(bf16[6,64,1024]{2,1,0:T(8,128)(2,1)S(1)} %collective-permute-done.12.refs_4_), channel_id=1, source_target_pairs={{0,16},{8,24},{16,32},{24,40},{32,48},{40,56},{48,0},{56,8},{64,80... | collective-permute-start | bytes 2359304 | tf_op jit(solution)/shard_map/ppermute | solution.py:28
  97.9 22.1 %copy-start.11 = (bf16[6,64,1024]{2,1,0:T(8,128)(2,1)}, bf16[6,64,1024]{2,1,0:T(8,128)(2,1)S(1)}, u32[]{:S(2)}) copy-start(bf16[6,64,1024]{2,1,0:T(8,128)(2,1)S(1)} %collective-permute-done.14.refs_6_) | copy-start | bytes 2359300
  97.9 22.1 %collective-permute-start.15 = (bf16[6,64,1024]{2,1,0:T(8,128)(2,1)S(1)}, bf16[6,64,1024]{2,1,0:T(8,128)(2,1)S(1)}, u32[]{:S(2)}, u32[]{:S(2)}) collective-permute-start(bf16[6,64,1024]{2,1,0:T(8,128)(2,1)S(1)} %collective-permute-done.14.refs_6_), channel_id=1, source_target_pairs={{0,48},{8,56},{16,0},{24,8},{32,16},{40,24},{48,32},{56,40},{64,11... | collective-permute-start | bytes 2359304 | tf_op jit(solution)/shard_map/ppermute | solution.py:28
  99.4 32.0 %collective-permute-start.7 = (bf16[6,64,1024]{2,1,0:T(8,128)(2,1)}, bf16[6,64,1024]{2,1,0:T(8,128)(2,1)}, u32[]{:S(2)}, u32[]{:S(2)}) collective-permute-start(bf16[6,64,1024]{2,1,0:T(8,128)(2,1)} %collective-permute-done.6.refs_1_), channel_id=1, source_target_pairs={{0,136},{8,128},{16,152},{24,144},{32,168},{40,160},{48,184},{56,1... | collective-permute-start | bytes 2359304 | tf_op jit(solution)/shard_map/ppermute | solution.py:28
  101.9 29.5 %collective-permute-start.3 = (bf16[6,64,1024]{2,1,0:T(8,128)(2,1)S(1)}, bf16[6,64,1024]{2,1,0:T(8,128)(2,1)}, u32[]{:S(2)}, u32[]{:S(2)}) collective-permute-start(bf16[6,64,1024]{2,1,0:T(8,128)(2,1)S(1)} %collective-permute-done.1.refs_0_), channel_id=1, source_target_pairs={{0,48},{8,56},{16,0},{24,8},{32,16},{40,24},{48,32},{56,40},{64,11... | collective-permute-start | bytes 2359304 | tf_op jit(solution)/shard_map/ppermute | solution.py:28
  117.6 2.4 %copy-start.12 = (bf16[6,64,1024]{2,1,0:T(8,128)(2,1)}, bf16[6,64,1024]{2,1,0:T(8,128)(2,1)S(1)}, u32[]{:S(2)}) copy-start(bf16[6,64,1024]{2,1,0:T(8,128)(2,1)S(1)} %collective-permute-done.13.refs_5_) | copy-start | bytes 2359300
  117.6 14.5 %collective-permute-start.11 = (bf16[6,64,1024]{2,1,0:T(8,128)(2,1)}, bf16[6,64,1024]{2,1,0:T(8,128)(2,1)}, u32[]{:S(2)}, u32[]{:S(2)}) collective-permute-start(bf16[6,64,1024]{2,1,0:T(8,128)(2,1)} %collective-permute-done.10.refs_3_), channel_id=1, source_target_pairs={{0,136},{8,128},{16,152},{24,144},{32,168},{40,160},{48,184},{56,1... | collective-permute-start | bytes 2359304 | tf_op jit(solution)/shard_map/ppermute | solution.py:28
  121.0 14.2 %collective-permute-start.4 = (bf16[6,64,1024]{2,1,0:T(8,128)(2,1)}, bf16[6,64,1024]{2,1,0:T(8,128)(2,1)}, u32[]{:S(2)}, u32[]{:S(2)}) collective-permute-start(bf16[6,64,1024]{2,1,0:T(8,128)(2,1)} %collective-permute-done.2.refs_1_), channel_id=1, source_target_pairs={{0,16},{8,24},{16,32},{24,40},{32,48},{40,56},{48,0},{56,8},{64,80... | collective-permute-start | bytes 2359304 | tf_op jit(solution)/shard_map/ppermute | solution.py:28
  131.4 16.2 %copy-start.1 = (bf16[896,1024]{1,0:T(8,128)(2,1)}, bf16[896,1024]{1,0:T(8,128)(2,1)S(1)}, u32[]{:S(2)}) copy-start(bf16[896,1024]{1,0:T(8,128)(2,1)S(1)} %collective-permute-done.16.refs_10_) | copy-start | bytes 5505028
  159.7 7.0 %collective-permute-start.17 = (f32[2,448,1024]{2,1,0:T(8,128)}, f32[2,448,1024]{2,1,0:T(8,128)S(1)}, u32[]{:S(2)}, u32[]{:S(2)}) collective-permute-start(f32[2,448,1024]{2,1,0:T(8,128)} %get-tuple-element.8), channel_id=1, source_target_pairs={{0,64},{64,0},{128,192},{192,128},{1,65},{65,1},{129,193},{193,129... | collective-permute-start | bytes 11010056 | tf_op jit(solution)/shard_map/ppermute | solution.py:36
  173.2 21.8 %collective-permute-start.19 = (bf16[448,1024]{1,0:T(8,128)(2,1)}, bf16[448,1024]{1,0:T(8,128)(2,1)S(1)}, u32[]{:S(2)}, u32[]{:S(2)}) collective-permute-start(bf16[448,1024]{1,0:T(8,128)(2,1)} %share.1.own), channel_id=1, source_target_pairs={{0,128},{64,192},{128,0},{192,64},{1,129},{65,193},{129,1},{193,65... | collective-permute-start | bytes 2752520 | tf_op jit(solution)/shard_map/ppermute | solution.py:32
  174.4 21.8 %collective-permute-start.18 = (bf16[448,1024]{1,0:T(8,128)(2,1)}, bf16[448,1024]{1,0:T(8,128)(2,1)S(1)}, u32[]{:S(2)}, u32[]{:S(2)}) collective-permute-start(bf16[448,1024]{1,0:T(8,128)(2,1)} %share.1.own), channel_id=1, source_target_pairs={{0,64},{64,0},{128,192},{192,128},{1,65},{65,1},{129,193},{193,129... | collective-permute-start | bytes 2752520 | tf_op jit(solution)/shard_map/ppermute | solution.py:36
  195.0 3.3 %copy-start.2 = (bf16[448,1024]{1,0:T(8,128)(2,1)}, bf16[448,1024]{1,0:T(8,128)(2,1)S(1)}, u32[]{:S(2)}) copy-start(bf16[448,1024]{1,0:T(8,128)(2,1)S(1)} %collective-permute-done.19.by_pair) | copy-start | bytes 2752516
  195.0 3.3 %collective-permute-start.20 = (bf16[448,1024]{1,0:T(8,128)(2,1)S(1)}, bf16[448,1024]{1,0:T(8,128)(2,1)S(1)}, u32[]{:S(2)}, u32[]{:S(2)}) collective-permute-start(bf16[448,1024]{1,0:T(8,128)(2,1)S(1)} %collective-permute-done.19.by_pair), channel_id=1, source_target_pairs={{0,64},{64,0},{128,192},{192,128},{1,65},{65,1},{129,193},{193,129... | collective-permute-start | bytes 2752520 | tf_op jit(solution)/shard_map/ppermute | solution.py:36
  (5 other events, 6.7 us)
Sparse Core Ops, SparseCore 0:
  9.1 70.8 all-gather.5
  81.9 65.6 all-gather.3

commit v2 on v0

v2 whole, which is shorter than its diff:
```python
import functools

import jax
import jax.numpy as jnp
from jax import lax
from jax.experimental import pallas as pl
from jax.experimental.pallas import tpu as pltpu
from jax.sharding import PartitionSpec as P

EPS = 1e-06
F32, BF16 = jnp.float32, jnp.bfloat16
ANY = pl.BlockSpec(memory_space=pl.ANY)
LIMIT = pltpu.CompilerParams(vmem_limit_bytes=56 * 2**20)
CHUNKS = (512, 384)


ORDER = (
    "o,o,0",
    "t,give,0",
    "g,g,0",
    "x,g,0",
    "o,o,1",
    "t,t,0",
    "d,g,0<t0",
    "g,g,1",
    "x,g,1",
    "o,o,2",
    "t,t,1",
    "u,d,0",
    "g,g,2",
    "d,d,0",
    "o,o,3",
    "t,t,2",
    "w,wgive,0",
    "d,d,1",
    "u,u,0",
    "x,g,2",
    "o,o,4",
    "t,t,3<x0<g3",
    "d,d,2",
    "u,u,1",
    "x,g,3",
    "o,o,5",
    "t,t,4",
    "u,u,2",
    "o,o,6",
    "t,t,5<d3<x1",
    "t,t,6<u3<x2",
)


def place():
    task, row = lax.axis_index("task"), lax.axis_index("row")
    return task // 2, task % 2, row // 2, row % 2


def ring_y(x):
    perm = [
        (t * 8 + 2 * y + h, t * 8 + 2 * ((y + 1 - 2 * (t % 2)) % 4) + h)
        for t in range(4)
        for y in range(4)
        for h in range(2)
    ]
    return lax.ppermute(x, ("task", "row"), perm)


def ring_z(x):
    perm = [(t * 8 + z, t * 8 + (z + 1 - 2 * (t % 2)) % 8) for t in range(4) for z in range(8)]
    return lax.ppermute(x, ("task", "col"), perm)


def cross(x):
    perm = [(t * 8 + r, (t ^ 2) * 8 + (r ^ 1)) for t in range(4) for r in range(8)]
    return lax.ppermute(x, ("task", "row"), perm)


def pair(x):
    return lax.ppermute(x, "task", [(t, t ^ 2) for t in range(4)])


def core(x):
    return lax.ppermute(x, "task", [(t, t ^ 1) for t in range(4)])


def grad_block(back, flip):
    _, me, y, hi = place()
    return 2 * ((y + 4 + (2 * me - 1) * back) % 4) + (hi ^ flip if flip else hi)


def act_block(back):
    return (lax.axis_index("col") + 8 + (2 * lax.rem(lax.axis_index("task"), 2) - 1) * back) % 8


def fetch(first, grad_from, acts, grads, a, g, sems):
    count, tok, size = a.shape[0], a.shape[1] // 8, a.shape[2]

    def begin():
        for s in range(count):
            for back, piece in enumerate(acts):
                rows = pl.ds(pl.multiple_of(tok * act_block(back), tok), tok)
                src = piece.at[s, :, pl.ds(first, size)]
                pltpu.make_async_copy(src, a.at[s, rows], sems.at[s]).start()
            for meta, piece in zip(grad_from, grads):
                rows = pl.ds(pl.multiple_of(tok * grad_block(*meta), tok), tok)
                pltpu.make_async_copy(piece.at[s], g.at[s, rows], sems.at[s]).start()

    def arrive(s):
        pltpu.make_async_copy(a.at[s], a.at[s], sems.at[s]).wait()
        pltpu.make_async_copy(g.at[s], g.at[s], sems.at[s]).wait()

    return begin, arrive


def square_sum(arrive, count, a, g, f):
    def step(s, _):
        arrive(s)
        d = lax.dot_general(
            a[s], g[s], (((0,), (0,)), ((), ())), preferred_element_type=F32
        )
        f[...] = jnp.where(s == 0, 0.0, f[...]) + d * d
        return 0

    lax.fori_loop(0, count, step, 0)


def first_kernel(n, grad_from, *refs):
    m = len(grad_from)
    acts, grads, (out, a, g, f, sems, osem) = refs[:n], refs[n : n + m], refs[n + m :]
    begin, arrive = fetch(0, grad_from, acts, grads, a, g, sems)
    begin()
    square_sum(arrive, a.shape[0], a, g, f)
    cp = pltpu.make_async_copy(f, out, osem)
    cp.start()
    cp.wait()


def second_kernel(n, grad_from, first, rows, *refs):
    m = len(grad_from)
    acts, grads = refs[:n], refs[n : n + m]
    f1_hbm, w1_hbm, w2_hbm, keep, send, a, g, f, f1, w1, w2, sems, xsem, osem = refs[n + m :]
    begin, arrive = fetch(first, grad_from, acts, grads, a, g, sems)
    count, size = a.shape[0], f.shape[0]
    lo, me, _, _ = place()
    half = size // 2
    own = pl.ds(pl.multiple_of(lo * rows + first, 16), size)
    extra = [
        pltpu.make_async_copy(f1_hbm.at[pl.ds(first, size)], f1, xsem.at[0]),
        pltpu.make_async_copy(w1_hbm.at[0, own], w1, xsem.at[1]),
        pltpu.make_async_copy(w2_hbm.at[pl.ds(first, size)], w2, xsem.at[2]),
    ]
    begin()
    for c in extra:
        c.start()
    square_sum(arrive, count, a, g, f)
    for c in extra:
        c.wait()
    one, two = f1[...], f[...]
    f1[...] = one * w1[...].astype(F32) + two * w2[...].astype(F32)
    f[...] = one + two
    outs = []
    for i, src in enumerate((f1, f)):
        for j, (dst, which) in enumerate(((send, 1 - me), (keep, me))):
            at = pl.ds(pl.multiple_of(which * half, 16), half)
            outs.append(pltpu.make_async_copy(src.at[at], dst.at[i], osem.at[2 * i + j]))
    for c in outs:
        c.start()
    for c in outs:
        c.wait()


def share_kernel(keep, got, out):
    den = keep[1] + got[1]
    out[...] = ((keep[0] + got[0]) / (den + EPS)).astype(BF16)


def whole_kernel(first, rows, *refs):
    own, by_core, by_pair, by_both, out, held, sems, osems = refs[-8:]
    lo, me, _, _ = place()
    n = own.shape[0]
    ins, outs = [], []
    for i, (src, l, c) in enumerate(
        ((own, lo, me), (by_core, lo, 1 - me), (by_pair, 1 - lo, me), (by_both, 1 - lo, 1 - me))
    ):
        at = pl.ds(pl.multiple_of(l * rows + first + c * n, 16), n)
        ins.append(pltpu.make_async_copy(src, held.at[i], sems.at[i]))
        outs.append(pltpu.make_async_copy(held.at[i], out.at[at], osems.at[i]))
    for c in ins:
        c.start()
    for i, o in zip(ins, outs):
        i.wait()
        o.start()
    for c in outs:
        c.wait()


def cost(flops, moved):
    return pl.CostEstimate(flops=flops, bytes_accessed=moved, transcendentals=0)


def body(acts, grads, weights):
    _, count, tok, rows = acts.shape
    cols = grads.shape[3]
    half = rows // 2
    total = tok * 8
    lo = lax.axis_index("task") // 2
    have = {"g": [grads[0]]}

    def part(x, which, axis):
        return lax.dynamic_slice_in_dim(x, which * half, half, axis)

    def run(name, move, source, *after):
        x = have[source[0]][source[1]]
        if after:
            x = lax.optimization_barrier((x, *[have[n][i] for n, i in after]))[0]
        have.setdefault(name, []).append(move(x))

    have["o"] = [part(acts[0], lo, 2)]
    have["give"] = [part(acts[0], 1 - lo, 2)]
    have["wgive"] = [part(weights[0], 1 - lo, 0)]
    for line in ORDER:
        name, source, at, *after = line.replace("<", ",").split(",")
        move = {"o": ring_z, "t": ring_z, "g": ring_y, "d": ring_y, "u": ring_y}.get(name, pair)
        if name == "x" or line.startswith("u,d"):
            move = cross
        if line.startswith(("t,give", "d,g")):
            move = pair
        run(name, move, (source, int(at)), *[(x[0], int(x[1:])) for x in after])

    grad_from = [(k, flip) for flip in (0, 1) for k in range(4)]
    sems = pltpu.SemaphoreType.DMA((count,))
    arrays = [*have["o"], *have["g"], *have["u"]]
    f1 = pl.pallas_call(
        functools.partial(first_kernel, 8, grad_from),
        out_shape=jax.ShapeDtypeStruct((half, cols), F32),
        in_specs=[ANY] * len(arrays),
        out_specs=ANY,
        scratch_shapes=[
            pltpu.VMEM((count, total, half), BF16),
            pltpu.VMEM((count, total, cols), BF16),
            pltpu.VMEM((half, cols), F32),
            sems,
            pltpu.SemaphoreType.DMA,
        ],
        compiler_params=LIMIT,
        cost_estimate=cost(2 * count * total * half * cols, 12 * 2**20),
        name="own_task",
    )(*arrays)
    arrays = [*have["t"], *have["d"], *have["x"], f1, weights, *have["w"]]
    out, first = None, 0
    for size in CHUNKS:
        mine = size // 2
        two = jax.ShapeDtypeStruct((2, mine, cols), F32)
        keep, send = pl.pallas_call(
            functools.partial(second_kernel, 8, grad_from, first, half),
            out_shape=(two, two),
            in_specs=[ANY] * len(arrays),
            out_specs=(ANY, ANY),
            scratch_shapes=[
                pltpu.VMEM((count, total, size), BF16),
                pltpu.VMEM((count, total, cols), BF16),
                pltpu.VMEM((size, cols), F32),
                pltpu.VMEM((size, cols), F32),
                pltpu.VMEM((size, cols), BF16),
                pltpu.VMEM((size, cols), BF16),
                sems,
                pltpu.SemaphoreType.DMA((3,)),
                pltpu.SemaphoreType.DMA((4,)),
            ],
            compiler_params=LIMIT,
            cost_estimate=cost(2 * count * total * size * cols, 12 * 2**20),
            name="other_task",
        )(*arrays)
        got = core(send)
        q = pl.pallas_call(
            share_kernel,
            out_shape=jax.ShapeDtypeStruct((mine, cols), BF16),
            compiler_params=LIMIT,
            name="share",
        )(keep, got)
        by_pair = pair(q)
        by_core = core(q)
        by_both = core(by_pair)
        args = (q, by_core, by_pair, by_both)
        args = args if out is None else (out, *args)
        out = pl.pallas_call(
            functools.partial(whole_kernel, first, half),
            out_shape=jax.ShapeDtypeStruct((rows, cols), BF16),
            in_specs=[ANY] * len(args),
            out_specs=ANY,
            scratch_shapes=[
                pltpu.VMEM((4, mine, cols), BF16),
                pltpu.SemaphoreType.DMA((4,)),
                pltpu.SemaphoreType.DMA((4,)),
            ],
            input_output_aliases={} if out is None else {0: 0},
            compiler_params=LIMIT,
            name="whole",
        )(*args)
        first += size
    return out


def solution(mesh):
    placed = (P("task", None, "col", "row"), P("task", None, "row", "col"), P("task", "row", "col"))
    return jax.shard_map(
        body, mesh=mesh, in_specs=placed, out_specs=P("row", "col"), check_vma=False
    )
```

time: 488 us -> 189 us (0.39)
  waiting for transfers between devices: 406 us -> 65.5 us
  starting transfers between devices: 0.16 us -> 74.1 us
  matrix products: 52.2 us -> 0 us
  Pallas kernels: 0 us -> 36.6 us
  between operations: 13.1 us -> 0.53 us
  other arithmetic: 12.3 us -> 0 us
  local copies, waits for them, and re-layouts: 4.25 us -> 11.8 us
    all_gather x3 -> x0, waiting for transfers between devices: 264 us -> none  [the longest x1 119 us: body(): all_acts = lax.all_gather(acts, 'col', axis=2, tiled=True)]
    reduce_scatter x2 -> x0, waiting for transfers between devices: 141 us -> none  [the longest x1 77 us: body(): lax.psum_scatter(fisher * weights[0].astype(jnp.float32), 'task', scatter...]
    ppermute x0 -> x39, starting transfers between devices: none -> 74.1 us  [the longest x14 29.7 us: ring_z(): return lax.ppermute(x, ('task', 'col'), perm)]
    ppermute x0 -> x39, waiting for transfers between devices: none -> 65.5 us  [the longest x5 21.4 us: pair(): return lax.ppermute(x, 'task', [(t, t ^ 2) for t in range(4)])]
    dot_general x6 -> x0, matrix products: 52.2 us -> none  [outer_square(): lax.dot_general(left, right, (((0,), (0,)), ((), ())), preferred_element_...]
    pallas_call x0 -> x7, Pallas kernels: none -> 36.6 us  [the longest x2 15.5 us: body(): pl.pallas_call(functools.partial(second_kernel, 8, grad_from, first, half...]
    mul x1 -> x0, other arithmetic: 8.98 us -> none  [body(): fisher * weights[0].astype(jnp.float32)]
  transfers between devices with their start and end apart: 5 -> 39, of which waited for: 5 -> 19; matrix products, arithmetic and copies ran while one was open for 2% -> 2% of each run, Pallas kernels for 0% -> 14%
where the time goes in v2:
time: 189 us
  starting transfers between devices  74.1 us (39%)
  waiting for transfers between devices  65.5 us (35%)
  Pallas kernels  36.6 us (19%)
  local copies, waits for them, and re-layouts  11.8 us (6%)
    ppermute x14, starting transfers between devices, ring_z(): return lax.ppermute(x, ('task', 'col'), perm)  29.7 us
    ppermute x9, starting transfers between devices, ring_y(): return lax.ppermute(x, ('task', 'row'), perm)  22 us
    ppermute x5, waiting for transfers between devices, pair(): return lax.ppermute(x, 'task', [(t, t ^ 2) for t in range(4)])  21.4 us
    ppermute x14, waiting for transfers between devices, ring_z(): return lax.ppermute(x, ('task', 'col'), perm)  18.6 us
    pallas_call x2, Pallas kernels, body(): pl.pallas_call(functools.partial(second_kernel, 8, grad_from, first, half...  15.5 us
    ppermute x5, waiting for transfers between devices, cross(): return lax.ppermute(x, ('task', 'row'), perm)  13.5 us
    ppermute x9, waiting for transfers between devices, ring_y(): return lax.ppermute(x, ('task', 'row'), perm)  12 us
    ppermute x5, starting transfers between devices, cross(): return lax.ppermute(x, ('task', 'row'), perm)  11.8 us
  transfers between devices with their start and end apart: 39, of which 19 were waited for; matrix products, arithmetic and copies ran while one was open for 2% of the time, Pallas kernels for 14%

profile of v2, /device:TPU:1, one launch (start us, length us, event | category | flops | bytes accessed | tf_op | source)
XLA Modules:
  0.0 188.5 jit_solution(12204402098150837959)
XLA Ops:
  3.6 5.6 %collective-permute-start.23 = (bf16[6,64,896]{2,1,0:T(8,128)(2,1)S(1)}, bf16[6,64,896]{2,1,0:T(8,128)(2,1)S(1)}, u32[]{:S(2)}, u32[]{:S(2)}) collective-permute-start(bf16[6,64,896]{2,1,0:T(8,128)(2,1)S(1)} %get-tuple-element.21.refs_0_), channel_id=1, source_target_pairs={{0,1},{1,2},{2,3},{3,4},{4,5},{5,6},{6,7},{7,0},{64,71},{65,64},{6... | collective-permute-start | bytes 2064392 | tf_op jit(solution)/shard_map/ppermute | solution.py:69
  9.2 2.7 %collective-permute-start.5 = (bf16[6,64,1024]{2,1,0:T(8,128)(2,1)S(1)}, bf16[6,64,1024]{2,1,0:T(8,128)(2,1)S(1)}, u32[]{:S(2)}, u32[]{:S(2)}) collective-permute-start(bf16[6,64,1024]{2,1,0:T(8,128)(2,1)S(1)} %bitcast.8), channel_id=1, source_target_pairs={{0,16},{8,24},{16,32},{24,40},{32,48},{40,56},{48,0},{56,8},{64,11... | collective-permute-start | bytes 2359304 | tf_op jit(solution)/shard_map/ppermute | solution.py:64
  11.9 5.5 %collective-permute-done.refs_0_ = bf16[6,64,896]{2,1,0:T(8,128)(2,1)S(1)} collective-permute-done((bf16[6,64,896]{2,1,0:T(8,128)(2,1)S(1)}, bf16[6,64,896]{2,1,0:T(8,128)(2,1)S(1)}, u32[]{:S(2)}, u32[]{:S(2)}) %collective-permute-start) | collective-permute-done | bytes 688160 | tf_op jit(solution)/shard_map/ppermute | solution.py:78
  17.5 6.8 %collective-permute-start.1 = (bf16[6,64,896]{2,1,0:T(8,128)(2,1)S(1)}, bf16[6,64,896]{2,1,0:T(8,128)(2,1)S(1)}, u32[]{:S(2)}, u32[]{:S(2)}) collective-permute-start(bf16[6,64,896]{2,1,0:T(8,128)(2,1)S(1)} %collective-permute-done.refs_0_), channel_id=1, source_target_pairs={{0,1},{1,2},{2,3},{3,4},{4,5},{5,6},{6,7},{7,0},{64,71},{65,64},{6... | collective-permute-start | bytes 2064392 | tf_op jit(solution)/shard_map/ppermute | solution.py:69
  28.1 2.7 %collective-permute-start.6 = (bf16[6,64,1024]{2,1,0:T(8,128)(2,1)S(1)}, bf16[6,64,1024]{2,1,0:T(8,128)(2,1)S(1)}, u32[]{:S(2)}, u32[]{:S(2)}) collective-permute-start(bf16[6,64,1024]{2,1,0:T(8,128)(2,1)S(1)} %collective-permute-done.5.refs_9_), channel_id=1, source_target_pairs={{0,16},{8,24},{16,32},{24,40},{32,48},{40,56},{48,0},{56,8},{64,11... | collective-permute-start | bytes 2359304 | tf_op jit(solution)/shard_map/ppermute | solution.py:64
  32.2 3.4 %collective-permute-start.2 = (bf16[6,64,896]{2,1,0:T(8,128)(2,1)S(1)}, bf16[6,64,896]{2,1,0:T(8,128)(2,1)S(1)}, u32[]{:S(2)}, u32[]{:S(2)}) collective-permute-start(bf16[6,64,896]{2,1,0:T(8,128)(2,1)S(1)} %collective-permute-done.1.refs_1_), channel_id=1, source_target_pairs={{0,1},{1,2},{2,3},{3,4},{4,5},{5,6},{6,7},{7,0},{64,71},{65,64},{6... | collective-permute-start | bytes 2064392 | tf_op jit(solution)/shard_map/ppermute | solution.py:69
  35.6 4.0 %collective-permute-done.24.refs_2_ = bf16[6,64,896]{2,1,0:T(8,128)(2,1)S(1)} collective-permute-done((bf16[6,64,896]{2,1,0:T(8,128)(2,1)S(1)}, bf16[6,64,896]{2,1,0:T(8,128)(2,1)S(1)}, u32[]{:S(2)}, u32[]{:S(2)}) %collective-permute-start.24) | collective-permute-done | bytes 688160 | tf_op jit(solution)/shard_map/ppermute | solution.py:69
  39.6 3.4 %collective-permute-start.25 = (bf16[6,64,896]{2,1,0:T(8,128)(2,1)S(1)}, bf16[6,64,896]{2,1,0:T(8,128)(2,1)S(1)}, u32[]{:S(2)}, u32[]{:S(2)}) collective-permute-start(bf16[6,64,896]{2,1,0:T(8,128)(2,1)S(1)} %collective-permute-done.24.refs_2_), channel_id=1, source_target_pairs={{0,1},{1,2},{2,3},{3,4},{4,5},{5,6},{6,7},{7,0},{64,71},{65,64},{6... | collective-permute-start | bytes 2064392 | tf_op jit(solution)/shard_map/ppermute | solution.py:69
  44.1 2.5 %collective-permute-start.16 = (bf16[6,64,1024]{2,1,0:T(8,128)(2,1)S(1)}, bf16[6,64,1024]{2,1,0:T(8,128)(2,1)S(1)}, u32[]{:S(2)}, u32[]{:S(2)}) collective-permute-start(bf16[6,64,1024]{2,1,0:T(8,128)(2,1)S(1)} %collective-permute-done.10.refs_8_), channel_id=1, source_target_pairs={{0,136},{8,128},{16,152},{24,144},{32,168},{40,160},{48,184},{56,1... | collective-permute-start | bytes 2359304 | tf_op jit(solution)/shard_map/ppermute | solution.py:74
  46.8 2.7 %collective-permute-start.11 = (bf16[6,64,1024]{2,1,0:T(8,128)(2,1)S(1)}, bf16[6,64,1024]{2,1,0:T(8,128)(2,1)S(1)}, u32[]{:S(2)}, u32[]{:S(2)}) collective-permute-start(bf16[6,64,1024]{2,1,0:T(8,128)(2,1)S(1)} %collective-permute-done.10.refs_8_), channel_id=1, source_target_pairs={{0,16},{8,24},{16,32},{24,40},{32,48},{40,56},{48,0},{56,8},{64,11... | collective-permute-start | bytes 2359304 | tf_op jit(solution)/shard_map/ppermute | solution.py:64
  50.3 4.0 %collective-permute-done.25.refs_3_ = bf16[6,64,896]{2,1,0:T(8,128)(2,1)S(1)} collective-permute-done((bf16[6,64,896]{2,1,0:T(8,128)(2,1)S(1)}, bf16[6,64,896]{2,1,0:T(8,128)(2,1)S(1)}, u32[]{:S(2)}, u32[]{:S(2)}) %collective-permute-start.25) | collective-permute-done | bytes 688160 | tf_op jit(solution)/shard_map/ppermute | solution.py:69
  54.3 3.4 %collective-permute-start.26 = (bf16[6,64,896]{2,1,0:T(8,128)(2,1)S(1)}, bf16[6,64,896]{2,1,0:T(8,128)(2,1)S(1)}, u32[]{:S(2)}, u32[]{:S(2)}) collective-permute-start(bf16[6,64,896]{2,1,0:T(8,128)(2,1)S(1)} %collective-permute-done.25.refs_3_), channel_id=1, source_target_pairs={{0,1},{1,2},{2,3},{3,4},{4,5},{5,6},{6,7},{7,0},{64,71},{65,64},{6... | collective-permute-start | bytes 2064392 | tf_op jit(solution)/shard_map/ppermute | solution.py:69
  57.7 6.9 %collective-permute-done.16.refs_12_ = bf16[6,64,1024]{2,1,0:T(8,128)(2,1)S(1)} collective-permute-done((bf16[6,64,1024]{2,1,0:T(8,128)(2,1)S(1)}, bf16[6,64,1024]{2,1,0:T(8,128)(2,1)S(1)}, u32[]{:S(2)}, u32[]{:S(2)}) %collective-permute-start.16) | collective-permute-done | bytes 786464 | tf_op jit(solution)/shard_map/ppermute | solution.py:74
  64.6 2.6 %collective-permute-start.17 = (bf16[6,64,1024]{2,1,0:T(8,128)(2,1)S(1)}, bf16[6,64,1024]{2,1,0:T(8,128)(2,1)S(1)}, u32[]{:S(2)}, u32[]{:S(2)}) collective-permute-start(bf16[6,64,1024]{2,1,0:T(8,128)(2,1)S(1)} %collective-permute-done.16.refs_12_), channel_id=1, source_target_pairs={{0,16},{8,24},{16,32},{24,40},{32,48},{40,56},{48,0},{56,8},{64,11... | collective-permute-start | bytes 2359304 | tf_op jit(solution)/shard_map/ppermute | solution.py:64
  69.1 3.4 %collective-permute-start.27 = (bf16[6,64,896]{2,1,0:T(8,128)(2,1)S(1)}, bf16[6,64,896]{2,1,0:T(8,128)(2,1)S(1)}, u32[]{:S(2)}, u32[]{:S(2)}) collective-permute-start(bf16[6,64,896]{2,1,0:T(8,128)(2,1)S(1)} %collective-permute-done.26.refs_4_), channel_id=1, source_target_pairs={{0,1},{1,2},{2,3},{3,4},{4,5},{5,6},{6,7},{7,0},{64,71},{65,64},{6... | collective-permute-start | bytes 2064392 | tf_op jit(solution)/shard_map/ppermute | solution.py:69
  76.2 3.4 %collective-permute-start.18 = (bf16[6,64,1024]{2,1,0:T(8,128)(2,1)S(1)}, bf16[6,64,1024]{2,1,0:T(8,128)(2,1)S(1)}, u32[]{:S(2)}, u32[]{:S(2)}) collective-permute-start(bf16[6,64,1024]{2,1,0:T(8,128)(2,1)S(1)} %collective-permute-done.17.refs_13_), channel_id=1, source_target_pairs={{0,16},{8,24},{16,32},{24,40},{32,48},{40,56},{48,0},{56,8},{64,11... | collective-permute-start | bytes 2359304 | tf_op jit(solution)/shard_map/ppermute | solution.py:64
  79.6 5.0 %collective-permute-done.12.refs_10_ = bf16[6,64,1024]{2,1,0:T(8,128)(2,1)S(1)} collective-permute-done((bf16[6,64,1024]{2,1,0:T(8,128)(2,1)S(1)}, bf16[6,64,1024]{2,1,0:T(8,128)(2,1)S(1)}, u32[]{:S(2)}, u32[]{:S(2)}) %collective-permute-start.12) | collective-permute-done | bytes 786464 | tf_op jit(solution)/shard_map/ppermute | solution.py:64
  84.6 3.4 %collective-permute-start.13 = (bf16[6,64,1024]{2,1,0:T(8,128)(2,1)S(1)}, bf16[6,64,1024]{2,1,0:T(8,128)(2,1)S(1)}, u32[]{:S(2)}, u32[]{:S(2)}) collective-permute-start(bf16[6,64,1024]{2,1,0:T(8,128)(2,1)S(1)} %collective-permute-done.12.refs_10_), channel_id=1, source_target_pairs={{0,16},{8,24},{16,32},{24,40},{32,48},{40,56},{48,0},{56,8},{64,11... | collective-permute-start | bytes 2359304 | tf_op jit(solution)/shard_map/ppermute | solution.py:64
  88.3 3.1 %dynamic-slice_bitcast_fusion = bf16[896,1024]{1,0:T(8,128)(2,1)} fusion(bf16[1,1792,1024]{2,1,0:T(8,128)(2,1)} %refs_17_.3, s32[]{:T(128)S(6)} %select_n.13), kind=kLoop, calls=%fused_computation | loop fusion | bytes 3670020 | tf_op jit(solution)/shard_map/dynamic_slice | solution.py:209
  93.2 2.6 %collective-permute-start.20 = (bf16[6,64,1024]{2,1,0:T(8,128)(2,1)S(1)}, bf16[6,64,1024]{2,1,0:T(8,128)(2,1)S(1)}, u32[]{:S(2)}, u32[]{:S(2)}) collective-permute-start(bf16[6,64,1024]{2,1,0:T(8,128)(2,1)S(1)} %collective-permute-done.6.refs_10_), channel_id=1, source_target_pairs={{0,136},{8,128},{16,152},{24,144},{32,168},{40,160},{48,184},{56,1... | collective-permute-start | bytes 2359304 | tf_op jit(solution)/shard_map/ppermute | solution.py:74
  95.7 5.7 %collective-permute-done.13.refs_11_ = bf16[6,64,1024]{2,1,0:T(8,128)(2,1)S(1)} collective-permute-done((bf16[6,64,1024]{2,1,0:T(8,128)(2,1)S(1)}, bf16[6,64,1024]{2,1,0:T(8,128)(2,1)S(1)}, u32[]{:S(2)}, u32[]{:S(2)}) %collective-permute-start.13) | collective-permute-done | bytes 786464 | tf_op jit(solution)/shard_map/ppermute | solution.py:64
  101.5 3.4 %collective-permute-start.19 = (bf16[6,64,1024]{2,1,0:T(8,128)(2,1)S(1)}, bf16[6,64,1024]{2,1,0:T(8,128)(2,1)S(1)}, u32[]{:S(2)}, u32[]{:S(2)}) collective-permute-start(bf16[6,64,1024]{2,1,0:T(8,128)(2,1)S(1)} %collective-permute-done.18.refs_14_), channel_id=1, source_target_pairs={{0,16},{8,24},{16,32},{24,40},{32,48},{40,56},{48,0},{56,8},{64,11... | collective-permute-start | bytes 2359304 | tf_op jit(solution)/shard_map/ppermute | solution.py:64
  106.8 4.7 %collective-permute-done.20.refs_14_ = bf16[6,64,1024]{2,1,0:T(8,128)(2,1)S(1)} collective-permute-done((bf16[6,64,1024]{2,1,0:T(8,128)(2,1)S(1)}, bf16[6,64,1024]{2,1,0:T(8,128)(2,1)S(1)}, u32[]{:S(2)}, u32[]{:S(2)}) %collective-permute-start.20) | collective-permute-done | bytes 786464 | tf_op jit(solution)/shard_map/ppermute | solution.py:74
  111.5 2.5 %collective-permute-start.22 = (bf16[6,64,1024]{2,1,0:T(8,128)(2,1)}, bf16[6,64,1024]{2,1,0:T(8,128)(2,1)S(1)}, u32[]{:S(2)}, u32[]{:S(2)}) collective-permute-start(bf16[6,64,1024]{2,1,0:T(8,128)(2,1)} %collective-permute-done.7.refs_11_), channel_id=1, source_target_pairs={{0,136},{8,128},{16,152},{24,144},{32,168},{40,160},{48,184},{56,1... | collective-permute-start | bytes 2359304 | tf_op jit(solution)/shard_map/ppermute | solution.py:74
  116.2 6.2 %collective-permute-done.29.refs_7_ = bf16[6,64,896]{2,1,0:T(8,128)(2,1)} collective-permute-done((bf16[6,64,896]{2,1,0:T(8,128)(2,1)S(1)}, bf16[6,64,896]{2,1,0:T(8,128)(2,1)}, u32[]{:S(2)}, u32[]{:S(2)}) %collective-permute-start.29) | collective-permute-done | bytes 688160 | tf_op jit(solution)/shard_map/ppermute | solution.py:69
  122.5 10.5 %own_task.1.refs_16_ = f32[896,1024]{1,0:T(8,128)} custom-call(bf16[6,64,896]{2,1,0:T(8,128)(2,1)} %copy-done.18, bf16[6,64,896]{2,1,0:T(8,128)(2,1)} %copy-done.32, bf16[6,64,896]{2,1,0:T(8,128)(2,1)} %copy-done.33, bf16[6,64,896]{2,1,0:T(8,128)(2,1)} %copy-done.34, bf16[6,64,896]{2,1,0:T(8,128)(2,1)} %copy-done.35, bf16[6,64,896]{2,1,0:T(8,128)(2,1)} %copy-done.36, ...), custom_call_target="tpu_custom_call" | custom-call | flops 5637144576 | bytes 12582912 | tf_op jit(solution)/shard_map/own_task/pallas_call | solution.py:232
  136.2 8.4 %other_task.2 = (f32[2,256,1024]{2,1,0:T(8,128)}, f32[2,256,1024]{2,1,0:T(8,128)}) custom-call(bf16[6,64,896]{2,1,0:T(8,128)(2,1)} %copy-done.9, bf16[6,64,896]{2,1,0:T(8,128)(2,1)} %copy-done.10, bf16[6,64,896]{2,1,0:T(8,128)(2,1)} %copy-done.11, bf16[6,64,896]{2,1,0:T(8,128)(2,1)} %copy-done.12, bf16[6,64,896]{2,1,0:T(8,128)(2,1)} %copy-done.13, ...), custom_call_target="tpu_custom_call" | custom-call | flops 3221225472 | bytes 12582912 | tf_op jit(solution)/shard_map/other_task/pallas_call | solution.py:253
  145.8 7.1 %other_task.3 = (f32[2,192,1024]{2,1,0:T(8,128)}, f32[2,192,1024]{2,1,0:T(8,128)}) custom-call(bf16[6,64,896]{2,1,0:T(8,128)(2,1)} %copy-done.9, bf16[6,64,896]{2,1,0:T(8,128)(2,1)} %copy-done.10, bf16[6,64,896]{2,1,0:T(8,128)(2,1)} %copy-done.11, bf16[6,64,896]{2,1,0:T(8,128)(2,1)} %copy-done.12, bf16[6,64,896]{2,1,0:T(8,128)(2,1)} %copy-done.13, ...), custom_call_target="tpu_custom_call" | custom-call | flops 2415919104 | bytes 12582912 | tf_op jit(solution)/shard_map/other_task/pallas_call | solution.py:253
  154.4 3.2 %share.2.refs_0_ = bf16[256,1024]{1,0:T(8,128)(2,1)} custom-call(f32[2,256,1024]{2,1,0:T(8,128)} %get-tuple-element.17.keep, f32[2,256,1024]{2,1,0:T(8,128)} %copy-done.15), custom_call_target="tpu_custom_call" | custom-call | tf_op jit(solution)/shard_map/share/pallas_call | solution.py:274
  158.8 2.8 %share.3.refs_1_ = bf16[192,1024]{1,0:T(8,128)(2,1)} custom-call(f32[2,192,1024]{2,1,0:T(8,128)} %get-tuple-element.19.keep, f32[2,192,1024]{2,1,0:T(8,128)} %copy-done.17), custom_call_target="tpu_custom_call" | custom-call | tf_op jit(solution)/shard_map/share/pallas_call | solution.py:274
  164.0 6.8 %collective-permute-done.33.refs_2_ = bf16[256,1024]{1,0:T(8,128)(2,1)S(1)} collective-permute-done((bf16[256,1024]{1,0:T(8,128)(2,1)}, bf16[256,1024]{1,0:T(8,128)(2,1)S(1)}, u32[]{:S(2)}, u32[]{:S(2)}) %collective-permute-start.33) | collective-permute-done | bytes 524320 | tf_op jit(solution)/shard_map/ppermute | solution.py:78
  173.1 6.2 %collective-permute-done.37.refs_3_ = bf16[192,1024]{1,0:T(8,128)(2,1)S(1)} collective-permute-done((bf16[192,1024]{1,0:T(8,128)(2,1)}, bf16[192,1024]{1,0:T(8,128)(2,1)S(1)}, u32[]{:S(2)}, u32[]{:S(2)}) %collective-permute-start.37) | collective-permute-done | bytes 393248 | tf_op jit(solution)/shard_map/ppermute | solution.py:78
  (131 shorter events, 43.1 us)
Async XLA Ops:
  1.5 15.9 %collective-permute-start = (bf16[6,64,896]{2,1,0:T(8,128)(2,1)S(1)}, bf16[6,64,896]{2,1,0:T(8,128)(2,1)S(1)}, u32[]{:S(2)}, u32[]{:S(2)}) collective-permute-start(bf16[6,64,896]{2,1,0:T(8,128)(2,1)S(1)} %get-tuple-element.22), channel_id=1, source_target_pairs={{0,128},{64,192},{128,0},{192,64},{1,129},{65,193},{129,1},{193,65... | collective-permute-start | bytes 2064392 | tf_op jit(solution)/shard_map/ppermute | solution.py:78
  3.6 20.7 %collective-permute-start.23 = (bf16[6,64,896]{2,1,0:T(8,128)(2,1)S(1)}, bf16[6,64,896]{2,1,0:T(8,128)(2,1)S(1)}, u32[]{:S(2)}, u32[]{:S(2)}) collective-permute-start(bf16[6,64,896]{2,1,0:T(8,128)(2,1)S(1)} %get-tuple-element.21.refs_0_), channel_id=1, source_target_pairs={{0,1},{1,2},{2,3},{3,4},{4,5},{5,6},{6,7},{7,0},{64,71},{65,64},{6... | collective-permute-start | bytes 2064392 | tf_op jit(solution)/shard_map/ppermute | solution.py:69
  9.2 18.9 %collective-permute-start.5 = (bf16[6,64,1024]{2,1,0:T(8,128)(2,1)S(1)}, bf16[6,64,1024]{2,1,0:T(8,128)(2,1)S(1)}, u32[]{:S(2)}, u32[]{:S(2)}) collective-permute-start(bf16[6,64,1024]{2,1,0:T(8,128)(2,1)S(1)} %bitcast.8), channel_id=1, source_target_pairs={{0,16},{8,24},{16,32},{24,40},{32,48},{40,56},{48,0},{56,8},{64,11... | collective-permute-start | bytes 2359304 | tf_op jit(solution)/shard_map/ppermute | solution.py:64
  17.5 14.7 %collective-permute-start.1 = (bf16[6,64,896]{2,1,0:T(8,128)(2,1)S(1)}, bf16[6,64,896]{2,1,0:T(8,128)(2,1)S(1)}, u32[]{:S(2)}, u32[]{:S(2)}) collective-permute-start(bf16[6,64,896]{2,1,0:T(8,128)(2,1)S(1)} %collective-permute-done.refs_0_), channel_id=1, source_target_pairs={{0,1},{1,2},{2,3},{3,4},{4,5},{5,6},{6,7},{7,0},{64,71},{65,64},{6... | collective-permute-start | bytes 2064392 | tf_op jit(solution)/shard_map/ppermute | solution.py:69
  24.3 15.2 %collective-permute-start.24 = (bf16[6,64,896]{2,1,0:T(8,128)(2,1)S(1)}, bf16[6,64,896]{2,1,0:T(8,128)(2,1)S(1)}, u32[]{:S(2)}, u32[]{:S(2)}) collective-permute-start(bf16[6,64,896]{2,1,0:T(8,128)(2,1)S(1)} %collective-permute-done.23.refs_1_), channel_id=1, source_target_pairs={{0,1},{1,2},{2,3},{3,4},{4,5},{5,6},{6,7},{7,0},{64,71},{65,64},{6... | collective-permute-start | bytes 2064392 | tf_op jit(solution)/shard_map/ppermute | solution.py:69
  25.0 19.1 %collective-permute-start.10 = (bf16[6,64,1024]{2,1,0:T(8,128)(2,1)S(1)}, bf16[6,64,1024]{2,1,0:T(8,128)(2,1)S(1)}, u32[]{:S(2)}, u32[]{:S(2)}) collective-permute-start(bf16[6,64,1024]{2,1,0:T(8,128)(2,1)S(1)} %bitcast.9), channel_id=1, source_target_pairs={{0,128},{64,192},{128,0},{192,64},{1,129},{65,193},{129,1},{193,65... | collective-permute-start | bytes 2359304 | tf_op jit(solution)/shard_map/ppermute | solution.py:78
  26.3 20.6 %collective-permute-start.4 = (bf16[6,64,1024]{2,1,0:T(8,128)(2,1)S(1)}, bf16[6,64,1024]{2,1,0:T(8,128)(2,1)S(1)}, u32[]{:S(2)}, u32[]{:S(2)}) collective-permute-start(bf16[6,64,1024]{2,1,0:T(8,128)(2,1)S(1)} %bitcast.10), channel_id=1, source_target_pairs={{0,136},{8,128},{16,152},{24,144},{32,168},{40,160},{48,184},{56,1... | collective-permute-start | bytes 2359304 | tf_op jit(solution)/shard_map/ppermute | solution.py:74
  28.1 21.5 %collective-permute-start.6 = (bf16[6,64,1024]{2,1,0:T(8,128)(2,1)S(1)}, bf16[6,64,1024]{2,1,0:T(8,128)(2,1)S(1)}, u32[]{:S(2)}, u32[]{:S(2)}) collective-permute-start(bf16[6,64,1024]{2,1,0:T(8,128)(2,1)S(1)} %collective-permute-done.5.refs_9_), channel_id=1, source_target_pairs={{0,16},{8,24},{16,32},{24,40},{32,48},{40,56},{48,0},{56,8},{64,11... | collective-permute-start | bytes 2359304 | tf_op jit(solution)/shard_map/ppermute | solution.py:64
  32.2 17.9 %collective-permute-start.2 = (bf16[6,64,896]{2,1,0:T(8,128)(2,1)S(1)}, bf16[6,64,896]{2,1,0:T(8,128)(2,1)S(1)}, u32[]{:S(2)}, u32[]{:S(2)}) collective-permute-start(bf16[6,64,896]{2,1,0:T(8,128)(2,1)S(1)} %collective-permute-done.1.refs_1_), channel_id=1, source_target_pairs={{0,1},{1,2},{2,3},{3,4},{4,5},{5,6},{6,7},{7,0},{64,71},{65,64},{6... | collective-permute-start | bytes 2064392 | tf_op jit(solution)/shard_map/ppermute | solution.py:69
  39.6 14.7 %collective-permute-start.25 = (bf16[6,64,896]{2,1,0:T(8,128)(2,1)S(1)}, bf16[6,64,896]{2,1,0:T(8,128)(2,1)S(1)}, u32[]{:S(2)}, u32[]{:S(2)}) collective-permute-start(bf16[6,64,896]{2,1,0:T(8,128)(2,1)S(1)} %collective-permute-done.24.refs_2_), channel_id=1, source_target_pairs={{0,1},{1,2},{2,3},{3,4},{4,5},{5,6},{6,7},{7,0},{64,71},{65,64},{6... | collective-permute-start | bytes 2064392 | tf_op jit(solution)/shard_map/ppermute | solution.py:69
  44.1 20.5 %collective-permute-start.16 = (bf16[6,64,1024]{2,1,0:T(8,128)(2,1)S(1)}, bf16[6,64,1024]{2,1,0:T(8,128)(2,1)S(1)}, u32[]{:S(2)}, u32[]{:S(2)}) collective-permute-start(bf16[6,64,1024]{2,1,0:T(8,128)(2,1)S(1)} %collective-permute-done.10.refs_8_), channel_id=1, source_target_pairs={{0,136},{8,128},{16,152},{24,144},{32,168},{40,160},{48,184},{56,1... | collective-permute-start | bytes 2359304 | tf_op jit(solution)/shard_map/ppermute | solution.py:74
  46.8 20.4 %collective-permute-start.11 = (bf16[6,64,1024]{2,1,0:T(8,128)(2,1)S(1)}, bf16[6,64,1024]{2,1,0:T(8,128)(2,1)S(1)}, u32[]{:S(2)}, u32[]{:S(2)}) collective-permute-start(bf16[6,64,1024]{2,1,0:T(8,128)(2,1)S(1)} %collective-permute-done.10.refs_8_), channel_id=1, source_target_pairs={{0,16},{8,24},{16,32},{24,40},{32,48},{40,56},{48,0},{56,8},{64,11... | collective-permute-start | bytes 2359304 | tf_op jit(solution)/shard_map/ppermute | solution.py:64
  49.6 18.2 %collective-permute-start.7 = (bf16[6,64,1024]{2,1,0:T(8,128)(2,1)S(1)}, bf16[6,64,1024]{2,1,0:T(8,128)(2,1)}, u32[]{:S(2)}, u32[]{:S(2)}) collective-permute-start(bf16[6,64,1024]{2,1,0:T(8,128)(2,1)S(1)} %collective-permute-done.6.refs_10_), channel_id=1, source_target_pairs={{0,16},{8,24},{16,32},{24,40},{32,48},{40,56},{48,0},{56,8},{64,11... | collective-permute-start | bytes 2359304 | tf_op jit(solution)/shard_map/ppermute | solution.py:64
  50.1 17.7 %collective-permute-start.3 = (bf16[6,64,896]{2,1,0:T(8,128)(2,1)S(1)}, bf16[6,64,896]{2,1,0:T(8,128)(2,1)S(1)}, u32[]{:S(2)}, u32[]{:S(2)}) collective-permute-start(bf16[6,64,896]{2,1,0:T(8,128)(2,1)S(1)} %collective-permute-done.2.refs_2_), channel_id=1, source_target_pairs={{0,1},{1,2},{2,3},{3,4},{4,5},{5,6},{6,7},{7,0},{64,71},{65,64},{6... | collective-permute-start | bytes 2064392 | tf_op jit(solution)/shard_map/ppermute | solution.py:69
  54.3 14.7 %collective-permute-start.26 = (bf16[6,64,896]{2,1,0:T(8,128)(2,1)S(1)}, bf16[6,64,896]{2,1,0:T(8,128)(2,1)S(1)}, u32[]{:S(2)}, u32[]{:S(2)}) collective-permute-start(bf16[6,64,896]{2,1,0:T(8,128)(2,1)S(1)} %collective-permute-done.25.refs_3_), channel_id=1, source_target_pairs={{0,1},{1,2},{2,3},{3,4},{4,5},{5,6},{6,7},{7,0},{64,71},{65,64},{6... | collective-permute-start | bytes 2064392 | tf_op jit(solution)/shard_map/ppermute | solution.py:69
  67.3 17.4 %collective-permute-start.12 = (bf16[6,64,1024]{2,1,0:T(8,128)(2,1)S(1)}, bf16[6,64,1024]{2,1,0:T(8,128)(2,1)S(1)}, u32[]{:S(2)}, u32[]{:S(2)}) collective-permute-start(bf16[6,64,1024]{2,1,0:T(8,128)(2,1)S(1)} %collective-permute-done.11.refs_9_), channel_id=1, source_target_pairs={{0,16},{8,24},{16,32},{24,40},{32,48},{40,56},{48,0},{56,8},{64,11... | collective-permute-start | bytes 2359304 | tf_op jit(solution)/shard_map/ppermute | solution.py:64
  67.7 20.3 %collective-permute-start.8 = (bf16[6,64,896]{2,1,0:T(8,128)(2,1)S(1)}, bf16[6,64,896]{2,1,0:T(8,128)(2,1)S(1)}, u32[]{:S(2)}, u32[]{:S(2)}) collective-permute-start(bf16[6,64,896]{2,1,0:T(8,128)(2,1)S(1)} %collective-permute-done.3.refs_3_), channel_id=1, source_target_pairs={{0,1},{1,2},{2,3},{3,4},{4,5},{5,6},{6,7},{7,0},{64,71},{65,64},{6... | collective-permute-start | bytes 2064392 | tf_op jit(solution)/shard_map/ppermute | solution.py:69
  69.1 19.1 %collective-permute-start.27 = (bf16[6,64,896]{2,1,0:T(8,128)(2,1)S(1)}, bf16[6,64,896]{2,1,0:T(8,128)(2,1)S(1)}, u32[]{:S(2)}, u32[]{:S(2)}) collective-permute-start(bf16[6,64,896]{2,1,0:T(8,128)(2,1)S(1)} %collective-permute-done.26.refs_4_), channel_id=1, source_target_pairs={{0,1},{1,2},{2,3},{3,4},{4,5},{5,6},{6,7},{7,0},{64,71},{65,64},{6... | collective-permute-start | bytes 2064392 | tf_op jit(solution)/shard_map/ppermute | solution.py:69
  72.5 20.7 %collective-permute-start.14 = (bf16[6,64,1024]{2,1,0:T(8,128)(2,1)S(1)}, bf16[6,64,1024]{2,1,0:T(8,128)(2,1)S(1)}, u32[]{:S(2)}, u32[]{:S(2)}) collective-permute-start(bf16[6,64,1024]{2,1,0:T(8,128)(2,1)S(1)} %collective-permute-done.5.refs_9_), channel_id=1, source_target_pairs={{0,136},{8,128},{16,152},{24,144},{32,168},{40,160},{48,184},{56,1... | collective-permute-start | bytes 2359304 | tf_op jit(solution)/shard_map/ppermute | solution.py:74
  76.2 17.0 %collective-permute-start.18 = (bf16[6,64,1024]{2,1,0:T(8,128)(2,1)S(1)}, bf16[6,64,1024]{2,1,0:T(8,128)(2,1)S(1)}, u32[]{:S(2)}, u32[]{:S(2)}) collective-permute-start(bf16[6,64,1024]{2,1,0:T(8,128)(2,1)S(1)} %collective-permute-done.17.refs_13_), channel_id=1, source_target_pairs={{0,16},{8,24},{16,32},{24,40},{32,48},{40,56},{48,0},{56,8},{64,11... | collective-permute-start | bytes 2359304 | tf_op jit(solution)/shard_map/ppermute | solution.py:64
  84.6 16.8 %collective-permute-start.13 = (bf16[6,64,1024]{2,1,0:T(8,128)(2,1)S(1)}, bf16[6,64,1024]{2,1,0:T(8,128)(2,1)S(1)}, u32[]{:S(2)}, u32[]{:S(2)}) collective-permute-start(bf16[6,64,1024]{2,1,0:T(8,128)(2,1)S(1)} %collective-permute-done.12.refs_10_), channel_id=1, source_target_pairs={{0,16},{8,24},{16,32},{24,40},{32,48},{40,56},{48,0},{56,8},{64,11... | collective-permute-start | bytes 2359304 | tf_op jit(solution)/shard_map/ppermute | solution.py:64
  88.1 16.8 %collective-permute-start.9 = (bf16[6,64,896]{2,1,0:T(8,128)(2,1)S(1)}, bf16[6,64,896]{2,1,0:T(8,128)(2,1)S(1)}, u32[]{:S(2)}, u32[]{:S(2)}) collective-permute-start(bf16[6,64,896]{2,1,0:T(8,128)(2,1)S(1)} %collective-permute-done.8.refs_4_), channel_id=1, source_target_pairs={{0,1},{1,2},{2,3},{3,4},{4,5},{5,6},{6,7},{7,0},{64,71},{65,64},{6... | collective-permute-start | bytes 2064392 | tf_op jit(solution)/shard_map/ppermute | solution.py:69
  88.2 17.4 %collective-permute-start.28 = (bf16[6,64,896]{2,1,0:T(8,128)(2,1)S(1)}, bf16[6,64,896]{2,1,0:T(8,128)(2,1)S(1)}, u32[]{:S(2)}, u32[]{:S(2)}) collective-permute-start(bf16[6,64,896]{2,1,0:T(8,128)(2,1)S(1)} %collective-permute-done.27.refs_5_), channel_id=1, source_target_pairs={{0,1},{1,2},{2,3},{3,4},{4,5},{5,6},{6,7},{7,0},{64,71},{65,64},{6... | collective-permute-start | bytes 2064392 | tf_op jit(solution)/shard_map/ppermute | solution.py:69
  93.2 41.5 %collective-permute-start.30 = (bf16[896,1024]{1,0:T(8,128)(2,1)}, bf16[896,1024]{1,0:T(8,128)(2,1)S(1)}, u32[]{:S(2)}, u32[]{:S(2)}) collective-permute-start(bf16[896,1024]{1,0:T(8,128)(2,1)} %dynamic-slice_bitcast_fusion), channel_id=1, source_target_pairs={{0,128},{64,192},{128,0},{192,64},{1,129},{65,193},{129,1},{193,65... | collective-permute-start | bytes 5505032 | tf_op jit(solution)/shard_map/ppermute | solution.py:78
  93.2 18.3 %collective-permute-start.20 = (bf16[6,64,1024]{2,1,0:T(8,128)(2,1)S(1)}, bf16[6,64,1024]{2,1,0:T(8,128)(2,1)S(1)}, u32[]{:S(2)}, u32[]{:S(2)}) collective-permute-start(bf16[6,64,1024]{2,1,0:T(8,128)(2,1)S(1)} %collective-permute-done.6.refs_10_), channel_id=1, source_target_pairs={{0,136},{8,128},{16,152},{24,144},{32,168},{40,160},{48,184},{56,1... | collective-permute-start | bytes 2359304 | tf_op jit(solution)/shard_map/ppermute | solution.py:74
  101.5 12.5 %collective-permute-start.19 = (bf16[6,64,1024]{2,1,0:T(8,128)(2,1)S(1)}, bf16[6,64,1024]{2,1,0:T(8,128)(2,1)S(1)}, u32[]{:S(2)}, u32[]{:S(2)}) collective-permute-start(bf16[6,64,1024]{2,1,0:T(8,128)(2,1)S(1)} %collective-permute-done.18.refs_14_), channel_id=1, source_target_pairs={{0,16},{8,24},{16,32},{24,40},{32,48},{40,56},{48,0},{56,8},{64,11... | collective-permute-start | bytes 2359304 | tf_op jit(solution)/shard_map/ppermute | solution.py:64
  105.6 16.8 %collective-permute-start.29 = (bf16[6,64,896]{2,1,0:T(8,128)(2,1)S(1)}, bf16[6,64,896]{2,1,0:T(8,128)(2,1)}, u32[]{:S(2)}, u32[]{:S(2)}) collective-permute-start(bf16[6,64,896]{2,1,0:T(8,128)(2,1)S(1)} %collective-permute-done.28.refs_6_), channel_id=1, source_target_pairs={{0,1},{1,2},{2,3},{3,4},{4,5},{5,6},{6,7},{7,0},{64,71},{65,64},{6... | collective-permute-start | bytes 2064392 | tf_op jit(solution)/shard_map/ppermute | solution.py:69
  111.5 23.2 %collective-permute-start.22 = (bf16[6,64,1024]{2,1,0:T(8,128)(2,1)}, bf16[6,64,1024]{2,1,0:T(8,128)(2,1)S(1)}, u32[]{:S(2)}, u32[]{:S(2)}) collective-permute-start(bf16[6,64,1024]{2,1,0:T(8,128)(2,1)} %collective-permute-done.7.refs_11_), channel_id=1, source_target_pairs={{0,136},{8,128},{16,152},{24,144},{32,168},{40,160},{48,184},{56,1... | collective-permute-start | bytes 2359304 | tf_op jit(solution)/shard_map/ppermute | solution.py:74
  115.1 19.6 %collective-permute-start.21 = (bf16[6,64,896]{2,1,0:T(8,128)(2,1)}, bf16[6,64,896]{2,1,0:T(8,128)(2,1)}, u32[]{:S(2)}, u32[]{:S(2)}) collective-permute-start(bf16[6,64,896]{2,1,0:T(8,128)(2,1)} %collective-permute-done.15.refs_6_), channel_id=1, source_target_pairs={{0,1},{1,2},{2,3},{3,4},{4,5},{5,6},{6,7},{7,0},{64,71},{65,64},{6... | collective-permute-start | bytes 2064392 | tf_op jit(solution)/shard_map/ppermute | solution.py:69
  157.6 13.3 %collective-permute-start.33 = (bf16[256,1024]{1,0:T(8,128)(2,1)}, bf16[256,1024]{1,0:T(8,128)(2,1)S(1)}, u32[]{:S(2)}, u32[]{:S(2)}) collective-permute-start(bf16[256,1024]{1,0:T(8,128)(2,1)} %share.2.refs_0_), channel_id=1, source_target_pairs={{0,128},{64,192},{128,0},{192,64},{1,129},{65,193},{129,1},{193,65... | collective-permute-start | bytes 1572872 | tf_op jit(solution)/shard_map/ppermute | solution.py:78
  161.6 17.7 %collective-permute-start.37 = (bf16[192,1024]{1,0:T(8,128)(2,1)}, bf16[192,1024]{1,0:T(8,128)(2,1)S(1)}, u32[]{:S(2)}, u32[]{:S(2)}) collective-permute-start(bf16[192,1024]{1,0:T(8,128)(2,1)} %share.3.refs_1_), channel_id=1, source_target_pairs={{0,128},{64,192},{128,0},{192,64},{1,129},{65,193},{129,1},{193,65... | collective-permute-start | bytes 1179656 | tf_op jit(solution)/shard_map/ppermute | solution.py:78
  163.0 17.6 %collective-permute-start.32 = (bf16[256,1024]{1,0:T(8,128)(2,1)S(1)}, bf16[256,1024]{1,0:T(8,128)(2,1)S(1)}, u32[]{:S(2)}, u32[]{:S(2)}) collective-permute-start(bf16[256,1024]{1,0:T(8,128)(2,1)S(1)} %copy-done.16), channel_id=1, source_target_pairs={{0,64},{64,0},{128,192},{192,128},{1,65},{65,1},{129,193},{193,129... | collective-permute-start | bytes 1572872 | tf_op jit(solution)/shard_map/ppermute | solution.py:82
  (45 other events, 1220.0 us)

commit v3 on v2

v3 whole, which is shorter than its diff:
```python
import functools

import jax
import jax.numpy as jnp
from jax import lax
from jax.experimental import pallas as pl
from jax.experimental.pallas import tpu as pltpu
from jax.sharding import PartitionSpec as P

EPS = 1e-06
F32, BF16 = jnp.float32, jnp.bfloat16
HBM = pl.BlockSpec(memory_space=pltpu.HBM)
NEAR = pl.BlockSpec(memory_space=pltpu.VMEM)
LIMIT = pltpu.CompilerParams(vmem_limit_bytes=42 * 2**20)
LITTLE = pltpu.CompilerParams(vmem_limit_bytes=16 * 2**20)
PIECES = (896,)
CHUNKS = (192, 256)


ORDER = (
    "o,o,0",
    "t,give,0",
    "g,g,0",
    "x,g,0",
    "o,o,1",
    "t,t,0",
    "d,g,0",
    "w,wgive,0",
    "g,g,1",
    "x,g,1",
    "o,o,2",
    "t,t,1",
    "u,d,0",
    "g,g,2",
    "d,d,0",
    "o,o,3",
    "t,t,2",
    "d,d,1",
    "u,u,0",
    "x,g,2<t1<w0",
    "o,o,4<d2",
    "t,t,3<x0<g3",
    "d,d,2",
    "u,u,1",
    "x,g,3",
    "o,o,5",
    "t,t,4",
    "u,u,2",
    "o,o,6",
    "t,t,5<x1",
    "t,t,6<x2",
)


def near(x):
    return pltpu.with_memory_space_constraint(x, pltpu.VMEM)


def far(x):
    return pltpu.with_memory_space_constraint(x, pltpu.HBM)


def place():
    task, row = lax.axis_index("task"), lax.axis_index("row")
    return task // 2, task % 2, row // 2, row % 2


def ring_y(x):
    perm = [
        (t * 8 + 2 * y + h, t * 8 + 2 * ((y + 1 - 2 * (t % 2)) % 4) + h)
        for t in range(4)
        for y in range(4)
        for h in range(2)
    ]
    return lax.ppermute(x, ("task", "row"), perm)


def ring_z(x):
    perm = [(t * 8 + z, t * 8 + (z + 1 - 2 * (t % 2)) % 8) for t in range(4) for z in range(8)]
    return lax.ppermute(x, ("task", "col"), perm)


def cross(x):
    perm = [(t * 8 + r, (t ^ 2) * 8 + (r ^ 1)) for t in range(4) for r in range(8)]
    return lax.ppermute(x, ("task", "row"), perm)


def pair(x):
    return lax.ppermute(x, "task", [(t, t ^ 2) for t in range(4)])


def core(x):
    return lax.ppermute(x, "task", [(t, t ^ 1) for t in range(4)])


def grad_block(back, flip):
    _, me, y, hi = place()
    return 2 * ((y + 4 + (2 * me - 1) * back) % 4) + (hi ^ flip if flip else hi)


def act_block(back):
    return (lax.axis_index("col") + 8 + (2 * lax.rem(lax.axis_index("task"), 2) - 1) * back) % 8


def fetch(grad_from, acts, grads, a, g, sems):
    count, tok = a.shape[0], a.shape[1] // 8

    def begin():
        for s in range(count):
            for back, piece in enumerate(acts):
                rows = pl.ds(pl.multiple_of(tok * act_block(back), tok), tok)
                pltpu.make_async_copy(piece.at[s], a.at[s, rows], sems.at[s]).start()
            for meta, piece in zip(grad_from, grads):
                rows = pl.ds(pl.multiple_of(tok * grad_block(*meta), tok), tok)
                pltpu.make_async_copy(piece.at[s], g.at[s, rows], sems.at[s]).start()

    def arrive(s):
        pltpu.make_async_copy(a.at[s], a.at[s], sems.at[s]).wait()
        pltpu.make_async_copy(g.at[s], g.at[s], sems.at[s]).wait()

    return begin, arrive


def square_sum(arrive, count, a, g, f):
    def step(s, _):
        arrive(s)
        d = lax.dot_general(
            a[s], g[s], (((0,), (0,)), ((), ())), preferred_element_type=F32
        )
        f[...] = jnp.where(s == 0, 0.0, f[...]) + d * d
        return 0

    lax.fori_loop(0, count, step, 0)


def first_kernel(n, grad_from, *refs):
    m = len(grad_from)
    acts, grads, (out, a, g, f, sems, osem) = refs[:n], refs[n : n + m], refs[n + m :]
    begin, arrive = fetch(grad_from, acts, grads, a, g, sems)
    begin()
    square_sum(arrive, a.shape[0], a, g, f)
    cp = pltpu.make_async_copy(f, out, osem)
    cp.start()
    cp.wait()


def second_kernel(n, grad_from, *refs):
    m = len(grad_from)
    acts, grads = refs[:n], refs[n : n + m]
    f1_hbm, w1_hbm, *w2_hbm = refs[n + m : n + m + 2 + len(PIECES)]
    keep, *sends, a, g, f, f1, w1, w2, sems, xsem = refs[n + m + 2 + len(PIECES) :]
    begin, arrive = fetch(grad_from, acts, grads, a, g, sems)
    count, size = a.shape[0], f.shape[0]
    lo, me, _, _ = place()
    half = size // 2
    own = pl.ds(pl.multiple_of(lo * size, 16), size)
    extra = [
        pltpu.make_async_copy(f1_hbm, f1, xsem.at[0]),
        pltpu.make_async_copy(w1_hbm.at[0, own], w1, xsem.at[1]),
    ]
    first = 0
    for i, piece in enumerate(w2_hbm):
        at = pl.ds(first, piece.shape[0])
        extra.append(pltpu.make_async_copy(piece, w2.at[at], xsem.at[2 + i]))
        first += piece.shape[0]
    begin()
    for c in extra:
        c.start()
    square_sum(arrive, count, a, g, f)
    for c in extra:
        c.wait()

    def write(out, which, first):
        at = pl.ds(pl.multiple_of(which * half + first, 16), out.shape[1])
        one, two = f1[at], f[at]
        out[0] = one * w1[at].astype(F32) + two * w2[at].astype(F32)
        out[1] = one + two

    first = 0
    for send in sends:
        write(send, 1 - me, first)
        first += send.shape[1]
    write(keep, me, 0)


def share_kernel(first, keep, got, q):
    at = pl.ds(first, q.shape[0])
    den = keep[1, at] + got[1]
    q[...] = ((keep[0, at] + got[0]) / (den + EPS)).astype(BF16)


def whole_kernel(chunks, *refs):
    *parts, out, sems = refs
    lo, me, _, _ = place()
    half = sum(chunks)
    outs, first = [], 0
    for k, n in enumerate(chunks):
        spots = ((lo, me), (lo, 1 - me), (1 - lo, me), (1 - lo, 1 - me))
        for i, (l, c) in enumerate(spots):
            at = pl.ds(pl.multiple_of((2 * l + c) * half + first, 16), n)
            outs.append(pltpu.make_async_copy(parts[4 * k + i], out.at[at], sems.at[k, i]))
        first += n
    for c in outs:
        c.start()
    for c in outs:
        c.wait()


def cost(flops, moved):
    return pl.CostEstimate(flops=flops, bytes_accessed=moved, transcendentals=0)


def body(acts, grads, weights):
    _, count, tok, rows = acts.shape
    cols = grads.shape[3]
    half = rows // 2
    total = tok * 8
    lo = lax.axis_index("task") // 2
    have = {"g": [grads[0]]}

    def part(x, which, axis):
        return lax.dynamic_slice_in_dim(x, which * half, half, axis)

    def run(name, move, source, *after):
        x = have[source[0]][source[1]]
        if after:
            x = lax.optimization_barrier((x, *[have[n][i] for n, i in after]))[0]
        have.setdefault(name, []).append(move(x))

    have["o"] = [part(acts[0], lo, 2)]
    have["give"] = [part(acts[0], 1 - lo, 2)]
    have["wgive"], first = [], 0
    for n in PIECES:
        at = (1 - lo) * half + first
        have["wgive"].append(lax.dynamic_slice_in_dim(weights[0], at, n, 0))
        first += n
    for line in ORDER:
        name, source, at, *after = line.replace("<", ",").split(",")
        move = {"o": ring_z, "t": ring_z, "g": ring_y, "d": ring_y, "u": ring_y}.get(name, pair)
        if name == "x" or line.startswith("u,d"):
            move = cross
        if line.startswith(("t,give", "d,g")):
            move = pair
        run(name, move, (source, int(at)), *[(x[0], int(x[1:])) for x in after])

    grad_from = [(k, flip) for flip in (0, 1) for k in range(4)]
    sems = pltpu.SemaphoreType.DMA((count,))
    arrays = [*have["o"], *have["g"], *have["u"]]
    f1 = pl.pallas_call(
        functools.partial(first_kernel, 8, grad_from),
        out_shape=jax.ShapeDtypeStruct((half, cols), F32),
        in_specs=[HBM] * len(arrays),
        out_specs=HBM,
        scratch_shapes=[
            pltpu.VMEM((count, total, half), BF16),
            pltpu.VMEM((count, total, cols), BF16),
            pltpu.VMEM((half, cols), F32),
            sems,
            pltpu.SemaphoreType.DMA,
        ],
        compiler_params=LIMIT,
        cost_estimate=cost(2 * count * total * half * cols, 12 * 2**20),
        name="own_task",
    )(*[far(x) for x in arrays])
    arrays = [*have["t"], *have["d"], *have["x"], f1, weights, *have["w"]]
    quarter = half // 2
    keep, *sends = pl.pallas_call(
        functools.partial(second_kernel, 8, grad_from),
        out_shape=[pltpu.VMEM((2, n, cols), F32) for n in (quarter, *CHUNKS)],
        in_specs=[HBM] * len(arrays),
        out_specs=[NEAR] * (1 + len(CHUNKS)),
        scratch_shapes=[
            pltpu.VMEM((count, total, half), BF16),
            pltpu.VMEM((count, total, cols), BF16),
            pltpu.VMEM((half, cols), F32),
            pltpu.VMEM((half, cols), F32),
            pltpu.VMEM((half, cols), BF16),
            pltpu.VMEM((half, cols), BF16),
            sems,
            pltpu.SemaphoreType.DMA((2 + len(PIECES),)),
        ],
        compiler_params=LIMIT,
        cost_estimate=cost(2 * count * total * half * cols, 24 * 2**20),
        name="other_task",
    )(*[far(x) for x in arrays])
    parts, first = [], 0
    for n, send in zip(CHUNKS, sends):
        got = core(send)
        q = pl.pallas_call(
            functools.partial(share_kernel, first),
            out_shape=pltpu.VMEM((n, cols), BF16),
            in_specs=[NEAR] * 2,
            out_specs=NEAR,
            compiler_params=LITTLE,
            name="share",
        )(near(keep), near(got))
        by_pair = pair(q)
        parts += [q, core(q), by_pair, core(by_pair)]
        first += n
    return pl.pallas_call(
        functools.partial(whole_kernel, CHUNKS),
        out_shape=jax.ShapeDtypeStruct((rows, cols), BF16),
        in_specs=[NEAR] * len(parts),
        out_specs=HBM,
        scratch_shapes=[pltpu.SemaphoreType.DMA((len(CHUNKS), 4))],
        compiler_params=LITTLE,
        name="whole",
    )(*[near(p) for p in parts])


def solution(mesh):
    placed = (P("task", None, "col", "row"), P("task", None, "row", "col"), P("task", "row", "col"))
    return jax.shard_map(
        body, mesh=mesh, in_specs=placed, out_specs=P("row", "col"), check_vma=False
    )
```

time: 189 us -> 173 us (0.915)
  Pallas kernels: 36.6 us -> 20.8 us
  starting transfers between devices: 74.1 us -> 85.5 us
  waiting for transfers between devices: 65.5 us -> 58 us
  local copies, waits for them, and re-layouts: 11.8 us -> 7.98 us
    ppermute x14, starting transfers between devices: 29.7 us -> 49.3 us  [ring_z(): return lax.ppermute(x, ('task', 'col'), perm)]
    pallas_call x6 -> x4, Pallas kernels: 26.1 us -> 11.9 us  [the longest x1 9.58 us: body(): pl.pallas_call(functools.partial(second_kernel, 8, grad_from), out_shape=...]
    ppermute x9, starting transfers between devices: 22 us -> 13.2 us  [ring_y(): return lax.ppermute(x, ('task', 'row'), perm)]
    ppermute x9, waiting for transfers between devices: 12 us -> 4.46 us  [ring_y(): return lax.ppermute(x, ('task', 'row'), perm)]
    ppermute x6, waiting for transfers between devices: 0.02 us -> 6.98 us  [core(): return lax.ppermute(x, 'task', [(t, t ^ 1) for t in range(4)])]
    ppermute x14, waiting for transfers between devices: 18.6 us -> 13.9 us  [ring_z(): return lax.ppermute(x, ('task', 'col'), perm)]
    dynamic_slice x2 -> x1, local copies, waits for them, and re-layouts: 4.62 us -> 1.49 us  [part(): return lax.dynamic_slice_in_dim(x, which * half, half, axis)]
    ppermute x5, waiting for transfers between devices: 13.5 us -> 10.5 us  [cross(): return lax.ppermute(x, ('task', 'row'), perm)]
  transfers between devices with their start and end apart: 39 -> 39, of which waited for: 19 -> 19; matrix products, arithmetic and copies ran while one was open for 2% -> 1% of each run, Pallas kernels for 14% -> 5%
where the time goes in v3:
time: 173 us
  starting transfers between devices  85.5 us (49%)
  waiting for transfers between devices  58 us (34%)
  Pallas kernels  20.8 us (12%)
  local copies, waits for them, and re-layouts  7.98 us (5%)
    ppermute x14, starting transfers between devices, ring_z(): return lax.ppermute(x, ('task', 'col'), perm)  49.3 us
    ppermute x5, waiting for transfers between devices, pair(): return lax.ppermute(x, 'task', [(t, t ^ 2) for t in range(4)])  22.1 us
    ppermute x14, waiting for transfers between devices, ring_z(): return lax.ppermute(x, ('task', 'col'), perm)  13.9 us
    ppermute x9, starting transfers between devices, ring_y(): return lax.ppermute(x, ('task', 'row'), perm)  13.2 us
    ppermute x5, starting transfers between devices, cross(): return lax.ppermute(x, ('task', 'row'), perm)  12.4 us
    ppermute x5, waiting for transfers between devices, cross(): return lax.ppermute(x, ('task', 'row'), perm)  10.5 us
    pallas_call x1, Pallas kernels, body(): pl.pallas_call(functools.partial(second_kernel, 8, grad_from), out_shape=...  9.58 us
    pallas_call x1, Pallas kernels, body(): pl.pallas_call(functools.partial(first_kernel, 8, grad_from), out_shape=j...  8.96 us
  transfers between devices with their start and end apart: 39, of which 19 were waited for; matrix products, arithmetic and copies ran while one was open for 1% of the time, Pallas kernels for 5%

profile of v3, /device:TPU:1, one launch (start us, length us, event | category | flops | bytes accessed | tf_op | source)
XLA Modules:
  0.0 172.8 jit_solution(8694864269325908858)
XLA Ops:
  3.6 5.6 %collective-permute-start.20 = (bf16[6,64,896]{2,1,0:T(8,128)(2,1)S(1)}, bf16[6,64,896]{2,1,0:T(8,128)(2,1)S(1)}, u32[]{:S(2)}, u32[]{:S(2)}) collective-permute-start(bf16[6,64,896]{2,1,0:T(8,128)(2,1)S(1)} %get-tuple-element.21.refs_0_), channel_id=1, source_target_pairs={{0,1},{1,2},{2,3},{3,4},{4,5},{5,6},{6,7},{7,0},{64,71},{65,64},{6... | collective-permute-start | bytes 2064392 | tf_op jit(solution)/shard_map/ppermute | solution.py:80
  9.2 2.7 %collective-permute-start.5 = (bf16[6,64,1024]{2,1,0:T(8,128)(2,1)S(1)}, bf16[6,64,1024]{2,1,0:T(8,128)(2,1)S(1)}, u32[]{:S(2)}, u32[]{:S(2)}) collective-permute-start(bf16[6,64,1024]{2,1,0:T(8,128)(2,1)S(1)} %bitcast.8), channel_id=1, source_target_pairs={{0,16},{8,24},{16,32},{24,40},{32,48},{40,56},{48,0},{56,8},{64,11... | collective-permute-start | bytes 2359304 | tf_op jit(solution)/shard_map/ppermute | solution.py:75
  12.2 2.5 %collective-permute-start.4 = (bf16[6,64,1024]{2,1,0:T(8,128)(2,1)S(1)}, bf16[6,64,1024]{2,1,0:T(8,128)(2,1)S(1)}, u32[]{:S(2)}, u32[]{:S(2)}) collective-permute-start(bf16[6,64,1024]{2,1,0:T(8,128)(2,1)S(1)} %bitcast.10), channel_id=1, source_target_pairs={{0,136},{8,128},{16,152},{24,144},{32,168},{40,160},{48,184},{56,1... | collective-permute-start | bytes 2359304 | tf_op jit(solution)/shard_map/ppermute | solution.py:85
  14.7 2.8 %collective-permute-done.refs_0_ = bf16[6,64,896]{2,1,0:T(8,128)(2,1)S(1)} collective-permute-done((bf16[6,64,896]{2,1,0:T(8,128)(2,1)S(1)}, bf16[6,64,896]{2,1,0:T(8,128)(2,1)S(1)}, u32[]{:S(2)}, u32[]{:S(2)}) %collective-permute-start) | collective-permute-done | bytes 688160 | tf_op jit(solution)/shard_map/ppermute | solution.py:89
  17.5 6.8 %collective-permute-start.1 = (bf16[6,64,896]{2,1,0:T(8,128)(2,1)S(1)}, bf16[6,64,896]{2,1,0:T(8,128)(2,1)S(1)}, u32[]{:S(2)}, u32[]{:S(2)}) collective-permute-start(bf16[6,64,896]{2,1,0:T(8,128)(2,1)S(1)} %collective-permute-done.refs_0_), channel_id=1, source_target_pairs={{0,1},{1,2},{2,3},{3,4},{4,5},{5,6},{6,7},{7,0},{64,71},{65,64},{6... | collective-permute-start | bytes 2064392 | tf_op jit(solution)/shard_map/ppermute | solution.py:80
  25.1 2.7 %collective-permute-start.6 = (bf16[6,64,1024]{2,1,0:T(8,128)(2,1)S(1)}, bf16[6,64,1024]{2,1,0:T(8,128)(2,1)S(1)}, u32[]{:S(2)}, u32[]{:S(2)}) collective-permute-start(bf16[6,64,1024]{2,1,0:T(8,128)(2,1)S(1)} %collective-permute-done.5.refs_9_), channel_id=1, source_target_pairs={{0,16},{8,24},{16,32},{24,40},{32,48},{40,56},{48,0},{56,8},{64,11... | collective-permute-start | bytes 2359304 | tf_op jit(solution)/shard_map/ppermute | solution.py:75
  27.8 4.4 %collective-permute-done.1.refs_1_ = bf16[6,64,896]{2,1,0:T(8,128)(2,1)S(1)} collective-permute-done((bf16[6,64,896]{2,1,0:T(8,128)(2,1)S(1)}, bf16[6,64,896]{2,1,0:T(8,128)(2,1)S(1)}, u32[]{:S(2)}, u32[]{:S(2)}) %collective-permute-start.1) | collective-permute-done | bytes 688160 | tf_op jit(solution)/shard_map/ppermute | solution.py:80
  32.2 3.4 %collective-permute-start.2 = (bf16[6,64,896]{2,1,0:T(8,128)(2,1)S(1)}, bf16[6,64,896]{2,1,0:T(8,128)(2,1)S(1)}, u32[]{:S(2)}, u32[]{:S(2)}) collective-permute-start(bf16[6,64,896]{2,1,0:T(8,128)(2,1)S(1)} %collective-permute-done.1.refs_1_), channel_id=1, source_target_pairs={{0,1},{1,2},{2,3},{3,4},{4,5},{5,6},{6,7},{7,0},{64,71},{65,64},{6... | collective-permute-start | bytes 2064392 | tf_op jit(solution)/shard_map/ppermute | solution.py:80
  35.6 2.7 %collective-permute-start.16 = (bf16[6,64,1024]{2,1,0:T(8,128)(2,1)S(1)}, bf16[6,64,1024]{2,1,0:T(8,128)(2,1)S(1)}, u32[]{:S(2)}, u32[]{:S(2)}) collective-permute-start(bf16[6,64,1024]{2,1,0:T(8,128)(2,1)S(1)} %collective-permute-done.15.refs_8_), channel_id=1, source_target_pairs={{0,16},{8,24},{16,32},{24,40},{32,48},{40,56},{48,0},{56,8},{64,11... | collective-permute-start | bytes 2359304 | tf_op jit(solution)/shard_map/ppermute | solution.py:75
  38.3 2.5 %collective-permute-start.27 = (bf16[6,64,1024]{2,1,0:T(8,128)(2,1)S(1)}, bf16[6,64,1024]{2,1,0:T(8,128)(2,1)S(1)}, u32[]{:S(2)}, u32[]{:S(2)}) collective-permute-start(bf16[6,64,1024]{2,1,0:T(8,128)(2,1)S(1)} %collective-permute-done.15.refs_8_), channel_id=1, source_target_pairs={{0,136},{8,128},{16,152},{24,144},{32,168},{40,160},{48,184},{56,1... | collective-permute-start | bytes 2359304 | tf_op jit(solution)/shard_map/ppermute | solution.py:85
  40.8 5.6 %collective-permute-start.22 = (bf16[6,64,896]{2,1,0:T(8,128)(2,1)S(1)}, bf16[6,64,896]{2,1,0:T(8,128)(2,1)S(1)}, u32[]{:S(2)}, u32[]{:S(2)}) collective-permute-start(bf16[6,64,896]{2,1,0:T(8,128)(2,1)S(1)} %collective-permute-done.21.refs_2_), channel_id=1, source_target_pairs={{0,1},{1,2},{2,3},{3,4},{4,5},{5,6},{6,7},{7,0},{64,71},{65,64},{6... | collective-permute-start | bytes 2064392 | tf_op jit(solution)/shard_map/ppermute | solution.py:80
  46.9 3.4 %collective-permute-start.3 = (bf16[6,64,896]{2,1,0:T(8,128)(2,1)S(1)}, bf16[6,64,896]{2,1,0:T(8,128)(2,1)S(1)}, u32[]{:S(2)}, u32[]{:S(2)}) collective-permute-start(bf16[6,64,896]{2,1,0:T(8,128)(2,1)S(1)} %collective-permute-done.2.refs_2_), channel_id=1, source_target_pairs={{0,1},{1,2},{2,3},{3,4},{4,5},{5,6},{6,7},{7,0},{64,71},{65,64},{6... | collective-permute-start | bytes 2064392 | tf_op jit(solution)/shard_map/ppermute | solution.py:80
  53.3 4.9 %collective-permute-done.27.refs_12_ = bf16[6,64,1024]{2,1,0:T(8,128)(2,1)S(1)} collective-permute-done((bf16[6,64,1024]{2,1,0:T(8,128)(2,1)S(1)}, bf16[6,64,1024]{2,1,0:T(8,128)(2,1)S(1)}, u32[]{:S(2)}, u32[]{:S(2)}) %collective-permute-start.27) | collective-permute-done | bytes 786464 | tf_op jit(solution)/shard_map/ppermute | solution.py:85
  58.3 5.8 %collective-permute-start.23 = (bf16[6,64,896]{2,1,0:T(8,128)(2,1)S(1)}, bf16[6,64,896]{2,1,0:T(8,128)(2,1)S(1)}, u32[]{:S(2)}, u32[]{:S(2)}) collective-permute-start(bf16[6,64,896]{2,1,0:T(8,128)(2,1)S(1)} %collective-permute-done.22.refs_3_), channel_id=1, source_target_pairs={{0,1},{1,2},{2,3},{3,4},{4,5},{5,6},{6,7},{7,0},{64,71},{65,64},{6... | collective-permute-start | bytes 2064392 | tf_op jit(solution)/shard_map/ppermute | solution.py:80
  65.0 4.4 %collective-permute-done.17.refs_10_ = bf16[6,64,1024]{2,1,0:T(8,128)(2,1)S(1)} collective-permute-done((bf16[6,64,1024]{2,1,0:T(8,128)(2,1)S(1)}, bf16[6,64,1024]{2,1,0:T(8,128)(2,1)S(1)}, u32[]{:S(2)}, u32[]{:S(2)}) %collective-permute-start.17) | collective-permute-done | bytes 786464 | tf_op jit(solution)/shard_map/ppermute | solution.py:75
  69.4 2.6 %collective-permute-done.23.refs_4_ = bf16[6,64,896]{2,1,0:T(8,128)(2,1)S(1)} collective-permute-done((bf16[6,64,896]{2,1,0:T(8,128)(2,1)S(1)}, bf16[6,64,896]{2,1,0:T(8,128)(2,1)S(1)}, u32[]{:S(2)}, u32[]{:S(2)}) %collective-permute-start.23) | collective-permute-done | bytes 688160 | tf_op jit(solution)/shard_map/ppermute | solution.py:80
  72.0 3.4 %collective-permute-start.24 = (bf16[6,64,896]{2,1,0:T(8,128)(2,1)S(1)}, bf16[6,64,896]{2,1,0:T(8,128)(2,1)S(1)}, u32[]{:S(2)}, u32[]{:S(2)}) collective-permute-start(bf16[6,64,896]{2,1,0:T(8,128)(2,1)S(1)} %collective-permute-done.23.refs_4_), channel_id=1, source_target_pairs={{0,1},{1,2},{2,3},{3,4},{4,5},{5,6},{6,7},{7,0},{64,71},{65,64},{6... | collective-permute-start | bytes 2064392 | tf_op jit(solution)/shard_map/ppermute | solution.py:80
  75.4 2.5 %collective-permute-start.10 = (bf16[6,64,1024]{2,1,0:T(8,128)(2,1)S(1)}, bf16[6,64,1024]{2,1,0:T(8,128)(2,1)S(1)}, u32[]{:S(2)}, u32[]{:S(2)}) collective-permute-start(bf16[6,64,1024]{2,1,0:T(8,128)(2,1)S(1)} %collective-permute-done.5.refs_9_), channel_id=1, source_target_pairs={{0,136},{8,128},{16,152},{24,144},{32,168},{40,160},{48,184},{56,1... | collective-permute-start | bytes 2359304 | tf_op jit(solution)/shard_map/ppermute | solution.py:85
  79.4 5.0 %collective-permute-start.9 = (bf16[6,64,896]{2,1,0:T(8,128)(2,1)S(1)}, bf16[6,64,896]{2,1,0:T(8,128)(2,1)S(1)}, u32[]{:S(2)}, u32[]{:S(2)}) collective-permute-start(bf16[6,64,896]{2,1,0:T(8,128)(2,1)S(1)} %collective-permute-done.8.refs_4_), channel_id=1, source_target_pairs={{0,1},{1,2},{2,3},{3,4},{4,5},{5,6},{6,7},{7,0},{64,71},{65,64},{6... | collective-permute-start | bytes 2064392 | tf_op jit(solution)/shard_map/ppermute | solution.py:80
  86.8 3.4 %collective-permute-start.25 = (bf16[6,64,896]{2,1,0:T(8,128)(2,1)S(1)}, bf16[6,64,896]{2,1,0:T(8,128)(2,1)S(1)}, u32[]{:S(2)}, u32[]{:S(2)}) collective-permute-start(bf16[6,64,896]{2,1,0:T(8,128)(2,1)S(1)} %collective-permute-done.24.refs_5_), channel_id=1, source_target_pairs={{0,1},{1,2},{2,3},{3,4},{4,5},{5,6},{6,7},{7,0},{64,71},{65,64},{6... | collective-permute-start | bytes 2064392 | tf_op jit(solution)/shard_map/ppermute | solution.py:80
  90.2 2.6 %collective-permute-done.12.refs_18_ = bf16[896,1024]{1,0:T(8,128)(2,1)S(1)} collective-permute-done((bf16[896,1024]{1,0:T(8,128)(2,1)S(1)}, bf16[896,1024]{1,0:T(8,128)(2,1)S(1)}, u32[]{:S(2)}, u32[]{:S(2)}) %collective-permute-start.12) | collective-permute-done | bytes 1835040 | tf_op jit(solution)/shard_map/ppermute | solution.py:89
  92.8 2.5 %collective-permute-start.13 = (bf16[6,64,1024]{2,1,0:T(8,128)(2,1)S(1)}, bf16[6,64,1024]{2,1,0:T(8,128)(2,1)S(1)}, u32[]{:S(2)}, u32[]{:S(2)}) collective-permute-start(bf16[6,64,1024]{2,1,0:T(8,128)(2,1)S(1)} %collective-permute-done.6.refs_10_), channel_id=1, source_target_pairs={{0,136},{8,128},{16,152},{24,144},{32,168},{40,160},{48,184},{56,1... | collective-permute-start | bytes 2359304 | tf_op jit(solution)/shard_map/ppermute | solution.py:85
  98.2 3.3 %collective-permute-done.25.refs_6_ = bf16[6,64,896]{2,1,0:T(8,128)(2,1)S(1)} collective-permute-done((bf16[6,64,896]{2,1,0:T(8,128)(2,1)S(1)}, bf16[6,64,896]{2,1,0:T(8,128)(2,1)S(1)}, u32[]{:S(2)}, u32[]{:S(2)}) %collective-permute-start.25) | collective-permute-done | bytes 688160 | tf_op jit(solution)/shard_map/ppermute | solution.py:80
  101.5 3.4 %collective-permute-start.26 = (bf16[6,64,896]{2,1,0:T(8,128)(2,1)S(1)}, bf16[6,64,896]{2,1,0:T(8,128)(2,1)}, u32[]{:S(2)}, u32[]{:S(2)}) collective-permute-start(bf16[6,64,896]{2,1,0:T(8,128)(2,1)S(1)} %collective-permute-done.25.refs_6_), channel_id=1, source_target_pairs={{0,1},{1,2},{2,3},{3,4},{4,5},{5,6},{6,7},{7,0},{64,71},{65,64},{6... | collective-permute-start | bytes 2064392 | tf_op jit(solution)/shard_map/ppermute | solution.py:80
  107.4 4.0 %collective-permute-done.13.refs_14_ = bf16[6,64,1024]{2,1,0:T(8,128)(2,1)S(1)} collective-permute-done((bf16[6,64,1024]{2,1,0:T(8,128)(2,1)S(1)}, bf16[6,64,1024]{2,1,0:T(8,128)(2,1)S(1)}, u32[]{:S(2)}, u32[]{:S(2)}) %collective-permute-start.13) | collective-permute-done | bytes 786464 | tf_op jit(solution)/shard_map/ppermute | solution.py:85
  111.4 2.7 %collective-permute-start.18 = (bf16[6,64,1024]{2,1,0:T(8,128)(2,1)S(1)}, bf16[6,64,1024]{2,1,0:T(8,128)(2,1)S(1)}, u32[]{:S(2)}, u32[]{:S(2)}) collective-permute-start(bf16[6,64,1024]{2,1,0:T(8,128)(2,1)S(1)} %collective-permute-done.17.refs_10_), channel_id=1, source_target_pairs={{0,16},{8,24},{16,32},{24,40},{32,48},{40,56},{48,0},{56,8},{64,11... | collective-permute-start | bytes 2359304 | tf_op jit(solution)/shard_map/ppermute | solution.py:75
  116.3 9.0 %own_task.1.refs_16_ = f32[896,1024]{1,0:T(8,128)S(1)} custom-call(bf16[6,64,896]{2,1,0:T(8,128)(2,1)} %copy-done.18, bf16[6,64,896]{2,1,0:T(8,128)(2,1)} %copy-done.27, bf16[6,64,896]{2,1,0:T(8,128)(2,1)} %copy-done.28, bf16[6,64,896]{2,1,0:T(8,128)(2,1)} %copy-done.29, bf16[6,64,896]{2,1,0:T(8,128)(2,1)} %copy-done.30, bf16[6,64,896]{2,1,0:T(8,128)(2,1)} %copy-done.31, ...), custom_call_target="tpu_custom_call" | custom-call | flops 5637144576 | bytes 12582912 | tf_op jit(solution)/shard_map/own_task/pallas_call | solution.py:249
  130.2 9.6 %other_task.1 = (f32[2,448,1024]{2,1,0:T(8,128)S(1)}, f32[2,192,1024]{2,1,0:T(8,128)S(1)}, f32[2,256,1024]{2,1,0:T(8,128)S(1)}) custom-call(bf16[6,64,896]{2,1,0:T(8,128)(2,1)} %copy-done.10, bf16[6,64,896]{2,1,0:T(8,128)(2,1)} %copy-done.11, bf16[6,64,896]{2,1,0:T(8,128)(2,1)} %copy-done.12, bf16[6,64,896]{2,1,0:T(8,128)(2,1)} %copy-done.13, ...), custom_call_target="tpu_custom_call" | custom-call | flops 5637144576 | bytes 25165824 | tf_op jit(solution)/shard_map/other_task/pallas_call | solution.py:267
  139.8 2.8 %collective-permute-start.35 = (f32[2,256,1024]{2,1,0:T(8,128)S(1)}, f32[2,256,1024]{2,1,0:T(8,128)S(1)}, u32[]{:S(2)}, u32[]{:S(2)}) collective-permute-start(f32[2,256,1024]{2,1,0:T(8,128)S(1)} %get-tuple-element.20), channel_id=1, source_target_pairs={{0,64},{64,0},{128,192},{192,128},{1,65},{65,1},{129,193},{193,129... | collective-permute-start | bytes 6291464 | tf_op jit(solution)/shard_map/ppermute | solution.py:93
  142.7 3.7 %collective-permute-done.35.got = f32[2,256,1024]{2,1,0:T(8,128)S(1)} collective-permute-done((f32[2,256,1024]{2,1,0:T(8,128)S(1)}, f32[2,256,1024]{2,1,0:T(8,128)S(1)}, u32[]{:S(2)}, u32[]{:S(2)}) %collective-permute-start.35) | collective-permute-done | bytes 2097184 | tf_op jit(solution)/shard_map/ppermute | solution.py:93
  149.5 10.3 %collective-permute-done.37.refs_6_ = bf16[256,1024]{1,0:T(8,128)(2,1)S(1)} collective-permute-done((bf16[256,1024]{1,0:T(8,128)(2,1)S(1)}, bf16[256,1024]{1,0:T(8,128)(2,1)S(1)}, u32[]{:S(2)}, u32[]{:S(2)}) %collective-permute-start.37) | collective-permute-done | bytes 524320 | tf_op jit(solution)/shard_map/ppermute | solution.py:89
  161.8 6.4 %collective-permute-done.33.refs_2_ = bf16[192,1024]{1,0:T(8,128)(2,1)S(1)} collective-permute-done((bf16[192,1024]{1,0:T(8,128)(2,1)S(1)}, bf16[192,1024]{1,0:T(8,128)(2,1)S(1)}, u32[]{:S(2)}, u32[]{:S(2)}) %collective-permute-start.33) | collective-permute-done | bytes 393248 | tf_op jit(solution)/shard_map/ppermute | solution.py:89
  (119 shorter events, 34.8 us)
Async XLA Ops:
  1.5 15.9 %collective-permute-start = (bf16[6,64,896]{2,1,0:T(8,128)(2,1)S(1)}, bf16[6,64,896]{2,1,0:T(8,128)(2,1)S(1)}, u32[]{:S(2)}, u32[]{:S(2)}) collective-permute-start(bf16[6,64,896]{2,1,0:T(8,128)(2,1)S(1)} %get-tuple-element.22), channel_id=1, source_target_pairs={{0,128},{64,192},{128,0},{192,64},{1,129},{65,193},{129,1},{193,65... | collective-permute-start | bytes 2064392 | tf_op jit(solution)/shard_map/ppermute | solution.py:89
  3.6 20.7 %collective-permute-start.20 = (bf16[6,64,896]{2,1,0:T(8,128)(2,1)S(1)}, bf16[6,64,896]{2,1,0:T(8,128)(2,1)S(1)}, u32[]{:S(2)}, u32[]{:S(2)}) collective-permute-start(bf16[6,64,896]{2,1,0:T(8,128)(2,1)S(1)} %get-tuple-element.21.refs_0_), channel_id=1, source_target_pairs={{0,1},{1,2},{2,3},{3,4},{4,5},{5,6},{6,7},{7,0},{64,71},{65,64},{6... | collective-permute-start | bytes 2064392 | tf_op jit(solution)/shard_map/ppermute | solution.py:80
  9.2 15.8 %collective-permute-start.5 = (bf16[6,64,1024]{2,1,0:T(8,128)(2,1)S(1)}, bf16[6,64,1024]{2,1,0:T(8,128)(2,1)S(1)}, u32[]{:S(2)}, u32[]{:S(2)}) collective-permute-start(bf16[6,64,1024]{2,1,0:T(8,128)(2,1)S(1)} %bitcast.8), channel_id=1, source_target_pairs={{0,16},{8,24},{16,32},{24,40},{32,48},{40,56},{48,0},{56,8},{64,11... | collective-permute-start | bytes 2359304 | tf_op jit(solution)/shard_map/ppermute | solution.py:75
  12.0 23.7 %collective-permute-start.15 = (bf16[6,64,1024]{2,1,0:T(8,128)(2,1)S(1)}, bf16[6,64,1024]{2,1,0:T(8,128)(2,1)S(1)}, u32[]{:S(2)}, u32[]{:S(2)}) collective-permute-start(bf16[6,64,1024]{2,1,0:T(8,128)(2,1)S(1)} %bitcast.9), channel_id=1, source_target_pairs={{0,128},{64,192},{128,0},{192,64},{1,129},{65,193},{129,1},{193,65... | collective-permute-start | bytes 2359304 | tf_op jit(solution)/shard_map/ppermute | solution.py:89
  12.2 26.1 %collective-permute-start.4 = (bf16[6,64,1024]{2,1,0:T(8,128)(2,1)S(1)}, bf16[6,64,1024]{2,1,0:T(8,128)(2,1)S(1)}, u32[]{:S(2)}, u32[]{:S(2)}) collective-permute-start(bf16[6,64,1024]{2,1,0:T(8,128)(2,1)S(1)} %bitcast.10), channel_id=1, source_target_pairs={{0,136},{8,128},{16,152},{24,144},{32,168},{40,160},{48,184},{56,1... | collective-permute-start | bytes 2359304 | tf_op jit(solution)/shard_map/ppermute | solution.py:85
  17.5 14.7 %collective-permute-start.1 = (bf16[6,64,896]{2,1,0:T(8,128)(2,1)S(1)}, bf16[6,64,896]{2,1,0:T(8,128)(2,1)S(1)}, u32[]{:S(2)}, u32[]{:S(2)}) collective-permute-start(bf16[6,64,896]{2,1,0:T(8,128)(2,1)S(1)} %collective-permute-done.refs_0_), channel_id=1, source_target_pairs={{0,1},{1,2},{2,3},{3,4},{4,5},{5,6},{6,7},{7,0},{64,71},{65,64},{6... | collective-permute-start | bytes 2064392 | tf_op jit(solution)/shard_map/ppermute | solution.py:80
  24.3 16.5 %collective-permute-start.21 = (bf16[6,64,896]{2,1,0:T(8,128)(2,1)S(1)}, bf16[6,64,896]{2,1,0:T(8,128)(2,1)S(1)}, u32[]{:S(2)}, u32[]{:S(2)}) collective-permute-start(bf16[6,64,896]{2,1,0:T(8,128)(2,1)S(1)} %collective-permute-done.20.refs_1_), channel_id=1, source_target_pairs={{0,1},{1,2},{2,3},{3,4},{4,5},{5,6},{6,7},{7,0},{64,71},{65,64},{6... | collective-permute-start | bytes 2064392 | tf_op jit(solution)/shard_map/ppermute | solution.py:80
  25.1 21.3 %collective-permute-start.6 = (bf16[6,64,1024]{2,1,0:T(8,128)(2,1)S(1)}, bf16[6,64,1024]{2,1,0:T(8,128)(2,1)S(1)}, u32[]{:S(2)}, u32[]{:S(2)}) collective-permute-start(bf16[6,64,1024]{2,1,0:T(8,128)(2,1)S(1)} %collective-permute-done.5.refs_9_), channel_id=1, source_target_pairs={{0,16},{8,24},{16,32},{24,40},{32,48},{40,56},{48,0},{56,8},{64,11... | collective-permute-start | bytes 2359304 | tf_op jit(solution)/shard_map/ppermute | solution.py:75
  32.2 14.7 %collective-permute-start.2 = (bf16[6,64,896]{2,1,0:T(8,128)(2,1)S(1)}, bf16[6,64,896]{2,1,0:T(8,128)(2,1)S(1)}, u32[]{:S(2)}, u32[]{:S(2)}) collective-permute-start(bf16[6,64,896]{2,1,0:T(8,128)(2,1)S(1)} %collective-permute-done.1.refs_1_), channel_id=1, source_target_pairs={{0,1},{1,2},{2,3},{3,4},{4,5},{5,6},{6,7},{7,0},{64,71},{65,64},{6... | collective-permute-start | bytes 2064392 | tf_op jit(solution)/shard_map/ppermute | solution.py:80
  35.6 16.4 %collective-permute-start.16 = (bf16[6,64,1024]{2,1,0:T(8,128)(2,1)S(1)}, bf16[6,64,1024]{2,1,0:T(8,128)(2,1)S(1)}, u32[]{:S(2)}, u32[]{:S(2)}) collective-permute-start(bf16[6,64,1024]{2,1,0:T(8,128)(2,1)S(1)} %collective-permute-done.15.refs_8_), channel_id=1, source_target_pairs={{0,16},{8,24},{16,32},{24,40},{32,48},{40,56},{48,0},{56,8},{64,11... | collective-permute-start | bytes 2359304 | tf_op jit(solution)/shard_map/ppermute | solution.py:75
  38.3 19.9 %collective-permute-start.27 = (bf16[6,64,1024]{2,1,0:T(8,128)(2,1)S(1)}, bf16[6,64,1024]{2,1,0:T(8,128)(2,1)S(1)}, u32[]{:S(2)}, u32[]{:S(2)}) collective-permute-start(bf16[6,64,1024]{2,1,0:T(8,128)(2,1)S(1)} %collective-permute-done.15.refs_8_), channel_id=1, source_target_pairs={{0,136},{8,128},{16,152},{24,144},{32,168},{40,160},{48,184},{56,1... | collective-permute-start | bytes 2359304 | tf_op jit(solution)/shard_map/ppermute | solution.py:85
  40.8 17.5 %collective-permute-start.22 = (bf16[6,64,896]{2,1,0:T(8,128)(2,1)S(1)}, bf16[6,64,896]{2,1,0:T(8,128)(2,1)S(1)}, u32[]{:S(2)}, u32[]{:S(2)}) collective-permute-start(bf16[6,64,896]{2,1,0:T(8,128)(2,1)S(1)} %collective-permute-done.21.refs_2_), channel_id=1, source_target_pairs={{0,1},{1,2},{2,3},{3,4},{4,5},{5,6},{6,7},{7,0},{64,71},{65,64},{6... | collective-permute-start | bytes 2064392 | tf_op jit(solution)/shard_map/ppermute | solution.py:80
  46.4 17.7 %collective-permute-start.7 = (bf16[6,64,1024]{2,1,0:T(8,128)(2,1)S(1)}, bf16[6,64,1024]{2,1,0:T(8,128)(2,1)S(1)}, u32[]{:S(2)}, u32[]{:S(2)}) collective-permute-start(bf16[6,64,1024]{2,1,0:T(8,128)(2,1)S(1)} %collective-permute-done.6.refs_10_), channel_id=1, source_target_pairs={{0,16},{8,24},{16,32},{24,40},{32,48},{40,56},{48,0},{56,8},{64,11... | collective-permute-start | bytes 2359304 | tf_op jit(solution)/shard_map/ppermute | solution.py:75
  46.9 17.2 %collective-permute-start.3 = (bf16[6,64,896]{2,1,0:T(8,128)(2,1)S(1)}, bf16[6,64,896]{2,1,0:T(8,128)(2,1)S(1)}, u32[]{:S(2)}, u32[]{:S(2)}) collective-permute-start(bf16[6,64,896]{2,1,0:T(8,128)(2,1)S(1)} %collective-permute-done.2.refs_2_), channel_id=1, source_target_pairs={{0,1},{1,2},{2,3},{3,4},{4,5},{5,6},{6,7},{7,0},{64,71},{65,64},{6... | collective-permute-start | bytes 2064392 | tf_op jit(solution)/shard_map/ppermute | solution.py:80
  52.0 40.8 %collective-permute-start.12 = (bf16[896,1024]{1,0:T(8,128)(2,1)S(1)}, bf16[896,1024]{1,0:T(8,128)(2,1)S(1)}, u32[]{:S(2)}, u32[]{:S(2)}) collective-permute-start(bf16[896,1024]{1,0:T(8,128)(2,1)S(1)} %dynamic-slice_bitcast_fusion), channel_id=1, source_target_pairs={{0,128},{64,192},{128,0},{192,64},{1,129},{65,193},{129,1},{193,65... | collective-permute-start | bytes 5505032 | tf_op jit(solution)/shard_map/ppermute | solution.py:89
  58.3 13.7 %collective-permute-start.23 = (bf16[6,64,896]{2,1,0:T(8,128)(2,1)S(1)}, bf16[6,64,896]{2,1,0:T(8,128)(2,1)S(1)}, u32[]{:S(2)}, u32[]{:S(2)}) collective-permute-start(bf16[6,64,896]{2,1,0:T(8,128)(2,1)S(1)} %collective-permute-done.22.refs_3_), channel_id=1, source_target_pairs={{0,1},{1,2},{2,3},{3,4},{4,5},{5,6},{6,7},{7,0},{64,71},{65,64},{6... | collective-permute-start | bytes 2064392 | tf_op jit(solution)/shard_map/ppermute | solution.py:80
  64.1 13.8 %collective-permute-start.28 = (bf16[6,64,1024]{2,1,0:T(8,128)(2,1)S(1)}, bf16[6,64,1024]{2,1,0:T(8,128)(2,1)S(1)}, u32[]{:S(2)}, u32[]{:S(2)}) collective-permute-start(bf16[6,64,1024]{2,1,0:T(8,128)(2,1)S(1)} %collective-permute-done.27.refs_12_), channel_id=1, source_target_pairs={{0,16},{8,24},{16,32},{24,40},{32,48},{40,56},{48,0},{56,8},{64,11... | collective-permute-start | bytes 2359304 | tf_op jit(solution)/shard_map/ppermute | solution.py:75
  64.2 15.2 %collective-permute-start.8 = (bf16[6,64,896]{2,1,0:T(8,128)(2,1)S(1)}, bf16[6,64,896]{2,1,0:T(8,128)(2,1)S(1)}, u32[]{:S(2)}, u32[]{:S(2)}) collective-permute-start(bf16[6,64,896]{2,1,0:T(8,128)(2,1)S(1)} %collective-permute-done.3.refs_3_), channel_id=1, source_target_pairs={{0,1},{1,2},{2,3},{3,4},{4,5},{5,6},{6,7},{7,0},{64,71},{65,64},{6... | collective-permute-start | bytes 2064392 | tf_op jit(solution)/shard_map/ppermute | solution.py:80
  72.0 14.7 %collective-permute-start.24 = (bf16[6,64,896]{2,1,0:T(8,128)(2,1)S(1)}, bf16[6,64,896]{2,1,0:T(8,128)(2,1)S(1)}, u32[]{:S(2)}, u32[]{:S(2)}) collective-permute-start(bf16[6,64,896]{2,1,0:T(8,128)(2,1)S(1)} %collective-permute-done.23.refs_4_), channel_id=1, source_target_pairs={{0,1},{1,2},{2,3},{3,4},{4,5},{5,6},{6,7},{7,0},{64,71},{65,64},{6... | collective-permute-start | bytes 2064392 | tf_op jit(solution)/shard_map/ppermute | solution.py:80
  75.4 20.5 %collective-permute-start.10 = (bf16[6,64,1024]{2,1,0:T(8,128)(2,1)S(1)}, bf16[6,64,1024]{2,1,0:T(8,128)(2,1)S(1)}, u32[]{:S(2)}, u32[]{:S(2)}) collective-permute-start(bf16[6,64,1024]{2,1,0:T(8,128)(2,1)S(1)} %collective-permute-done.5.refs_9_), channel_id=1, source_target_pairs={{0,136},{8,128},{16,152},{24,144},{32,168},{40,160},{48,184},{56,1... | collective-permute-start | bytes 2359304 | tf_op jit(solution)/shard_map/ppermute | solution.py:85
  77.9 19.6 %collective-permute-start.29 = (bf16[6,64,1024]{2,1,0:T(8,128)(2,1)S(1)}, bf16[6,64,1024]{2,1,0:T(8,128)(2,1)S(1)}, u32[]{:S(2)}, u32[]{:S(2)}) collective-permute-start(bf16[6,64,1024]{2,1,0:T(8,128)(2,1)S(1)} %collective-permute-done.28.refs_13_), channel_id=1, source_target_pairs={{0,16},{8,24},{16,32},{24,40},{32,48},{40,56},{48,0},{56,8},{64,11... | collective-permute-start | bytes 2359304 | tf_op jit(solution)/shard_map/ppermute | solution.py:75
  79.4 16.6 %collective-permute-start.9 = (bf16[6,64,896]{2,1,0:T(8,128)(2,1)S(1)}, bf16[6,64,896]{2,1,0:T(8,128)(2,1)S(1)}, u32[]{:S(2)}, u32[]{:S(2)}) collective-permute-start(bf16[6,64,896]{2,1,0:T(8,128)(2,1)S(1)} %collective-permute-done.8.refs_4_), channel_id=1, source_target_pairs={{0,1},{1,2},{2,3},{3,4},{4,5},{5,6},{6,7},{7,0},{64,71},{65,64},{6... | collective-permute-start | bytes 2064392 | tf_op jit(solution)/shard_map/ppermute | solution.py:80
  86.8 14.7 %collective-permute-start.25 = (bf16[6,64,896]{2,1,0:T(8,128)(2,1)S(1)}, bf16[6,64,896]{2,1,0:T(8,128)(2,1)S(1)}, u32[]{:S(2)}, u32[]{:S(2)}) collective-permute-start(bf16[6,64,896]{2,1,0:T(8,128)(2,1)S(1)} %collective-permute-done.24.refs_5_), channel_id=1, source_target_pairs={{0,1},{1,2},{2,3},{3,4},{4,5},{5,6},{6,7},{7,0},{64,71},{65,64},{6... | collective-permute-start | bytes 2064392 | tf_op jit(solution)/shard_map/ppermute | solution.py:80
  92.8 18.6 %collective-permute-start.13 = (bf16[6,64,1024]{2,1,0:T(8,128)(2,1)S(1)}, bf16[6,64,1024]{2,1,0:T(8,128)(2,1)S(1)}, u32[]{:S(2)}, u32[]{:S(2)}) collective-permute-start(bf16[6,64,1024]{2,1,0:T(8,128)(2,1)S(1)} %collective-permute-done.6.refs_10_), channel_id=1, source_target_pairs={{0,136},{8,128},{16,152},{24,144},{32,168},{40,160},{48,184},{56,1... | collective-permute-start | bytes 2359304 | tf_op jit(solution)/shard_map/ppermute | solution.py:85
  96.0 18.2 %collective-permute-start.11 = (bf16[6,64,896]{2,1,0:T(8,128)(2,1)S(1)}, bf16[6,64,896]{2,1,0:T(8,128)(2,1)S(1)}, u32[]{:S(2)}, u32[]{:S(2)}) collective-permute-start(bf16[6,64,896]{2,1,0:T(8,128)(2,1)S(1)} %collective-permute-done.9.refs_5_), channel_id=1, source_target_pairs={{0,1},{1,2},{2,3},{3,4},{4,5},{5,6},{6,7},{7,0},{64,71},{65,64},{6... | collective-permute-start | bytes 2064392 | tf_op jit(solution)/shard_map/ppermute | solution.py:80
  97.5 16.9 %collective-permute-start.30 = (bf16[6,64,1024]{2,1,0:T(8,128)(2,1)S(1)}, bf16[6,64,1024]{2,1,0:T(8,128)(2,1)S(1)}, u32[]{:S(2)}, u32[]{:S(2)}) collective-permute-start(bf16[6,64,1024]{2,1,0:T(8,128)(2,1)S(1)} %collective-permute-done.29.refs_14_), channel_id=1, source_target_pairs={{0,16},{8,24},{16,32},{24,40},{32,48},{40,56},{48,0},{56,8},{64,11... | collective-permute-start | bytes 2359304 | tf_op jit(solution)/shard_map/ppermute | solution.py:75
  101.5 14.7 %collective-permute-start.26 = (bf16[6,64,896]{2,1,0:T(8,128)(2,1)S(1)}, bf16[6,64,896]{2,1,0:T(8,128)(2,1)}, u32[]{:S(2)}, u32[]{:S(2)}) collective-permute-start(bf16[6,64,896]{2,1,0:T(8,128)(2,1)S(1)} %collective-permute-done.25.refs_6_), channel_id=1, source_target_pairs={{0,1},{1,2},{2,3},{3,4},{4,5},{5,6},{6,7},{7,0},{64,71},{65,64},{6... | collective-permute-start | bytes 2064392 | tf_op jit(solution)/shard_map/ppermute | solution.py:80
  104.9 23.2 %collective-permute-start.19 = (bf16[6,64,1024]{2,1,0:T(8,128)(2,1)S(1)}, bf16[6,64,1024]{2,1,0:T(8,128)(2,1)S(1)}, u32[]{:S(2)}, u32[]{:S(2)}) collective-permute-start(bf16[6,64,1024]{2,1,0:T(8,128)(2,1)S(1)} %collective-permute-done.7.refs_11_), channel_id=1, source_target_pairs={{0,136},{8,128},{16,152},{24,144},{32,168},{40,160},{48,184},{56,1... | collective-permute-start | bytes 2359304 | tf_op jit(solution)/shard_map/ppermute | solution.py:85
  111.4 16.8 %collective-permute-start.18 = (bf16[6,64,1024]{2,1,0:T(8,128)(2,1)S(1)}, bf16[6,64,1024]{2,1,0:T(8,128)(2,1)S(1)}, u32[]{:S(2)}, u32[]{:S(2)}) collective-permute-start(bf16[6,64,1024]{2,1,0:T(8,128)(2,1)S(1)} %collective-permute-done.17.refs_10_), channel_id=1, source_target_pairs={{0,16},{8,24},{16,32},{24,40},{32,48},{40,56},{48,0},{56,8},{64,11... | collective-permute-start | bytes 2359304 | tf_op jit(solution)/shard_map/ppermute | solution.py:75
  114.2 14.0 %collective-permute-start.14 = (bf16[6,64,896]{2,1,0:T(8,128)(2,1)S(1)}, bf16[6,64,896]{2,1,0:T(8,128)(2,1)S(1)}, u32[]{:S(2)}, u32[]{:S(2)}) collective-permute-start(bf16[6,64,896]{2,1,0:T(8,128)(2,1)S(1)} %collective-permute-done.11.refs_6_), channel_id=1, source_target_pairs={{0,1},{1,2},{2,3},{3,4},{4,5},{5,6},{6,7},{7,0},{64,71},{65,64},{6... | collective-permute-start | bytes 2064392 | tf_op jit(solution)/shard_map/ppermute | solution.py:80
  148.7 19.5 %collective-permute-start.33 = (bf16[192,1024]{1,0:T(8,128)(2,1)S(1)}, bf16[192,1024]{1,0:T(8,128)(2,1)S(1)}, u32[]{:S(2)}, u32[]{:S(2)}) collective-permute-start(bf16[192,1024]{1,0:T(8,128)(2,1)S(1)} %share.2.refs_0_), channel_id=1, source_target_pairs={{0,128},{64,192},{128,0},{192,64},{1,129},{65,193},{129,1},{193,65... | collective-permute-start | bytes 1179656 | tf_op jit(solution)/shard_map/ppermute | solution.py:89
  148.8 21.9 %collective-permute-start.36 = (bf16[256,1024]{1,0:T(8,128)(2,1)S(1)}, bf16[256,1024]{1,0:T(8,128)(2,1)S(1)}, u32[]{:S(2)}, u32[]{:S(2)}) collective-permute-start(bf16[256,1024]{1,0:T(8,128)(2,1)S(1)} %share.3.refs_4_), channel_id=1, source_target_pairs={{0,64},{64,0},{128,192},{192,128},{1,65},{65,1},{129,193},{193,129... | collective-permute-start | bytes 1572872 | tf_op jit(solution)/shard_map/ppermute | solution.py:93
  (40 other events, 1459.0 us)

commit v4 on v3

--- a/solution.py
+++ b/solution.py
@@ -11,7 +11,7 @@
 F32, BF16 = jnp.float32, jnp.bfloat16
 HBM = pl.BlockSpec(memory_space=pltpu.HBM)
 NEAR = pl.BlockSpec(memory_space=pltpu.VMEM)
-LIMIT = pltpu.CompilerParams(vmem_limit_bytes=42 * 2**20)
+LIMIT = pltpu.CompilerParams(vmem_limit_bytes=36 * 2**20)
 LITTLE = pltpu.CompilerParams(vmem_limit_bytes=16 * 2**20)
 PIECES = (896,)
 CHUNKS = (192, 256)
@@ -102,21 +102,30 @@
     return (lax.axis_index("col") + 8 + (2 * lax.rem(lax.axis_index("task"), 2) - 1) * back) % 8
 
 
-def fetch(grad_from, acts, grads, a, g, sems):
+def fetch(grad_from, late, acts, grads, a, g, sems):
     count, tok = a.shape[0], a.shape[1] // 8
+
+    def act_rows(back):
+        return pl.ds(pl.multiple_of(tok * act_block(back), tok), tok)
+
+    def grad_rows(i):
+        return pl.ds(pl.multiple_of(tok * grad_block(*grad_from[i]), tok), tok)
 
     def begin():
         for s in range(count):
-            for back, piece in enumerate(acts):
-                rows = pl.ds(pl.multiple_of(tok * act_block(back), tok), tok)
-                pltpu.make_async_copy(piece.at[s], a.at[s, rows], sems.at[s]).start()
-            for meta, piece in zip(grad_from, grads):
-                rows = pl.ds(pl.multiple_of(tok * grad_block(*meta), tok), tok)
-                pltpu.make_async_copy(piece.at[s], g.at[s, rows], sems.at[s]).start()
+            for back, piece in enumerate(acts[:-1]):
+                pltpu.make_async_copy(piece.at[s], a.at[s, act_rows(back)], sems.at[s]).start()
+            for i, piece in enumerate(grads):
+                if i not in late:
+                    pltpu.make_async_copy(piece.at[s], g.at[s, grad_rows(i)], sems.at[s]).start()
 
     def arrive(s):
-        pltpu.make_async_copy(a.at[s], a.at[s], sems.at[s]).wait()
-        pltpu.make_async_copy(g.at[s], g.at[s], sems.at[s]).wait()
+        some, more = a.at[s, pl.ds(0, 7 * tok)], g.at[s, pl.ds(0, (8 - len(late)) * tok)]
+        pltpu.make_async_copy(some, some, sems.at[s]).wait()
+        pltpu.make_async_copy(more, more, sems.at[s]).wait()
+        a[s, act_rows(7)] = acts[7][s]
+        for i in late:
+            g[s, grad_rows(i)] = grads[i][s]
 
     return begin, arrive
 
@@ -133,35 +142,31 @@
     lax.fori_loop(0, count, step, 0)
 
 
-def first_kernel(n, grad_from, *refs):
+def first_kernel(n, grad_from, late, *refs):
     m = len(grad_from)
-    acts, grads, (out, a, g, f, sems, osem) = refs[:n], refs[n : n + m], refs[n + m :]
-    begin, arrive = fetch(grad_from, acts, grads, a, g, sems)
+    acts, grads, (out, a, g, sems) = refs[:n], refs[n : n + m], refs[n + m :]
+    begin, arrive = fetch(grad_from, late, acts, grads, a, g, sems)
     begin()
-    square_sum(arrive, a.shape[0], a, g, f)
-    cp = pltpu.make_async_copy(f, out, osem)
-    cp.start()
-    cp.wait()
-
-
-def second_kernel(n, grad_from, *refs):
+    square_sum(arrive, a.shape[0], a, g, out)
+
+
+def second_kernel(n, grad_from, late, *refs):
     m = len(grad_from)
     acts, grads = refs[:n], refs[n : n + m]
-    f1_hbm, w1_hbm, *w2_hbm = refs[n + m : n + m + 2 + len(PIECES)]
-    keep, *sends, a, g, f, f1, w1, w2, sems, xsem = refs[n + m + 2 + len(PIECES) :]
-    begin, arrive = fetch(grad_from, acts, grads, a, g, sems)
+    f1, w1_hbm, *w2_hbm = refs[n + m : n + m + 2 + len(PIECES)]
+    keep, *sends, a, g, f, w1, w2, sems, xsem = refs[n + m + 2 + len(PIECES) :]
+    begin, arrive = fetch(grad_from, late, acts, grads, a, g, sems)
     count, size = a.shape[0], f.shape[0]
     lo, me, _, _ = place()
     half = size // 2
     own = pl.ds(pl.multiple_of(lo * size, 16), size)
     extra = [
-        pltpu.make_async_copy(f1_hbm, f1, xsem.at[0]),
-        pltpu.make_async_copy(w1_hbm.at[0, own], w1, xsem.at[1]),
+        pltpu.make_async_copy(w1_hbm.at[0, own], w1, xsem.at[0]),
     ]
     first = 0
     for i, piece in enumerate(w2_hbm):
         at = pl.ds(first, piece.shape[0])
-        extra.append(pltpu.make_async_copy(piece, w2.at[at], xsem.at[2 + i]))
+        extra.append(pltpu.make_async_copy(piece, w2.at[at], xsem.at[1 + i]))
         first += piece.shape[0]
     begin()
     for c in extra:
@@ -189,17 +194,15 @@
     q[...] = ((keep[0, at] + got[0]) / (den + EPS)).astype(BF16)
 
 
-def whole_kernel(chunks, *refs):
+def whole_kernel(spots, half, *refs):
+    refs = refs[-len(spots) - 2 :]
     *parts, out, sems = refs
     lo, me, _, _ = place()
-    half = sum(chunks)
-    outs, first = [], 0
-    for k, n in enumerate(chunks):
-        spots = ((lo, me), (lo, 1 - me), (1 - lo, me), (1 - lo, 1 - me))
-        for i, (l, c) in enumerate(spots):
-            at = pl.ds(pl.multiple_of((2 * l + c) * half + first, 16), n)
-            outs.append(pltpu.make_async_copy(parts[4 * k + i], out.at[at], sems.at[k, i]))
-        first += n
+    outs = []
+    for i, (part, (l, c, first)) in enumerate(zip(parts, spots)):
+        l, c = (1 - lo if l else lo), (1 - me if c else me)
+        at = pl.ds(pl.multiple_of((2 * l + c) * half + first, 16), part.shape[0])
+        outs.append(pltpu.make_async_copy(part, out.at[at], sems.at[i]))
     for c in outs:
         c.start()
     for c in outs:
@@ -246,43 +249,44 @@
     grad_from = [(k, flip) for flip in (0, 1) for k in range(4)]
     sems = pltpu.SemaphoreType.DMA((count,))
     arrays = [*have["o"], *have["g"], *have["u"]]
+    late = (7,)
+    near_at = [7, *(8 + i for i in late)]
     f1 = pl.pallas_call(
-        functools.partial(first_kernel, 8, grad_from),
-        out_shape=jax.ShapeDtypeStruct((half, cols), F32),
-        in_specs=[HBM] * len(arrays),
-        out_specs=HBM,
+        functools.partial(first_kernel, 8, grad_from, late),
+        out_shape=pltpu.VMEM((half, cols), F32),
+        in_specs=[NEAR if i in near_at else HBM for i in range(len(arrays))],
+        out_specs=NEAR,
         scratch_shapes=[
             pltpu.VMEM((count, total, half), BF16),
             pltpu.VMEM((count, total, cols), BF16),
-            pltpu.VMEM((half, cols), F32),
             sems,
-            pltpu.SemaphoreType.DMA,
         ],
         compiler_params=LIMIT,
         cost_estimate=cost(2 * count * total * half * cols, 12 * 2**20),
         name="own_task",
-    )(*[far(x) for x in arrays])
+    )(*[near(x) if i in near_at else far(x) for i, x in enumerate(arrays)])
     arrays = [*have["t"], *have["d"], *have["x"], f1, weights, *have["w"]]
     quarter = half // 2
+    late = (3, 7)
+    near_at = [7, *(8 + i for i in late), 16]
     keep, *sends = pl.pallas_call(
-        functools.partial(second_kernel, 8, grad_from),
+        functools.partial(second_kernel, 8, grad_from, late),
         out_shape=[pltpu.VMEM((2, n, cols), F32) for n in (quarter, *CHUNKS)],
-        in_specs=[HBM] * len(arrays),
+        in_specs=[NEAR if i in near_at else HBM for i in range(len(arrays))],
         out_specs=[NEAR] * (1 + len(CHUNKS)),
         scratch_shapes=[
             pltpu.VMEM((count, total, half), BF16),
             pltpu.VMEM((count, total, cols), BF16),
             pltpu.VMEM((half, cols), F32),
-            pltpu.VMEM((half, cols), F32),
             pltpu.VMEM((half, cols), BF16),
             pltpu.VMEM((half, cols), BF16),
             sems,
-            pltpu.SemaphoreType.DMA((2 + len(PIECES),)),
+            pltpu.SemaphoreType.DMA((1 + len(PIECES),)),
         ],
         compiler_params=LIMIT,
         cost_estimate=cost(2 * count * total * half * cols, 24 * 2**20),
         name="other_task",
-    )(*[far(x) for x in arrays])
+    )(*[near(x) if i in near_at else far(x) for i, x in enumerate(arrays)])
     parts, first = [], 0
     for n, send in zip(CHUNKS, sends):
         got = core(send)
@@ -295,17 +299,23 @@
             name="share",
         )(near(keep), near(got))
         by_pair = pair(q)
-        parts += [q, core(q), by_pair, core(by_pair)]
+        parts += [(q, (0, 0, first)), (core(q), (0, 1, first))]
+        parts += [(by_pair, (1, 0, first)), (core(by_pair), (1, 1, first))]
         first += n
-    return pl.pallas_call(
-        functools.partial(whole_kernel, CHUNKS),
-        out_shape=jax.ShapeDtypeStruct((rows, cols), BF16),
-        in_specs=[NEAR] * len(parts),
-        out_specs=HBM,
-        scratch_shapes=[pltpu.SemaphoreType.DMA((len(CHUNKS), 4))],
-        compiler_params=LITTLE,
-        name="whole",
-    )(*[near(p) for p in parts])
+    out = None
+    for some in (parts[:2] + parts[4:], parts[2:4]):
+        args = [near(x) for x, _ in some]
+        out = pl.pallas_call(
+            functools.partial(whole_kernel, [spot for _, spot in some], quarter),
+            out_shape=jax.ShapeDtypeStruct((rows, cols), BF16),
+            in_specs=[HBM] * (out is not None) + [NEAR] * len(args),
+            out_specs=HBM,
+            scratch_shapes=[pltpu.SemaphoreType.DMA((len(args),))],
+            input_output_aliases={} if out is None else {0: 0},
+            compiler_params=LITTLE,
+            name="whole",
+        )(*([] if out is None else [out]), *args)
+    return out
 
 
 def solution(mesh):

time: 173 us -> 170 us (0.983)
  local copies, waits for them, and re-layouts: 7.98 us -> 3.24 us
  waiting for transfers between devices: 58 us -> 59.9 us
    unnamed x66 -> x56, local copies, waits for them, and re-layouts: 4.85 us -> 0.11 us
    ppermute x5, waiting for transfers between devices: 10.5 us -> 12.4 us  [cross(): return lax.ppermute(x, ('task', 'row'), perm)]
    pallas_call x3 -> x4, Pallas kernels: 20.4 us -> 20.9 us  [the longest x1 9.58 us: body(): pl.pallas_call(functools.partial(second_kernel, 8, grad_from, late), out_...]
  transfers between devices with their start and end apart: 39 -> 39, of which waited for: 19 -> 18; matrix products, arithmetic and copies ran while one was open for 1% -> 1% of each run, Pallas kernels for 5% -> 6%
where the time goes in v4:
time: 170 us
  starting transfers between devices  85.1 us (50%)
  waiting for transfers between devices  59.9 us (35%)
  Pallas kernels  21.3 us (13%)
  local copies, waits for them, and re-layouts  3.24 us (2%)
    ppermute x14, starting transfers between devices, ring_z(): return lax.ppermute(x, ('task', 'col'), perm)  49 us
    ppermute x5, waiting for transfers between devices, pair(): return lax.ppermute(x, 'task', [(t, t ^ 2) for t in range(4)])  22.1 us
    ppermute x14, waiting for transfers between devices, ring_z(): return lax.ppermute(x, ('task', 'col'), perm)  15.3 us
    ppermute x9, starting transfers between devices, ring_y(): return lax.ppermute(x, ('task', 'row'), perm)  13.2 us
    ppermute x5, starting transfers between devices, cross(): return lax.ppermute(x, ('task', 'row'), perm)  12.4 us
    ppermute x5, waiting for transfers between devices, cross(): return lax.ppermute(x, ('task', 'row'), perm)  12.4 us
    pallas_call x1, Pallas kernels, body(): pl.pallas_call(functools.partial(second_kernel, 8, grad_from, late), out_...  9.58 us
    pallas_call x1, Pallas kernels, body(): pl.pallas_call(functools.partial(first_kernel, 8, grad_from, late), out_s...  8.79 us
  transfers between devices with their start and end apart: 39, of which 18 were waited for; matrix products, arithmetic and copies ran while one was open for 1% of the time, Pallas kernels for 6%

profile of v4, /device:TPU:1, one launch (start us, length us, event | category | flops | bytes accessed | tf_op | source)
XLA Modules:
  0.0 170.1 jit_solution(15465358866804750346)
XLA Ops:
  3.6 5.6 %collective-permute-start.20 = (bf16[6,64,896]{2,1,0:T(8,128)(2,1)S(1)}, bf16[6,64,896]{2,1,0:T(8,128)(2,1)S(1)}, u32[]{:S(2)}, u32[]{:S(2)}) collective-permute-start(bf16[6,64,896]{2,1,0:T(8,128)(2,1)S(1)} %get-tuple-element.21.refs_0_), channel_id=1, source_target_pairs={{0,1},{1,2},{2,3},{3,4},{4,5},{5,6},{6,7},{7,0},{64,71},{65,64},{6... | collective-permute-start | bytes 2064392 | tf_op jit(solution)/shard_map/ppermute | solution.py:80
  9.2 2.7 %collective-permute-start.5 = (bf16[6,64,1024]{2,1,0:T(8,128)(2,1)S(1)}, bf16[6,64,1024]{2,1,0:T(8,128)(2,1)S(1)}, u32[]{:S(2)}, u32[]{:S(2)}) collective-permute-start(bf16[6,64,1024]{2,1,0:T(8,128)(2,1)S(1)} %bitcast.8), channel_id=1, source_target_pairs={{0,16},{8,24},{16,32},{24,40},{32,48},{40,56},{48,0},{56,8},{64,11... | collective-permute-start | bytes 2359304 | tf_op jit(solution)/shard_map/ppermute | solution.py:75
  12.2 2.5 %collective-permute-start.4 = (bf16[6,64,1024]{2,1,0:T(8,128)(2,1)S(1)}, bf16[6,64,1024]{2,1,0:T(8,128)(2,1)S(1)}, u32[]{:S(2)}, u32[]{:S(2)}) collective-permute-start(bf16[6,64,1024]{2,1,0:T(8,128)(2,1)S(1)} %bitcast.10), channel_id=1, source_target_pairs={{0,136},{8,128},{16,152},{24,144},{32,168},{40,160},{48,184},{56,1... | collective-permute-start | bytes 2359304 | tf_op jit(solution)/shard_map/ppermute | solution.py:85
  14.7 2.8 %collective-permute-done.refs_0_ = bf16[6,64,896]{2,1,0:T(8,128)(2,1)S(1)} collective-permute-done((bf16[6,64,896]{2,1,0:T(8,128)(2,1)S(1)}, bf16[6,64,896]{2,1,0:T(8,128)(2,1)S(1)}, u32[]{:S(2)}, u32[]{:S(2)}) %collective-permute-start) | collective-permute-done | bytes 688160 | tf_op jit(solution)/shard_map/ppermute | solution.py:89
  17.5 6.8 %collective-permute-start.1 = (bf16[6,64,896]{2,1,0:T(8,128)(2,1)S(1)}, bf16[6,64,896]{2,1,0:T(8,128)(2,1)S(1)}, u32[]{:S(2)}, u32[]{:S(2)}) collective-permute-start(bf16[6,64,896]{2,1,0:T(8,128)(2,1)S(1)} %collective-permute-done.refs_0_), channel_id=1, source_target_pairs={{0,1},{1,2},{2,3},{3,4},{4,5},{5,6},{6,7},{7,0},{64,71},{65,64},{6... | collective-permute-start | bytes 2064392 | tf_op jit(solution)/shard_map/ppermute | solution.py:80
  25.1 2.7 %collective-permute-start.6 = (bf16[6,64,1024]{2,1,0:T(8,128)(2,1)S(1)}, bf16[6,64,1024]{2,1,0:T(8,128)(2,1)S(1)}, u32[]{:S(2)}, u32[]{:S(2)}) collective-permute-start(bf16[6,64,1024]{2,1,0:T(8,128)(2,1)S(1)} %collective-permute-done.5.refs_9_), channel_id=1, source_target_pairs={{0,16},{8,24},{16,32},{24,40},{32,48},{40,56},{48,0},{56,8},{64,11... | collective-permute-start | bytes 2359304 | tf_op jit(solution)/shard_map/ppermute | solution.py:75
  27.8 4.4 %collective-permute-done.1.refs_1_ = bf16[6,64,896]{2,1,0:T(8,128)(2,1)S(1)} collective-permute-done((bf16[6,64,896]{2,1,0:T(8,128)(2,1)S(1)}, bf16[6,64,896]{2,1,0:T(8,128)(2,1)S(1)}, u32[]{:S(2)}, u32[]{:S(2)}) %collective-permute-start.1) | collective-permute-done | bytes 688160 | tf_op jit(solution)/shard_map/ppermute | solution.py:80
  32.2 3.4 %collective-permute-start.2 = (bf16[6,64,896]{2,1,0:T(8,128)(2,1)S(1)}, bf16[6,64,896]{2,1,0:T(8,128)(2,1)S(1)}, u32[]{:S(2)}, u32[]{:S(2)}) collective-permute-start(bf16[6,64,896]{2,1,0:T(8,128)(2,1)S(1)} %collective-permute-done.1.refs_1_), channel_id=1, source_target_pairs={{0,1},{1,2},{2,3},{3,4},{4,5},{5,6},{6,7},{7,0},{64,71},{65,64},{6... | collective-permute-start | bytes 2064392 | tf_op jit(solution)/shard_map/ppermute | solution.py:80
  35.6 2.7 %collective-permute-start.16 = (bf16[6,64,1024]{2,1,0:T(8,128)(2,1)S(1)}, bf16[6,64,1024]{2,1,0:T(8,128)(2,1)S(1)}, u32[]{:S(2)}, u32[]{:S(2)}) collective-permute-start(bf16[6,64,1024]{2,1,0:T(8,128)(2,1)S(1)} %collective-permute-done.15.refs_8_), channel_id=1, source_target_pairs={{0,16},{8,24},{16,32},{24,40},{32,48},{40,56},{48,0},{56,8},{64,11... | collective-permute-start | bytes 2359304 | tf_op jit(solution)/shard_map/ppermute | solution.py:75
  38.3 2.5 %collective-permute-start.27 = (bf16[6,64,1024]{2,1,0:T(8,128)(2,1)S(1)}, bf16[6,64,1024]{2,1,0:T(8,128)(2,1)S(1)}, u32[]{:S(2)}, u32[]{:S(2)}) collective-permute-start(bf16[6,64,1024]{2,1,0:T(8,128)(2,1)S(1)} %collective-permute-done.15.refs_8_), channel_id=1, source_target_pairs={{0,136},{8,128},{16,152},{24,144},{32,168},{40,160},{48,184},{56,1... | collective-permute-start | bytes 2359304 | tf_op jit(solution)/shard_map/ppermute | solution.py:85
  40.8 5.6 %collective-permute-start.22 = (bf16[6,64,896]{2,1,0:T(8,128)(2,1)S(1)}, bf16[6,64,896]{2,1,0:T(8,128)(2,1)S(1)}, u32[]{:S(2)}, u32[]{:S(2)}) collective-permute-start(bf16[6,64,896]{2,1,0:T(8,128)(2,1)S(1)} %collective-permute-done.21.refs_2_), channel_id=1, source_target_pairs={{0,1},{1,2},{2,3},{3,4},{4,5},{5,6},{6,7},{7,0},{64,71},{65,64},{6... | collective-permute-start | bytes 2064392 | tf_op jit(solution)/shard_map/ppermute | solution.py:80
  46.9 3.4 %collective-permute-start.3 = (bf16[6,64,896]{2,1,0:T(8,128)(2,1)S(1)}, bf16[6,64,896]{2,1,0:T(8,128)(2,1)S(1)}, u32[]{:S(2)}, u32[]{:S(2)}) collective-permute-start(bf16[6,64,896]{2,1,0:T(8,128)(2,1)S(1)} %collective-permute-done.2.refs_2_), channel_id=1, source_target_pairs={{0,1},{1,2},{2,3},{3,4},{4,5},{5,6},{6,7},{7,0},{64,71},{65,64},{6... | collective-permute-start | bytes 2064392 | tf_op jit(solution)/shard_map/ppermute | solution.py:80
  53.3 5.0 %collective-permute-done.27.refs_12_ = bf16[6,64,1024]{2,1,0:T(8,128)(2,1)S(1)} collective-permute-done((bf16[6,64,1024]{2,1,0:T(8,128)(2,1)S(1)}, bf16[6,64,1024]{2,1,0:T(8,128)(2,1)S(1)}, u32[]{:S(2)}, u32[]{:S(2)}) %collective-permute-start.27) | collective-permute-done | bytes 786464 | tf_op jit(solution)/shard_map/ppermute | solution.py:85
  58.3 5.8 %collective-permute-start.23 = (bf16[6,64,896]{2,1,0:T(8,128)(2,1)S(1)}, bf16[6,64,896]{2,1,0:T(8,128)(2,1)S(1)}, u32[]{:S(2)}, u32[]{:S(2)}) collective-permute-start(bf16[6,64,896]{2,1,0:T(8,128)(2,1)S(1)} %collective-permute-done.22.refs_3_), channel_id=1, source_target_pairs={{0,1},{1,2},{2,3},{3,4},{4,5},{5,6},{6,7},{7,0},{64,71},{65,64},{6... | collective-permute-start | bytes 2064392 | tf_op jit(solution)/shard_map/ppermute | solution.py:80
  65.0 4.4 %collective-permute-done.17.refs_10_ = bf16[6,64,1024]{2,1,0:T(8,128)(2,1)S(1)} collective-permute-done((bf16[6,64,1024]{2,1,0:T(8,128)(2,1)S(1)}, bf16[6,64,1024]{2,1,0:T(8,128)(2,1)S(1)}, u32[]{:S(2)}, u32[]{:S(2)}) %collective-permute-start.17) | collective-permute-done | bytes 786464 | tf_op jit(solution)/shard_map/ppermute | solution.py:75
  69.4 2.6 %collective-permute-done.23.refs_4_ = bf16[6,64,896]{2,1,0:T(8,128)(2,1)S(1)} collective-permute-done((bf16[6,64,896]{2,1,0:T(8,128)(2,1)S(1)}, bf16[6,64,896]{2,1,0:T(8,128)(2,1)S(1)}, u32[]{:S(2)}, u32[]{:S(2)}) %collective-permute-start.23) | collective-permute-done | bytes 688160 | tf_op jit(solution)/shard_map/ppermute | solution.py:80
  72.0 3.4 %collective-permute-start.24 = (bf16[6,64,896]{2,1,0:T(8,128)(2,1)S(1)}, bf16[6,64,896]{2,1,0:T(8,128)(2,1)S(1)}, u32[]{:S(2)}, u32[]{:S(2)}) collective-permute-start(bf16[6,64,896]{2,1,0:T(8,128)(2,1)S(1)} %collective-permute-done.23.refs_4_), channel_id=1, source_target_pairs={{0,1},{1,2},{2,3},{3,4},{4,5},{5,6},{6,7},{7,0},{64,71},{65,64},{6... | collective-permute-start | bytes 2064392 | tf_op jit(solution)/shard_map/ppermute | solution.py:80
  79.4 5.0 %collective-permute-start.9 = (bf16[6,64,896]{2,1,0:T(8,128)(2,1)S(1)}, bf16[6,64,896]{2,1,0:T(8,128)(2,1)S(1)}, u32[]{:S(2)}, u32[]{:S(2)}) collective-permute-start(bf16[6,64,896]{2,1,0:T(8,128)(2,1)S(1)} %collective-permute-done.8.refs_4_), channel_id=1, source_target_pairs={{0,1},{1,2},{2,3},{3,4},{4,5},{5,6},{6,7},{7,0},{64,71},{65,64},{6... | collective-permute-start | bytes 2064392 | tf_op jit(solution)/shard_map/ppermute | solution.py:80
  86.8 3.4 %collective-permute-start.25 = (bf16[6,64,896]{2,1,0:T(8,128)(2,1)S(1)}, bf16[6,64,896]{2,1,0:T(8,128)(2,1)S(1)}, u32[]{:S(2)}, u32[]{:S(2)}) collective-permute-start(bf16[6,64,896]{2,1,0:T(8,128)(2,1)S(1)} %collective-permute-done.24.refs_5_), channel_id=1, source_target_pairs={{0,1},{1,2},{2,3},{3,4},{4,5},{5,6},{6,7},{7,0},{64,71},{65,64},{6... | collective-permute-start | bytes 2064392 | tf_op jit(solution)/shard_map/ppermute | solution.py:80
  90.2 2.6 %collective-permute-done.12.refs_18_ = bf16[896,1024]{1,0:T(8,128)(2,1)S(1)} collective-permute-done((bf16[896,1024]{1,0:T(8,128)(2,1)S(1)}, bf16[896,1024]{1,0:T(8,128)(2,1)S(1)}, u32[]{:S(2)}, u32[]{:S(2)}) %collective-permute-start.12) | collective-permute-done | bytes 1835040 | tf_op jit(solution)/shard_map/ppermute | solution.py:89
  98.2 3.3 %collective-permute-done.25.refs_6_ = bf16[6,64,896]{2,1,0:T(8,128)(2,1)S(1)} collective-permute-done((bf16[6,64,896]{2,1,0:T(8,128)(2,1)S(1)}, bf16[6,64,896]{2,1,0:T(8,128)(2,1)S(1)}, u32[]{:S(2)}, u32[]{:S(2)}) %collective-permute-start.25) | collective-permute-done | bytes 688160 | tf_op jit(solution)/shard_map/ppermute | solution.py:80
  101.5 3.4 %collective-permute-start.26 = (bf16[6,64,896]{2,1,0:T(8,128)(2,1)S(1)}, bf16[6,64,896]{2,1,0:T(8,128)(2,1)S(1)}, u32[]{:S(2)}, u32[]{:S(2)}) collective-permute-start(bf16[6,64,896]{2,1,0:T(8,128)(2,1)S(1)} %collective-permute-done.25.refs_6_), channel_id=1, source_target_pairs={{0,1},{1,2},{2,3},{3,4},{4,5},{5,6},{6,7},{7,0},{64,71},{65,64},{6... | collective-permute-start | bytes 2064392 | tf_op jit(solution)/shard_map/ppermute | solution.py:80
  104.9 2.5 %collective-permute-start.19 = (bf16[6,64,1024]{2,1,0:T(8,128)(2,1)S(1)}, bf16[6,64,1024]{2,1,0:T(8,128)(2,1)S(1)}, u32[]{:S(2)}, u32[]{:S(2)}) collective-permute-start(bf16[6,64,1024]{2,1,0:T(8,128)(2,1)S(1)} %collective-permute-done.7.refs_11_), channel_id=1, source_target_pairs={{0,136},{8,128},{16,152},{24,144},{32,168},{40,160},{48,184},{56,1... | collective-permute-start | bytes 2359304 | tf_op jit(solution)/shard_map/ppermute | solution.py:85
  107.4 3.9 %collective-permute-done.13.refs_14_ = bf16[6,64,1024]{2,1,0:T(8,128)(2,1)S(1)} collective-permute-done((bf16[6,64,1024]{2,1,0:T(8,128)(2,1)S(1)}, bf16[6,64,1024]{2,1,0:T(8,128)(2,1)S(1)}, u32[]{:S(2)}, u32[]{:S(2)}) %collective-permute-start.13) | collective-permute-done | bytes 786464 | tf_op jit(solution)/shard_map/ppermute | solution.py:85
  111.3 2.7 %collective-permute-start.18 = (bf16[6,64,1024]{2,1,0:T(8,128)(2,1)S(1)}, bf16[6,64,1024]{2,1,0:T(8,128)(2,1)S(1)}, u32[]{:S(2)}, u32[]{:S(2)}) collective-permute-start(bf16[6,64,1024]{2,1,0:T(8,128)(2,1)S(1)} %collective-permute-done.17.refs_10_), channel_id=1, source_target_pairs={{0,16},{8,24},{16,32},{24,40},{32,48},{40,56},{48,0},{56,8},{64,11... | collective-permute-start | bytes 2359304 | tf_op jit(solution)/shard_map/ppermute | solution.py:75
  116.3 8.8 %own_task.1.refs_16_ = f32[896,1024]{1,0:T(8,128)S(1)} custom-call(bf16[6,64,896]{2,1,0:T(8,128)(2,1)} %copy-done.14, bf16[6,64,896]{2,1,0:T(8,128)(2,1)} %copy-done.22, bf16[6,64,896]{2,1,0:T(8,128)(2,1)} %copy-done.23, bf16[6,64,896]{2,1,0:T(8,128)(2,1)} %copy-done.24, bf16[6,64,896]{2,1,0:T(8,128)(2,1)} %copy-done.25, bf16[6,64,896]{2,1,0:T(8,128)(2,1)} %copy-done.26, ...), custom_call_target="tpu_custom_call" | custom-call | flops 5637144576 | bytes 12582912 | tf_op jit(solution)/shard_map/own_task/pallas_call | solution.py:254
  125.3 2.9 %collective-permute-done.19.refs_15_ = bf16[6,64,1024]{2,1,0:T(8,128)(2,1)S(1)} collective-permute-done((bf16[6,64,1024]{2,1,0:T(8,128)(2,1)S(1)}, bf16[6,64,1024]{2,1,0:T(8,128)(2,1)S(1)}, u32[]{:S(2)}, u32[]{:S(2)}) %collective-permute-start.19) | collective-permute-done | bytes 786464 | tf_op jit(solution)/shard_map/ppermute | solution.py:85
  128.2 9.6 %other_task.1 = (f32[2,448,1024]{2,1,0:T(8,128)S(1)}, f32[2,192,1024]{2,1,0:T(8,128)S(1)}, f32[2,256,1024]{2,1,0:T(8,128)S(1)}) custom-call(bf16[6,64,896]{2,1,0:T(8,128)(2,1)} %copy-done.7, bf16[6,64,896]{2,1,0:T(8,128)(2,1)} %copy-done.8, bf16[6,64,896]{2,1,0:T(8,128)(2,1)} %copy-done.9, bf16[6,64,896]{2,1,0:T(8,128)(2,1)} %copy-done.10, ...), custom_call_target="tpu_custom_call" | custom-call | flops 5637144576 | bytes 25165824 | tf_op jit(solution)/shard_map/other_task/pallas_call | solution.py:272
  137.7 2.8 %collective-permute-start.33 = (f32[2,256,1024]{2,1,0:T(8,128)S(1)}, f32[2,256,1024]{2,1,0:T(8,128)S(1)}, u32[]{:S(2)}, u32[]{:S(2)}) collective-permute-start(f32[2,256,1024]{2,1,0:T(8,128)S(1)} %get-tuple-element.20), channel_id=1, source_target_pairs={{0,64},{64,0},{128,192},{192,128},{1,65},{65,1},{129,193},{193,129... | collective-permute-start | bytes 6291464 | tf_op jit(solution)/shard_map/ppermute | solution.py:93
  140.6 3.7 %collective-permute-done.33.got = f32[2,256,1024]{2,1,0:T(8,128)S(1)} collective-permute-done((f32[2,256,1024]{2,1,0:T(8,128)S(1)}, f32[2,256,1024]{2,1,0:T(8,128)S(1)}, u32[]{:S(2)}, u32[]{:S(2)}) %collective-permute-start.33) | collective-permute-done | bytes 2097184 | tf_op jit(solution)/shard_map/ppermute | solution.py:93
  147.4 10.3 %collective-permute-done.35.refs_4_ = bf16[256,1024]{1,0:T(8,128)(2,1)S(1)} collective-permute-done((bf16[256,1024]{1,0:T(8,128)(2,1)S(1)}, bf16[256,1024]{1,0:T(8,128)(2,1)S(1)}, u32[]{:S(2)}, u32[]{:S(2)}) %collective-permute-start.35) | collective-permute-done | bytes 524320 | tf_op jit(solution)/shard_map/ppermute | solution.py:89
  159.7 6.4 %collective-permute-done.37.refs_1_ = bf16[192,1024]{1,0:T(8,128)(2,1)S(1)} collective-permute-done((bf16[192,1024]{1,0:T(8,128)(2,1)S(1)}, bf16[192,1024]{1,0:T(8,128)(2,1)S(1)}, u32[]{:S(2)}, u32[]{:S(2)}) %collective-permute-start.37) | collective-permute-done | bytes 393248 | tf_op jit(solution)/shard_map/ppermute | solution.py:89
  (110 shorter events, 32.0 us)
Async XLA Ops:
  1.5 15.9 %collective-permute-start = (bf16[6,64,896]{2,1,0:T(8,128)(2,1)S(1)}, bf16[6,64,896]{2,1,0:T(8,128)(2,1)S(1)}, u32[]{:S(2)}, u32[]{:S(2)}) collective-permute-start(bf16[6,64,896]{2,1,0:T(8,128)(2,1)S(1)} %get-tuple-element.22), channel_id=1, source_target_pairs={{0,128},{64,192},{128,0},{192,64},{1,129},{65,193},{129,1},{193,65... | collective-permute-start | bytes 2064392 | tf_op jit(solution)/shard_map/ppermute | solution.py:89
  3.6 20.7 %collective-permute-start.20 = (bf16[6,64,896]{2,1,0:T(8,128)(2,1)S(1)}, bf16[6,64,896]{2,1,0:T(8,128)(2,1)S(1)}, u32[]{:S(2)}, u32[]{:S(2)}) collective-permute-start(bf16[6,64,896]{2,1,0:T(8,128)(2,1)S(1)} %get-tuple-element.21.refs_0_), channel_id=1, source_target_pairs={{0,1},{1,2},{2,3},{3,4},{4,5},{5,6},{6,7},{7,0},{64,71},{65,64},{6... | collective-permute-start | bytes 2064392 | tf_op jit(solution)/shard_map/ppermute | solution.py:80
  9.2 15.8 %collective-permute-start.5 = (bf16[6,64,1024]{2,1,0:T(8,128)(2,1)S(1)}, bf16[6,64,1024]{2,1,0:T(8,128)(2,1)S(1)}, u32[]{:S(2)}, u32[]{:S(2)}) collective-permute-start(bf16[6,64,1024]{2,1,0:T(8,128)(2,1)S(1)} %bitcast.8), channel_id=1, source_target_pairs={{0,16},{8,24},{16,32},{24,40},{32,48},{40,56},{48,0},{56,8},{64,11... | collective-permute-start | bytes 2359304 | tf_op jit(solution)/shard_map/ppermute | solution.py:75
  12.0 23.7 %collective-permute-start.15 = (bf16[6,64,1024]{2,1,0:T(8,128)(2,1)S(1)}, bf16[6,64,1024]{2,1,0:T(8,128)(2,1)S(1)}, u32[]{:S(2)}, u32[]{:S(2)}) collective-permute-start(bf16[6,64,1024]{2,1,0:T(8,128)(2,1)S(1)} %bitcast.9), channel_id=1, source_target_pairs={{0,128},{64,192},{128,0},{192,64},{1,129},{65,193},{129,1},{193,65... | collective-permute-start | bytes 2359304 | tf_op jit(solution)/shard_map/ppermute | solution.py:89
  12.2 26.1 %collective-permute-start.4 = (bf16[6,64,1024]{2,1,0:T(8,128)(2,1)S(1)}, bf16[6,64,1024]{2,1,0:T(8,128)(2,1)S(1)}, u32[]{:S(2)}, u32[]{:S(2)}) collective-permute-start(bf16[6,64,1024]{2,1,0:T(8,128)(2,1)S(1)} %bitcast.10), channel_id=1, source_target_pairs={{0,136},{8,128},{16,152},{24,144},{32,168},{40,160},{48,184},{56,1... | collective-permute-start | bytes 2359304 | tf_op jit(solution)/shard_map/ppermute | solution.py:85
  17.5 14.7 %collective-permute-start.1 = (bf16[6,64,896]{2,1,0:T(8,128)(2,1)S(1)}, bf16[6,64,896]{2,1,0:T(8,128)(2,1)S(1)}, u32[]{:S(2)}, u32[]{:S(2)}) collective-permute-start(bf16[6,64,896]{2,1,0:T(8,128)(2,1)S(1)} %collective-permute-done.refs_0_), channel_id=1, source_target_pairs={{0,1},{1,2},{2,3},{3,4},{4,5},{5,6},{6,7},{7,0},{64,71},{65,64},{6... | collective-permute-start | bytes 2064392 | tf_op jit(solution)/shard_map/ppermute | solution.py:80
  24.3 16.5 %collective-permute-start.21 = (bf16[6,64,896]{2,1,0:T(8,128)(2,1)S(1)}, bf16[6,64,896]{2,1,0:T(8,128)(2,1)S(1)}, u32[]{:S(2)}, u32[]{:S(2)}) collective-permute-start(bf16[6,64,896]{2,1,0:T(8,128)(2,1)S(1)} %collective-permute-done.20.refs_1_), channel_id=1, source_target_pairs={{0,1},{1,2},{2,3},{3,4},{4,5},{5,6},{6,7},{7,0},{64,71},{65,64},{6... | collective-permute-start | bytes 2064392 | tf_op jit(solution)/shard_map/ppermute | solution.py:80
  25.1 21.3 %collective-permute-start.6 = (bf16[6,64,1024]{2,1,0:T(8,128)(2,1)S(1)}, bf16[6,64,1024]{2,1,0:T(8,128)(2,1)S(1)}, u32[]{:S(2)}, u32[]{:S(2)}) collective-permute-start(bf16[6,64,1024]{2,1,0:T(8,128)(2,1)S(1)} %collective-permute-done.5.refs_9_), channel_id=1, source_target_pairs={{0,16},{8,24},{16,32},{24,40},{32,48},{40,56},{48,0},{56,8},{64,11... | collective-permute-start | bytes 2359304 | tf_op jit(solution)/shard_map/ppermute | solution.py:75
  32.2 14.7 %collective-permute-start.2 = (bf16[6,64,896]{2,1,0:T(8,128)(2,1)S(1)}, bf16[6,64,896]{2,1,0:T(8,128)(2,1)S(1)}, u32[]{:S(2)}, u32[]{:S(2)}) collective-permute-start(bf16[6,64,896]{2,1,0:T(8,128)(2,1)S(1)} %collective-permute-done.1.refs_1_), channel_id=1, source_target_pairs={{0,1},{1,2},{2,3},{3,4},{4,5},{5,6},{6,7},{7,0},{64,71},{65,64},{6... | collective-permute-start | bytes 2064392 | tf_op jit(solution)/shard_map/ppermute | solution.py:80
  35.6 16.4 %collective-permute-start.16 = (bf16[6,64,1024]{2,1,0:T(8,128)(2,1)S(1)}, bf16[6,64,1024]{2,1,0:T(8,128)(2,1)S(1)}, u32[]{:S(2)}, u32[]{:S(2)}) collective-permute-start(bf16[6,64,1024]{2,1,0:T(8,128)(2,1)S(1)} %collective-permute-done.15.refs_8_), channel_id=1, source_target_pairs={{0,16},{8,24},{16,32},{24,40},{32,48},{40,56},{48,0},{56,8},{64,11... | collective-permute-start | bytes 2359304 | tf_op jit(solution)/shard_map/ppermute | solution.py:75
  38.3 19.9 %collective-permute-start.27 = (bf16[6,64,1024]{2,1,0:T(8,128)(2,1)S(1)}, bf16[6,64,1024]{2,1,0:T(8,128)(2,1)S(1)}, u32[]{:S(2)}, u32[]{:S(2)}) collective-permute-start(bf16[6,64,1024]{2,1,0:T(8,128)(2,1)S(1)} %collective-permute-done.15.refs_8_), channel_id=1, source_target_pairs={{0,136},{8,128},{16,152},{24,144},{32,168},{40,160},{48,184},{56,1... | collective-permute-start | bytes 2359304 | tf_op jit(solution)/shard_map/ppermute | solution.py:85
  40.8 17.5 %collective-permute-start.22 = (bf16[6,64,896]{2,1,0:T(8,128)(2,1)S(1)}, bf16[6,64,896]{2,1,0:T(8,128)(2,1)S(1)}, u32[]{:S(2)}, u32[]{:S(2)}) collective-permute-start(bf16[6,64,896]{2,1,0:T(8,128)(2,1)S(1)} %collective-permute-done.21.refs_2_), channel_id=1, source_target_pairs={{0,1},{1,2},{2,3},{3,4},{4,5},{5,6},{6,7},{7,0},{64,71},{65,64},{6... | collective-permute-start | bytes 2064392 | tf_op jit(solution)/shard_map/ppermute | solution.py:80
  46.4 17.7 %collective-permute-start.7 = (bf16[6,64,1024]{2,1,0:T(8,128)(2,1)S(1)}, bf16[6,64,1024]{2,1,0:T(8,128)(2,1)S(1)}, u32[]{:S(2)}, u32[]{:S(2)}) collective-permute-start(bf16[6,64,1024]{2,1,0:T(8,128)(2,1)S(1)} %collective-permute-done.6.refs_10_), channel_id=1, source_target_pairs={{0,16},{8,24},{16,32},{24,40},{32,48},{40,56},{48,0},{56,8},{64,11... | collective-permute-start | bytes 2359304 | tf_op jit(solution)/shard_map/ppermute | solution.py:75
  46.9 17.2 %collective-permute-start.3 = (bf16[6,64,896]{2,1,0:T(8,128)(2,1)S(1)}, bf16[6,64,896]{2,1,0:T(8,128)(2,1)S(1)}, u32[]{:S(2)}, u32[]{:S(2)}) collective-permute-start(bf16[6,64,896]{2,1,0:T(8,128)(2,1)S(1)} %collective-permute-done.2.refs_2_), channel_id=1, source_target_pairs={{0,1},{1,2},{2,3},{3,4},{4,5},{5,6},{6,7},{7,0},{64,71},{65,64},{6... | collective-permute-start | bytes 2064392 | tf_op jit(solution)/shard_map/ppermute | solution.py:80
  52.0 40.8 %collective-permute-start.12 = (bf16[896,1024]{1,0:T(8,128)(2,1)S(1)}, bf16[896,1024]{1,0:T(8,128)(2,1)S(1)}, u32[]{:S(2)}, u32[]{:S(2)}) collective-permute-start(bf16[896,1024]{1,0:T(8,128)(2,1)S(1)} %dynamic-slice_bitcast_fusion), channel_id=1, source_target_pairs={{0,128},{64,192},{128,0},{192,64},{1,129},{65,193},{129,1},{193,65... | collective-permute-start | bytes 5505032 | tf_op jit(solution)/shard_map/ppermute | solution.py:89
  58.3 13.7 %collective-permute-start.23 = (bf16[6,64,896]{2,1,0:T(8,128)(2,1)S(1)}, bf16[6,64,896]{2,1,0:T(8,128)(2,1)S(1)}, u32[]{:S(2)}, u32[]{:S(2)}) collective-permute-start(bf16[6,64,896]{2,1,0:T(8,128)(2,1)S(1)} %collective-permute-done.22.refs_3_), channel_id=1, source_target_pairs={{0,1},{1,2},{2,3},{3,4},{4,5},{5,6},{6,7},{7,0},{64,71},{65,64},{6... | collective-permute-start | bytes 2064392 | tf_op jit(solution)/shard_map/ppermute | solution.py:80
  64.1 13.8 %collective-permute-start.28 = (bf16[6,64,1024]{2,1,0:T(8,128)(2,1)S(1)}, bf16[6,64,1024]{2,1,0:T(8,128)(2,1)S(1)}, u32[]{:S(2)}, u32[]{:S(2)}) collective-permute-start(bf16[6,64,1024]{2,1,0:T(8,128)(2,1)S(1)} %collective-permute-done.27.refs_12_), channel_id=1, source_target_pairs={{0,16},{8,24},{16,32},{24,40},{32,48},{40,56},{48,0},{56,8},{64,11... | collective-permute-start | bytes 2359304 | tf_op jit(solution)/shard_map/ppermute | solution.py:75
  64.2 15.2 %collective-permute-start.8 = (bf16[6,64,896]{2,1,0:T(8,128)(2,1)S(1)}, bf16[6,64,896]{2,1,0:T(8,128)(2,1)S(1)}, u32[]{:S(2)}, u32[]{:S(2)}) collective-permute-start(bf16[6,64,896]{2,1,0:T(8,128)(2,1)S(1)} %collective-permute-done.3.refs_3_), channel_id=1, source_target_pairs={{0,1},{1,2},{2,3},{3,4},{4,5},{5,6},{6,7},{7,0},{64,71},{65,64},{6... | collective-permute-start | bytes 2064392 | tf_op jit(solution)/shard_map/ppermute | solution.py:80
  72.0 14.7 %collective-permute-start.24 = (bf16[6,64,896]{2,1,0:T(8,128)(2,1)S(1)}, bf16[6,64,896]{2,1,0:T(8,128)(2,1)S(1)}, u32[]{:S(2)}, u32[]{:S(2)}) collective-permute-start(bf16[6,64,896]{2,1,0:T(8,128)(2,1)S(1)} %collective-permute-done.23.refs_4_), channel_id=1, source_target_pairs={{0,1},{1,2},{2,3},{3,4},{4,5},{5,6},{6,7},{7,0},{64,71},{65,64},{6... | collective-permute-start | bytes 2064392 | tf_op jit(solution)/shard_map/ppermute | solution.py:80
  75.4 20.5 %collective-permute-start.10 = (bf16[6,64,1024]{2,1,0:T(8,128)(2,1)S(1)}, bf16[6,64,1024]{2,1,0:T(8,128)(2,1)S(1)}, u32[]{:S(2)}, u32[]{:S(2)}) collective-permute-start(bf16[6,64,1024]{2,1,0:T(8,128)(2,1)S(1)} %collective-permute-done.5.refs_9_), channel_id=1, source_target_pairs={{0,136},{8,128},{16,152},{24,144},{32,168},{40,160},{48,184},{56,1... | collective-permute-start | bytes 2359304 | tf_op jit(solution)/shard_map/ppermute | solution.py:85
  77.9 19.6 %collective-permute-start.29 = (bf16[6,64,1024]{2,1,0:T(8,128)(2,1)S(1)}, bf16[6,64,1024]{2,1,0:T(8,128)(2,1)S(1)}, u32[]{:S(2)}, u32[]{:S(2)}) collective-permute-start(bf16[6,64,1024]{2,1,0:T(8,128)(2,1)S(1)} %collective-permute-done.28.refs_13_), channel_id=1, source_target_pairs={{0,16},{8,24},{16,32},{24,40},{32,48},{40,56},{48,0},{56,8},{64,11... | collective-permute-start | bytes 2359304 | tf_op jit(solution)/shard_map/ppermute | solution.py:75
  79.4 16.5 %collective-permute-start.9 = (bf16[6,64,896]{2,1,0:T(8,128)(2,1)S(1)}, bf16[6,64,896]{2,1,0:T(8,128)(2,1)S(1)}, u32[]{:S(2)}, u32[]{:S(2)}) collective-permute-start(bf16[6,64,896]{2,1,0:T(8,128)(2,1)S(1)} %collective-permute-done.8.refs_4_), channel_id=1, source_target_pairs={{0,1},{1,2},{2,3},{3,4},{4,5},{5,6},{6,7},{7,0},{64,71},{65,64},{6... | collective-permute-start | bytes 2064392 | tf_op jit(solution)/shard_map/ppermute | solution.py:80
  86.8 14.7 %collective-permute-start.25 = (bf16[6,64,896]{2,1,0:T(8,128)(2,1)S(1)}, bf16[6,64,896]{2,1,0:T(8,128)(2,1)S(1)}, u32[]{:S(2)}, u32[]{:S(2)}) collective-permute-start(bf16[6,64,896]{2,1,0:T(8,128)(2,1)S(1)} %collective-permute-done.24.refs_5_), channel_id=1, source_target_pairs={{0,1},{1,2},{2,3},{3,4},{4,5},{5,6},{6,7},{7,0},{64,71},{65,64},{6... | collective-permute-start | bytes 2064392 | tf_op jit(solution)/shard_map/ppermute | solution.py:80
  92.8 18.5 %collective-permute-start.13 = (bf16[6,64,1024]{2,1,0:T(8,128)(2,1)S(1)}, bf16[6,64,1024]{2,1,0:T(8,128)(2,1)S(1)}, u32[]{:S(2)}, u32[]{:S(2)}) collective-permute-start(bf16[6,64,1024]{2,1,0:T(8,128)(2,1)S(1)} %collective-permute-done.6.refs_10_), channel_id=1, source_target_pairs={{0,136},{8,128},{16,152},{24,144},{32,168},{40,160},{48,184},{56,1... | collective-permute-start | bytes 2359304 | tf_op jit(solution)/shard_map/ppermute | solution.py:85
  95.9 18.1 %collective-permute-start.11 = (bf16[6,64,896]{2,1,0:T(8,128)(2,1)S(1)}, bf16[6,64,896]{2,1,0:T(8,128)(2,1)S(1)}, u32[]{:S(2)}, u32[]{:S(2)}) collective-permute-start(bf16[6,64,896]{2,1,0:T(8,128)(2,1)S(1)} %collective-permute-done.9.refs_5_), channel_id=1, source_target_pairs={{0,1},{1,2},{2,3},{3,4},{4,5},{5,6},{6,7},{7,0},{64,71},{65,64},{6... | collective-permute-start | bytes 2064392 | tf_op jit(solution)/shard_map/ppermute | solution.py:80
  97.5 16.5 %collective-permute-start.30 = (bf16[6,64,1024]{2,1,0:T(8,128)(2,1)S(1)}, bf16[6,64,1024]{2,1,0:T(8,128)(2,1)S(1)}, u32[]{:S(2)}, u32[]{:S(2)}) collective-permute-start(bf16[6,64,1024]{2,1,0:T(8,128)(2,1)S(1)} %collective-permute-done.29.refs_14_), channel_id=1, source_target_pairs={{0,16},{8,24},{16,32},{24,40},{32,48},{40,56},{48,0},{56,8},{64,11... | collective-permute-start | bytes 2359304 | tf_op jit(solution)/shard_map/ppermute | solution.py:75
  101.5 14.7 %collective-permute-start.26 = (bf16[6,64,896]{2,1,0:T(8,128)(2,1)S(1)}, bf16[6,64,896]{2,1,0:T(8,128)(2,1)S(1)}, u32[]{:S(2)}, u32[]{:S(2)}) collective-permute-start(bf16[6,64,896]{2,1,0:T(8,128)(2,1)S(1)} %collective-permute-done.25.refs_6_), channel_id=1, source_target_pairs={{0,1},{1,2},{2,3},{3,4},{4,5},{5,6},{6,7},{7,0},{64,71},{65,64},{6... | collective-permute-start | bytes 2064392 | tf_op jit(solution)/shard_map/ppermute | solution.py:80
  104.9 23.2 %collective-permute-start.19 = (bf16[6,64,1024]{2,1,0:T(8,128)(2,1)S(1)}, bf16[6,64,1024]{2,1,0:T(8,128)(2,1)S(1)}, u32[]{:S(2)}, u32[]{:S(2)}) collective-permute-start(bf16[6,64,1024]{2,1,0:T(8,128)(2,1)S(1)} %collective-permute-done.7.refs_11_), channel_id=1, source_target_pairs={{0,136},{8,128},{16,152},{24,144},{32,168},{40,160},{48,184},{56,1... | collective-permute-start | bytes 2359304 | tf_op jit(solution)/shard_map/ppermute | solution.py:85
  111.3 16.9 %collective-permute-start.18 = (bf16[6,64,1024]{2,1,0:T(8,128)(2,1)S(1)}, bf16[6,64,1024]{2,1,0:T(8,128)(2,1)S(1)}, u32[]{:S(2)}, u32[]{:S(2)}) collective-permute-start(bf16[6,64,1024]{2,1,0:T(8,128)(2,1)S(1)} %collective-permute-done.17.refs_10_), channel_id=1, source_target_pairs={{0,16},{8,24},{16,32},{24,40},{32,48},{40,56},{48,0},{56,8},{64,11... | collective-permute-start | bytes 2359304 | tf_op jit(solution)/shard_map/ppermute | solution.py:75
  114.0 14.1 %collective-permute-start.14 = (bf16[6,64,896]{2,1,0:T(8,128)(2,1)S(1)}, bf16[6,64,896]{2,1,0:T(8,128)(2,1)S(1)}, u32[]{:S(2)}, u32[]{:S(2)}) collective-permute-start(bf16[6,64,896]{2,1,0:T(8,128)(2,1)S(1)} %collective-permute-done.11.refs_6_), channel_id=1, source_target_pairs={{0,1},{1,2},{2,3},{3,4},{4,5},{5,6},{6,7},{7,0},{64,71},{65,64},{6... | collective-permute-start | bytes 2064392 | tf_op jit(solution)/shard_map/ppermute | solution.py:80
  146.7 19.5 %collective-permute-start.37 = (bf16[192,1024]{1,0:T(8,128)(2,1)S(1)}, bf16[192,1024]{1,0:T(8,128)(2,1)S(1)}, u32[]{:S(2)}, u32[]{:S(2)}) collective-permute-start(bf16[192,1024]{1,0:T(8,128)(2,1)S(1)} %share.2.refs_0_), channel_id=1, source_target_pairs={{0,128},{64,192},{128,0},{192,64},{1,129},{65,193},{129,1},{193,65... | collective-permute-start | bytes 1179656 | tf_op jit(solution)/shard_map/ppermute | solution.py:89
  146.8 20.6 %collective-permute-start.34 = (bf16[256,1024]{1,0:T(8,128)(2,1)S(1)}, bf16[256,1024]{1,0:T(8,128)(2,1)S(1)}, u32[]{:S(2)}, u32[]{:S(2)}) collective-permute-start(bf16[256,1024]{1,0:T(8,128)(2,1)S(1)} %share.3.refs_2_), channel_id=1, source_target_pairs={{0,64},{64,0},{128,192},{192,128},{1,65},{65,1},{129,193},{193,129... | collective-permute-start | bytes 1572872 | tf_op jit(solution)/shard_map/ppermute | solution.py:93
  (35 other events, 1610.5 us)
